TPU v7x, 512 devices: a whole 4x4x16 slice. The times are simulated.
512 devices in a mesh: ctx: 64 (over z, x), tp: 8 (over y, core).
Axes of the slice: x: 4, y: 4, z: 16, core: 2. Of those that a mesh axis runs over, the one named last changes fastest.
Arguments:
- tokens: bfloat16 [65536, 4096], P(('ctx', 'tp')), may hold values from -26 to 26
- query_weight: bfloat16 [4096, 2048], P('ctx', 'tp'), may hold values from -0.09375 to 0.09375
- kv_weight: bfloat16 [4096, 2048], P('ctx', 'tp'), may hold values from -0.09375 to 0.09375
- reach: int32 [1024], P('ctx'), may hold values from 1 to 2, as said below
- global_ids: int32 [2], replicated, may hold values from 0 to 1023, as said below
- rand_ids: int32 [1024, 3], replicated, may hold values from -1 to 1023, as said below
Outputs:
- attended: bfloat16 [65536, 2048], P('ctx', 'tp')
Inputs may be any that keep to these rules, and one draw needn't show every extreme that they name: Some query block has reach 2. `global_ids`: distinct block numbers; the last entry is block 1023. `rand_ids`: the -1 entries of a query block come after its other entries; the 16 query blocks of a run (blocks 16 * i to 16 * i + 15) list at most 2 entries, repeats counted, that name blocks of any one run; in some run all entries are filled and some run of key blocks is named by exactly 2 of them.
All inputs are finite; a program needn't handle non-finite values.
Results may differ from a plain program's by a relative error of at most 0.012.
The roundings to bfloat16 on the way count: a program that leaves them out, or rounds other values in their place, can miss the bound.
Values may be sent and summed in bfloat16 or wider, within the bound.
No kernel may reach another device: no remote copies, remote signals or barrier semaphores. Data moves between devices by JAX's collectives and lax.ppermute only.
A program may use at most 64 MiB of HBM per device.

v0:
```python
import jax
import jax.numpy as jnp
from jax import lax
from jax.sharding import PartitionSpec as P

HD = 128
GROUP = 2
BS = 64
WMAX = 2
G = 2


masked_score = -1e30


def with_halo(shard, sides, width):
    for axis, dim in sides:
        size, length = (lax.axis_size(axis), shard.shape[dim])
        up = [(i, (i + 1) % size) for i in range(size - 1)]
        down = [(j, i) for i, j in up]
        last = lax.slice_in_dim(shard, length - width, length, axis=dim)
        initial = lax.slice_in_dim(shard, 0, width, axis=dim)
        before = lax.ppermute(last, axis, up)
        after = lax.ppermute(initial, axis, down)
        shard = jnp.concatenate([before, shard, after], axis=dim)
    return shard


def attend_group(query_group, slab_group, valid_group, kv_local):
    group_blocks = query_group.shape[0]
    slot_count = slab_group.shape[1]
    queries = query_group.reshape(group_blocks, BS, kv_local, GROUP, HD)
    slabs = slab_group.reshape(group_blocks, slot_count, BS, kv_local, 2, HD)
    scores = jnp.einsum(
        "bqkgd,bsjkd->bkgqsj", queries, slabs[:, :, :, :, 0, :], preferred_element_type=jnp.float32
    )
    scores = scores.reshape(scores.shape[:4] + (slot_count * BS,)) * HD ** (-0.5)
    key_live = jnp.repeat(valid_group, BS, axis=1)
    scores = jnp.where(key_live[:, None, None, None, :], scores, masked_score)
    row_max = jnp.max(scores, axis=-1, keepdims=True)
    exponent = jnp.exp(scores - row_max)
    weights = (exponent / jnp.sum(exponent, axis=-1, keepdims=True)).astype(jnp.bfloat16)
    weights = weights.reshape(weights.shape[:4] + (slot_count, BS))
    mixed = jnp.einsum(
        "bkgqsj,bsjkd->bqkgd", weights, slabs[:, :, :, :, 1, :], preferred_element_type=jnp.float32
    )
    return mixed.astype(jnp.bfloat16).reshape(group_blocks * BS, kv_local * GROUP * HD)


def fetch_blocks(key_rows, global_ids, rand_ids, ctx_index, ctx_count):
    row_count, lane_width = key_rows.shape
    run_blocks = row_count // BS
    blocks = key_rows.reshape(run_blocks, BS, lane_width)
    padded = with_halo(key_rows, (("ctx", 0),), WMAX * BS)
    padded_blocks = padded.reshape(run_blocks + 2 * WMAX, BS, lane_width)
    window_kv = jnp.stack(
        [padded_blocks[shift_at : shift_at + run_blocks] for shift_at in range(2 * WMAX + 1)],
        axis=1,
    )
    global_owner = global_ids // run_blocks
    global_local = global_ids % run_blocks
    is_held = (global_owner == ctx_index)[:, None, None]
    sum_term = jnp.where(is_held, blocks[global_local].astype(jnp.float32), 0.0)
    global_kv = lax.psum(sum_term, "ctx").astype(jnp.bfloat16)
    slot_count = run_blocks * rand_ids.shape[1]
    capacity = max(2, (slot_count + ctx_count - 1) // ctx_count)
    listed = rand_ids.reshape(ctx_count, slot_count)
    owners = jnp.where(listed >= 0, listed // run_blocks, -1)
    owned_here = owners == ctx_index
    ranks = jnp.cumsum(owned_here.astype(jnp.int32), axis=1) - 1
    picks = owned_here[:, None, :] & (ranks[:, None, :] == jnp.arange(capacity)[None, :, None])
    local_ids = jnp.sum(jnp.where(picks, listed[:, None, :] % run_blocks, 0), axis=2)
    filled = jnp.any(picks, axis=2)
    outgoing = jnp.where(filled[:, :, None, None], blocks[local_ids], jnp.zeros((), jnp.bfloat16))
    incoming = lax.all_to_all(outgoing, "ctx", split_axis=0, concat_axis=0, tiled=True)
    wanted = lax.dynamic_index_in_dim(owners, ctx_index, 0, keepdims=False)
    slot_order = jnp.arange(slot_count)
    earlier = (wanted[None, :] == wanted[:, None]) & (slot_order[None, :] < slot_order[:, None])
    position = jnp.sum(earlier.astype(jnp.int32), axis=1)
    flat_index = jnp.where(wanted >= 0, wanted * capacity + position, 0)
    random_kv = incoming.reshape(ctx_count * capacity, BS, lane_width)[flat_index]
    random_kv = random_kv.reshape(run_blocks, -1, BS, lane_width)
    return (window_kv, global_kv, random_kv)


def per_device(tokens, query_weight, kv_weight, reach, global_ids, rand_ids):
    ctx_count = lax.axis_size("ctx")
    ctx_index = lax.axis_index("ctx")
    full_query_w, full_kv_w = (
        lax.all_gather(query_weight, "ctx", axis=0, tiled=True),
        lax.all_gather(kv_weight, "ctx", axis=0, tiled=True),
    )
    query_width = full_query_w.shape[1]
    token_piece = lax.all_gather(tokens, "tp", axis=0, tiled=True)
    query_part = jnp.dot(token_piece, full_query_w, preferred_element_type=jnp.float32)
    key_part = jnp.dot(token_piece, full_kv_w, preferred_element_type=jnp.float32)
    projected = jnp.concatenate([query_part, key_part], axis=1)
    query_rows = projected[:, :query_width].astype(jnp.bfloat16)
    key_rows = projected[:, query_width:].astype(jnp.bfloat16)
    window_kv, global_kv, random_kv = fetch_blocks(
        key_rows, global_ids, rand_ids, ctx_index, ctx_count
    )
    row_count, lane_width = key_rows.shape
    run_blocks = row_count // BS
    kv_local = lane_width // (2 * HD)
    offsets = jnp.arange(-WMAX, WMAX + 1)
    first_block = ctx_index * run_blocks
    target = first_block + jnp.arange(run_blocks)[:, None] + offsets[None, :]
    window_live = (
        (jnp.abs(offsets)[None, :] <= reach[:, None])
        & (target >= 0)
        & (target < run_blocks * ctx_count)
    )
    own_lists = lax.dynamic_slice_in_dim(rand_ids, first_block, run_blocks, 0)
    slot_valid = jnp.concatenate(
        [window_live, jnp.ones((run_blocks, G), jnp.bool_), own_lists >= 0], axis=1
    )
    global_tiled = jnp.broadcast_to(global_kv[None], (run_blocks,) + global_kv.shape)
    slab_all = jnp.concatenate([window_kv, global_tiled, random_kv], axis=1)
    slot_total = slab_all.shape[1]
    group_size = max((divisor for divisor in range(1, 9) if run_blocks % divisor == 0))
    group_count = run_blocks // group_size
    query_groups = query_rows.reshape(group_count, group_size, BS, query_width)
    slab_groups = slab_all.reshape(group_count, group_size, slot_total, BS, lane_width)
    valid_groups = slot_valid.reshape(group_count, group_size, slot_total)

    def one_group(operands):
        return attend_group(operands[0], operands[1], operands[2], kv_local)

    outputs = lax.map(one_group, (query_groups, slab_groups, valid_groups))
    return outputs.reshape(row_count, query_width)


def solution(mesh):
    in_specs = (P(("ctx", "tp"), None), P("ctx", "tp"), P("ctx", "tp"), P("ctx"), P(), P())
    out_specs = P("ctx", "tp")
    return jax.shard_map(
        per_device, mesh=mesh, in_specs=in_specs, out_specs=out_specs, check_vma=False
    )
```

profile of v0, /device:TPU:16, one launch (start us, length us, event | category | flops | bytes accessed | tf_op | source)
XLA Modules:
  0.0 769.0 jit_solution(11982867577212984012)
XLA Ops:
  8.0 0.9 copy.68
  10.9 144.7 %all-gather.6.cloned.1.call-done = bf16[4096,256]{1,0:T(8,128)(2,1)} async-done(((bf16[64,256]{1,0:T(8,128)(2,1)}), bf16[4096,256]{1,0:T(8,128)(2,1)}) %all-gather.6.cloned.1.call-update) | async-done | bytes 2097168 | tf_op jit(solution)/shard_map/all_gather | solution.py:91
  155.6 54.5 %all-gather.4.cloned.1.call-done = bf16[1024,4096]{1,0:T(8,128)(2,1)} async-done(((bf16[128,4096]{1,0:T(8,128)(2,1)}), bf16[1024,4096]{1,0:T(8,128)(2,1)}) %all-gather.4.cloned.1.call-update) | async-done | bytes 8388624 | tf_op jit(solution)/shard_map/all_gather | solution.py:94
  210.1 6.3 convolution_convert_fusion.1
  216.4 2.7 gather_fusion.1
  219.1 4.5 broadcast_select_fusion
  223.6 16.0 %all-to-all-start = ((bf16[64,2,64,256]{3,2,1,0:T(8,128)(2,1)}), bf16[64,2,64,256]{3,2,1,0:T(8,128)(2,1)}, u32[]{:S(2)}, u32[]{:S(2)}) async-start(bf16[64,2,64,256]{3,2,1,0:T(8,128)(2,1)} %broadcast_select_fusion), calls=%async_computation | async-start | bytes 8388608 | tf_op jit(solution)/shard_map/all_to_all | solution.py:75
  241.8 1.3 collective-permute-start.1
  243.1 4.5 collective-permute-start
  248.3 184.3 %all-gather.8.cloned.1.call-done = bf16[4096,256]{1,0:T(8,128)(2,1)} async-done(((bf16[64,256]{1,0:T(8,128)(2,1)}), bf16[4096,256]{1,0:T(8,128)(2,1)}) %all-gather.8.cloned.1.call-update) | async-done | bytes 2097168 | tf_op jit(solution)/shard_map/all_gather | solution.py:90
  432.6 6.3 convolution_convert_fusion
  438.9 279.9 %all-reduce.1 = bf16[2,64,256]{2,1,0:T(8,128)(2,1)S(1)} all-reduce(f32[2,64,256]{2,1,0:T(8,128)S(1)} %convert_select_fusion), channel_id=1, replica_groups=mesh['ctx'=64,'tp'=8] {'ctx'}, use_global_device_ids=true, to_apply=%region_0.1 | all-reduce | flops 32768 | bytes 196608 | tf_op jit(solution)/shard_map/psum | solution.py:64
  718.9 0.9 constant_dynamic-update-slice_fusion.6
  719.8 0.9 constant_dynamic-update-slice_fusion.5
  720.7 0.9 constant_dynamic-update-slice_fusion.4
  721.5 0.9 constant_dynamic-update-slice_fusion.3
  723.3 1.1 broadcast_dynamic-update-slice_fusion
  724.3 2.8 gather_fusion.2
  727.2 1.3 constant_dynamic-update-slice_fusion.1
  728.5 34.0 %while.10 = (s32[]{:T(128)}, bf16[2,512,256]{2,1,0:T(8,128)(2,1)}, bf16[2,8,10,64,256]{4,3,2,1,0:T(8,128)(2,1)}, pred[2,8,10]{2,1,0:T(8,128)(4,1)S(1)}, bf16[2,8,64,256]{3,2,1,0:T(8,128)(2,1)S(1)}, /*index=5*/s32[]{:T(128)}) while((s32[]{:T(128)}, bf16[2,512,256]{2,1,0:T(8,128)(2,1)}, bf16[2,8,10,64,256]{4,3,2,1,0:T(8,128)(2,1)}, ...), condition=%wide.region_8.9_spmd, body=%wide.region_5.8_spmd.sunk | while | flops 343537664 | bytes 33575460 | solution.py:130
  728.6 3.6 constant_dynamic-slice_fusion.6
  732.2 3.5 reshape.320
  735.7 3.7 fusion.55
  739.4 1.3 bitcast_reduce_fusion.2
  740.7 1.5 fusion.56
  742.3 1.9 fusion.57
  745.6 3.6 constant_dynamic-slice_fusion.6
  749.1 3.5 reshape.320
  752.7 3.7 fusion.55
  756.4 1.3 bitcast_reduce_fusion.2
  757.7 1.5 fusion.56
  759.3 1.9 fusion.57
  (68 shorter events, 9.7 us)
Async XLA Ops:
  6.5 149.0 %all-gather.6.cloned.1.call-start = ((), (), s32[]{:S(2)}) async-start(), calls=%async_computation.2 | async-start | bytes 2129920 | tf_op jit(solution)/shard_map/all_gather | solution.py:91
  7.3 202.8 %all-gather.4.cloned.1.call-start = ((), (), s32[]{:S(2)}) async-start(), calls=%async_computation.1 | async-start | bytes 9437184 | tf_op jit(solution)/shard_map/all_gather | solution.py:94
  223.6 17.6 %copy-start = (s32[16]{0:T(128)S(1)}, s32[16]{0:T(128)}, u32[]{:S(2)}) copy-start(s32[16]{0:T(128)} %param.11) | copy-start | bytes 196
  223.6 18.1 %copy-start.3 = (s32[2]{0:T(128)S(1)}, s32[2]{0:T(128)}, u32[]{:S(2)}) copy-start(s32[2]{0:T(128)} %param.12) | copy-start | bytes 28
  223.6 500.7 %all-to-all-start = ((bf16[64,2,64,256]{3,2,1,0:T(8,128)(2,1)}), bf16[64,2,64,256]{3,2,1,0:T(8,128)(2,1)}, u32[]{:S(2)}, u32[]{:S(2)}) async-start(bf16[64,2,64,256]{3,2,1,0:T(8,128)(2,1)} %broadcast_select_fusion), calls=%async_computation | async-start | bytes 8388608 | tf_op jit(solution)/shard_map/all_to_all | solution.py:75
  239.6 192.9 %all-gather.8.cloned.1.call-start = ((), (), s32[]{:S(2)}) async-start(), calls=%async_computation.3 | async-start | bytes 2129920 | tf_op jit(solution)/shard_map/all_gather | solution.py:90
  241.8 477.0 %collective-permute-start.1 = (bf16[128,256]{1,0:T(8,128)(2,1)S(1)}, bf16[128,256]{1,0:T(8,128)(2,1)S(1)}, u32[]{:S(2)}, u32[]{:S(2)}) collective-permute-start(bf16[128,256]{1,0:T(8,128)(2,1)S(1)} %get-tuple-element.61), channel_id=1, source_target_pairs={{8,0},{16,8},{24,16},{32,24},{40,32},{48,40},{56,48},{64,56},{72,6... | collective-permute-start | bytes 196616 | tf_op jit(solution)/shard_map/ppermute | solution.py:24
  243.1 475.7 %collective-permute-start = (bf16[128,256]{1,0:T(8,128)(2,1)S(1)}, bf16[128,256]{1,0:T(8,128)(2,1)S(1)}, u32[]{:S(2)}, u32[]{:S(2)}) collective-permute-start(bf16[128,256]{1,0:T(8,128)(2,1)S(1)} %get-tuple-element.62), channel_id=1, source_target_pairs={{0,8},{8,16},{16,24},{24,32},{32,40},{40,48},{48,56},{56,64},{64,7... | collective-permute-start | bytes 196616 | tf_op jit(solution)/shard_map/ppermute | solution.py:23
  742.2 2.4 copy-start.1
  744.7 0.8 copy-start.2
  759.2 2.4 copy-start.1
  761.7 0.8 copy-start.2
Sparse Core Ops, SparseCore 0:
  10.3 145.2 all-gather.5
  157.7 52.2 all-gather.3
  243.4 189.1 all-gather.7
where the time goes:
time: 770 us; the launch traced here: 769 us
  waiting for transfers between devices  386 us (50%)
  blocking collectives  280 us (36%)
  local copies, waits for them, and re-layouts  39.2 us (5%)
  starting transfers between devices  21.9 us (3%)
  matrix products  19 us (2%)
  between operations  13.3 us (2%)
  other arithmetic  9.89 us (1%)
    psum x1, blocking collectives, fetch_blocks(): global_kv = lax.psum(sum_term, 'ctx').astype(jnp.bfloat16)  280 us
    all_gather x1, waiting for transfers between devices, per_device(): lax.all_gather(query_weight, 'ctx', axis=0, tiled=True)  184 us
    all_gather x1, waiting for transfers between devices, per_device(): lax.all_gather(kv_weight, 'ctx', axis=0, tiled=True)  145 us
    all_gather x1, waiting for transfers between devices, per_device(): token_piece = lax.all_gather(tokens, 'tp', axis=0, tiled=True)  54.5 us
    all_to_all x1, starting transfers between devices, fetch_blocks(): lax.all_to_all(outgoing, 'ctx', split_axis=0, concat_axis=0, tiled=True)  16 us
  transfers between devices with their start and end apart: 6, of which 3 were waited for; matrix products, arithmetic and copies ran while one was open for 2% of the time, Pallas kernels for 0%

commit v1 on v0

v1 whole, which is shorter than its diff:
```python
import functools

import jax
import jax.numpy as jnp
from jax import lax
from jax.experimental import pallas as pl
from jax.experimental.pallas import tpu as pltpu
from jax.sharding import Mesh, PartitionSpec as P

HD = 128
BS = 64
WMAX = 2
SLOTS = 10
CHUNK = 4
UNROLL = 4
SLOT_ROOM = 12
RUN_BLOCKS = 16
PAD = 16
LOG2E = 1.4426950408889634
MASKED = -1e30
F32 = jnp.float32
BF16 = jnp.bfloat16
NT = (((1,), (1,)), ((), ()))
TN = (((0,), (0,)), ((), ()))


def shift(value, axis, by):
    size = lax.axis_size(axis)
    return lax.ppermute(value, axis, [(i, (i + by) % size) for i in range(size)])


def project_kernel(place, rows, part0, part1, part2, part3, out, weight):
    @pl.when(pl.program_id(0) == 0)
    def _():
        for s, part in enumerate((part0, part1, part2, part3)):
            owner = lax.rem(place[0] + 4 - s, 4)
            for za in range(4):
                for zb in range(4):
                    weight[za * 4 + zb, owner] = part[zb, za]

    depth = rows.shape[1]
    flat = weight[...].reshape(depth, out.shape[1])
    out[...] = jnp.dot(rows[...], flat, preferred_element_type=F32).astype(BF16)


def project(place, rows, parts):
    count, depth = rows.shape
    width = parts[0].shape[-1]
    tile = 256
    whole = pl.BlockSpec(parts[0].shape, lambda i, p: (0, 0, 0, 0))
    return pl.pallas_call(
        project_kernel,
        grid_spec=pltpu.PrefetchScalarGridSpec(
            num_scalar_prefetch=1,
            grid=(count // tile,),
            in_specs=[pl.BlockSpec((tile, depth), lambda i, p: (i, 0))] + [whole] * 4,
            out_specs=pl.BlockSpec((tile, width), lambda i, p: (i, 0)),
            scratch_shapes=[pltpu.VMEM((16, 4, 64, width), BF16)],
        ),
        out_shape=jax.ShapeDtypeStruct((count, width), BF16),
        compiler_params=pltpu.CompilerParams(vmem_limit_bytes=40 << 20),
        cost_estimate=pl.CostEstimate(
            flops=2 * count * depth * width,
            bytes_accessed=2 * (count * depth + depth * width + count * width),
            transcendentals=0,
        ),
        name="project",
    )(place, rows, *parts)


def partial_kernel(from_x, index, counts, query, held, out, slabs, sems):
    base = from_x[0] * RUN_BLOCKS

    def copy(j, p):
        block = index[(base + j) * SLOTS + p]
        return pltpu.make_async_copy(
            held.at[block], slabs.at[j, pl.ds(p * BS, BS)], sems.at[j, p]
        )

    def start_block(j, carry):
        def start(p, inner):
            copy(j, p).start()
            return inner

        return lax.fori_loop(0, counts[base + j], start, carry)

    lax.fori_loop(0, RUN_BLOCKS, start_block, 0)

    def group(g, carry):
        first = g * UNROLL
        live = [counts[base + first + u] for u in range(UNROLL)]

        for u in range(UNROLL):

            def wait(p, inner, u=u):
                copy(first + u, p).wait()
                return inner

            lax.fori_loop(0, live[u], wait, 0)

        most = functools.reduce(jnp.maximum, live)
        row0 = g * (UNROLL * BS + PAD)

        def attend(chunks):
            keys = chunks * CHUNK * BS
            line = lax.broadcasted_iota(jnp.int32, (keys, HD), 0)
            spot = lax.broadcasted_iota(jnp.int32, (PAD, HD), 0)
            stats = jnp.zeros((PAD, HD), F32)
            for u in range(UNROLL):
                q_rows = query[pl.ds((first + u) * BS, BS), :]
                q_both = jnp.concatenate([q_rows[:, :HD], q_rows[:, HD:]], axis=0)
                key = slabs[first + u, 0:keys, 0:HD]
                value = slabs[first + u, 0:keys, HD : 2 * HD]
                inside = line < live[u] * BS
                value = jnp.where(inside, value, jnp.zeros_like(value))
                scores = lax.dot_general(key, q_both, NT, preferred_element_type=F32)
                scores = jnp.where(inside, scores * (HD**-0.5 * LOG2E), MASKED)
                top = jnp.max(scores, axis=0, keepdims=True)
                power = jnp.where(inside, jnp.exp2(scores - top), 0.0)
                total = jnp.sum(power, axis=0, keepdims=True)
                some = total > 0.0
                total = jnp.where(some, total, 1.0)
                weights = (power * (1.0 / total)).astype(BF16)
                mixed = lax.dot_general(weights, value, TN, preferred_element_type=F32)
                mixed = mixed.astype(BF16)
                out[pl.ds(row0 + u * BS, BS), 0:HD] = mixed[:BS]
                out[pl.ds(row0 + u * BS, BS), HD : 2 * HD] = mixed[BS:]
                level = jnp.where(some, top + jnp.log2(total), MASKED)
                high = level.astype(BF16).astype(F32)
                middle = (level - high).astype(BF16).astype(F32)
                low = level - high - middle
                for t, piece in enumerate((high, middle, low)):
                    stats = jnp.where(spot == 3 * u + t, piece, stats)
            out[pl.ds(row0 + UNROLL * BS, PAD), 0:HD] = stats.astype(BF16)
            out[pl.ds(row0 + UNROLL * BS, PAD), HD : 2 * HD] = jnp.zeros((PAD, HD), BF16)

        for chunks in (1, 2, 3):
            low_edge = (chunks - 1) * CHUNK if chunks > 1 else -1

            @pl.when((most > low_edge) & (most <= chunks * CHUNK))
            def _(chunks=chunks):
                attend(chunks)

        return carry

    lax.fori_loop(0, RUN_BLOCKS // UNROLL, group, 0)


def partial_attention(from_x, index, counts, query, held):
    rows = RUN_BLOCKS // UNROLL * (UNROLL * BS + PAD)
    smem = pl.BlockSpec(memory_space=pltpu.SMEM)
    vmem = pl.BlockSpec(memory_space=pltpu.VMEM)
    return pl.pallas_call(
        partial_kernel,
        in_specs=[smem, smem, smem, vmem, pl.BlockSpec(memory_space=pl.ANY)],
        out_specs=vmem,
        out_shape=jax.ShapeDtypeStruct((rows, 2 * HD), BF16),
        scratch_shapes=[
            pltpu.VMEM((RUN_BLOCKS, SLOT_ROOM * BS, 2 * HD), BF16),
            pltpu.SemaphoreType.DMA((RUN_BLOCKS, SLOTS)),
        ],
        compiler_params=pltpu.CompilerParams(vmem_limit_bytes=40 << 20),
        cost_estimate=pl.CostEstimate(
            flops=10 * 10**9, bytes_accessed=4 << 20, transcendentals=0
        ),
        name="partial_attention",
    )(from_x, index, counts, query, held)


def combine_kernel(part0, part1, part2, part3, out):
    parts = (part0, part1, part2, part3)
    spot = lax.broadcasted_iota(jnp.int32, (HD, HD), 0)
    tail = [part[pl.ds(UNROLL * BS, PAD), 0:HD].astype(F32) for part in parts]
    for u in range(UNROLL):
        levels = [
            t[3 * u : 3 * u + 1] + t[3 * u + 1 : 3 * u + 2] + t[3 * u + 2 : 3 * u + 3]
            for t in tail
        ]
        top = functools.reduce(jnp.maximum, levels)
        shares = [jnp.exp2(level - top) for level in levels]
        norm = 1.0 / functools.reduce(jnp.add, shares)
        table = jnp.zeros((HD, HD), F32)
        for k, share in enumerate(shares):
            table = jnp.where(spot == k, share * norm, table)
        table = table.T
        for h in range(2):
            lanes = slice(h * HD, (h + 1) * HD)
            mixed = jnp.zeros((BS, HD), F32)
            for k, part in enumerate(parts):
                scale = table[h * BS : (h + 1) * BS, k : k + 1]
                mixed += scale * part[u * BS : (u + 1) * BS, lanes].astype(F32)
            out[u * BS : (u + 1) * BS, lanes] = mixed.astype(BF16)


def combine(parts):
    groups = RUN_BLOCKS // UNROLL
    spec = pl.BlockSpec((UNROLL * BS + PAD, 2 * HD), lambda i: (i, 0))
    return pl.pallas_call(
        combine_kernel,
        grid=(groups,),
        in_specs=[spec] * 4,
        out_specs=pl.BlockSpec((UNROLL * BS, 2 * HD), lambda i: (i, 0)),
        out_shape=jax.ShapeDtypeStruct((RUN_BLOCKS * BS, 2 * HD), BF16),
        name="combine",
    )(*parts)


def slot_lists(reach_plane, global_ids, rand_ids, plane, place):
    plane_blocks = 4 * RUN_BLOCKS
    block_total = rand_ids.shape[0]
    first = plane * plane_blocks
    blocks = first + jnp.arange(plane_blocks, dtype=jnp.int32)
    offsets = jnp.arange(-WMAX, WMAX + 1, dtype=jnp.int32)
    target = blocks[:, None] + offsets[None, :]
    window_live = (
        (jnp.abs(offsets)[None, :] <= reach_plane[:, None])
        & (target >= 0)
        & (target < block_total)
    )
    listed = lax.dynamic_slice_in_dim(rand_ids, first, plane_blocks, 0)
    globals_all = jnp.broadcast_to(global_ids[None, :], (plane_blocks, global_ids.shape[0]))
    slots = jnp.concatenate([target, globals_all, listed], axis=1)
    live = jnp.concatenate(
        [window_live, jnp.ones(globals_all.shape, jnp.bool_), listed >= 0], axis=1
    )
    held = live & ((slots >> 4) % 4 == place)
    local = (slots >> 6) * RUN_BLOCKS + (slots & (RUN_BLOCKS - 1))
    order = jnp.arange(SLOTS)
    before = order[:, None] < order[None, :]
    rank = jnp.sum(jnp.where(held[:, :, None] & before[None], 1, 0), axis=1)
    at = held[:, :, None] & (rank[:, :, None] == order[None, None, :])
    index = jnp.sum(jnp.where(at, local[:, :, None], 0), axis=1)
    counts = jnp.sum(held.astype(jnp.int32), axis=1)
    return index.reshape(-1).astype(jnp.int32), counts.astype(jnp.int32)


def per_device(tokens, query_weight, kv_weight, reach, global_ids, rand_ids):
    place = lax.axis_index("x").astype(jnp.int32)
    plane = (lax.axis_index("a") * 4 + lax.axis_index("b")).astype(jnp.int32)
    width = query_weight.shape[1]

    rows = lax.all_gather(tokens, ("y", "c"), axis=0, tiled=True)

    both = jnp.concatenate([kv_weight, query_weight], axis=1)
    both = lax.all_gather(both, "a", axis=0, tiled=True)
    kv_own = lax.all_gather(both[:, :width], "b", axis=0, tiled=True)
    query_own_in, kv_own = lax.optimization_barrier((both[:, width:], kv_own))
    query_own = lax.all_gather(query_own_in, "b", axis=0, tiled=True)

    def spread(own):
        own = own.reshape(4, 4, 64, width)
        return [own] + [shift(own, "x", s) for s in (1, 2, 3)]

    place_1 = place.reshape(1)
    kv_rows = project(place_1, rows, spread(kv_own))
    held = lax.all_gather(kv_rows, ("a", "b"), axis=0, tiled=True)
    held = held.reshape(-1, BS, 2 * HD)
    query_rows = project(place_1, rows, spread(query_own))
    queries = [query_rows] + [shift(query_rows, "x", s) for s in (1, 2, 3)]

    reach_plane = lax.all_gather(reach, "x", axis=0, tiled=True)
    index, counts = slot_lists(reach_plane, global_ids, rand_ids, plane, place)

    parts = [None] * 4
    for s in (2, 1, 3, 0):
        from_x = ((place + 4 - s) % 4).reshape(1)
        part = partial_attention(from_x, index, counts, queries[s], held)
        parts[s] = part if s == 0 else shift(part, "x", 4 - s)
    return combine(parts)


def solution(mesh):
    inner = Mesh(mesh.devices.reshape(4, 4, 4, 4, 2), ("a", "b", "x", "y", "c"))
    ctx, tp = ("a", "b", "x"), ("y", "c")
    in_specs = (P(ctx + tp, None), P(ctx, tp), P(ctx, tp), P(ctx), P(), P())
    return jax.shard_map(
        per_device, mesh=inner, in_specs=in_specs, out_specs=P(ctx, tp), check_vma=False
    )
```

time: 770 us -> 252 us (0.33)
  the two profiles are of different devices: /device:TPU:16 before, /device:TPU:1 now
where the time goes in v1:
time: 252 us; the launch traced here: 251 us
  blocking collectives  67.3 us (27%)
  waiting for transfers between devices  62.7 us (25%)
  starting transfers between devices  48 us (19%)
  Pallas kernels  41.2 us (16%)
  local copies, waits for them, and re-layouts  15.4 us (6%)
  between operations  14.4 us (6%)
    ppermute x12, starting transfers between devices, shift(): lax.ppermute(value, axis, [(i, (i + by) % size) for i in range(size)])  48 us
    all_gather x1, waiting for transfers between devices, per_device(): held = lax.all_gather(kv_rows, ('a', 'b'), axis=0, tiled=True)  41.9 us
    pallas_call x4, Pallas kernels, partial_attention(): pl.pallas_call(partial_kernel, in_specs=[smem, smem, smem, vmem, pl.Block...  29.7 us
    all_gather x1, blocking collectives, per_device(): both = lax.all_gather(both, 'a', axis=0, tiled=True)  25.2 us
    ppermute x12, waiting for transfers between devices, shift(): lax.ppermute(value, axis, [(i, (i + by) % size) for i in range(size)])  20 us
    unnamed x1, blocking collectives  15.9 us
    unnamed x25, local copies, waits for them, and re-layouts  15 us
    all_gather x1, blocking collectives, per_device(): query_own = lax.all_gather(query_own_in, 'b', axis=0, tiled=True)  13.4 us
  transfers between devices with their start and end apart: 14, of which 6 were waited for; matrix products, arithmetic and copies ran while one was open for 2% of the time, Pallas kernels for 13%

profile of v1, /device:TPU:1, one launch (start us, length us, event | category | flops | bytes accessed | tf_op | source)
XLA Modules:
  0.0 251.0 jit_solution(7444033200982712394)
XLA Ops:
  8.1 25.2 %all_gather.20 = bf16[256,512]{1,0:T(8,128)(2,1)S(1)} all-gather(bf16[64,512]{1,0:T(8,128)(2,1)S(1)} %pad_maximum_fusion), channel_id=1, replica_groups=mesh['a'=4,'b'=4,'x'=4,'y'=4,'c'=2] {'a'}, dimensions={0}, use_global_device_ids=true | all-gather | bytes 327680 | tf_op jit(solution)/shard_map/all_gather | solution.py:245
  33.4 12.8 %all_gather.21 = bf16[1024,256]{1,0:T(8,128)(2,1)S(1)} all-gather(bf16[256,256]{1,0:T(8,128)(2,1)S(1)} %get-tuple-element.13), channel_id=1, replica_groups=mesh['a'=4,'b'=4,'x'=4,'y'=4,'c'=2] {'b'}, dimensions={0}, use_global_device_ids=true | all-gather | bytes 655360 | tf_op jit(solution)/shard_map/all_gather | solution.py:246
  46.1 3.1 %collective-permute-start.3 = (bf16[4,4,64,256]{3,2,1,0:T(8,128)(2,1)S(1)}, bf16[4,4,64,256]{3,2,1,0:T(8,128)(2,1)S(1)}, u32[]{:S(2)}, u32[]{:S(2)}) collective-permute-start(bf16[4,4,64,256]{3,2,1,0:T(8,128)(2,1)S(1)} %bitcast.13), channel_id=1, source_target_pairs={{0,8},{8,16},{16,24},{24,0},{1,9},{9,17},{17,25},{25,1},{2,10},{10... | collective-permute-start | bytes 1572872 | tf_op jit(solution)/shard_map/ppermute | solution.py:29
  49.2 4.4 %collective-permute-start.4 = (bf16[4,4,64,256]{3,2,1,0:T(8,128)(2,1)S(1)}, bf16[4,4,64,256]{3,2,1,0:T(8,128)(2,1)S(1)}, u32[]{:S(2)}, u32[]{:S(2)}) collective-permute-start(bf16[4,4,64,256]{3,2,1,0:T(8,128)(2,1)S(1)} %bitcast.14), channel_id=1, source_target_pairs={{0,16},{8,24},{16,0},{24,8},{1,17},{9,25},{17,1},{25,9},{2,18},{10... | collective-permute-start | bytes 1572872 | tf_op jit(solution)/shard_map/ppermute | solution.py:29
  53.6 3.1 %collective-permute-start.5 = (bf16[4,4,64,256]{3,2,1,0:T(8,128)(2,1)S(1)}, bf16[4,4,64,256]{3,2,1,0:T(8,128)(2,1)S(1)}, u32[]{:S(2)}, u32[]{:S(2)}) collective-permute-start(bf16[4,4,64,256]{3,2,1,0:T(8,128)(2,1)S(1)} %bitcast.15), channel_id=1, source_target_pairs={{0,24},{8,0},{16,8},{24,16},{1,25},{9,1},{17,9},{25,17},{2,26},{10... | collective-permute-start | bytes 1572872 | tf_op jit(solution)/shard_map/ppermute | solution.py:29
  57.6 11.0 %collective-permute-done.4.part2 = bf16[4,4,64,256]{3,2,1,0:T(8,128)(2,1)S(1)} collective-permute-done((bf16[4,4,64,256]{3,2,1,0:T(8,128)(2,1)S(1)}, bf16[4,4,64,256]{3,2,1,0:T(8,128)(2,1)S(1)}, u32[]{:S(2)}, u32[]{:S(2)}) %collective-permute-start.4) | collective-permute-done | bytes 524320 | tf_op jit(solution)/shard_map/ppermute | solution.py:29
  68.6 4.2 %collective-permute-done.5.part3 = bf16[4,4,64,256]{3,2,1,0:T(8,128)(2,1)S(1)} collective-permute-done((bf16[4,4,64,256]{3,2,1,0:T(8,128)(2,1)S(1)}, bf16[4,4,64,256]{3,2,1,0:T(8,128)(2,1)S(1)}, u32[]{:S(2)}, u32[]{:S(2)}) %collective-permute-start.5) | collective-permute-done | bytes 524320 | tf_op jit(solution)/shard_map/ppermute | solution.py:29
  72.8 3.4 %copy-done = bf16[1024,4096]{1,0:T(8,128)(2,1)S(1)} copy-done((bf16[1024,4096]{1,0:T(8,128)(2,1)S(1)}, bf16[1024,4096]{1,0:T(8,128)(2,1)}, u32[]{:S(2)}) %copy-start) | copy-done | bytes 8388632
  76.2 3.8 %project.3 = bf16[1024,256]{1,0:T(8,128)(2,1)} custom-call(s32[1]{0:T(128)} %bitcast.2.place, bf16[1024,4096]{1,0:T(8,128)(2,1)S(1)} %copy-done, bf16[4,4,64,256]{3,2,1,0:T(8,128)(2,1)S(1)} %bitcast.16, bf16[4,4,64,256]{3,2,1,0:T(8,128)(2,1)S(1)} %collective-permute-done.3.part1, bf16[4,4,64,256]{3,2,1,0:T(8,128)(2,1)S(1)} %collective-permute-done.4.part2, ...), custom_call_target="tpu_custom_call" | custom-call | flops 2147483648 | bytes 11010048 | tf_op jit(solution)/shard_map/project/pallas_call | solution.py:51
  80.0 13.4 %all_gather.22 = bf16[1024,256]{1,0:T(8,128)(2,1)S(1)} all-gather(bf16[256,256]{1,0:T(8,128)(2,1)S(1)} %get-tuple-element.7), channel_id=1, replica_groups=mesh['a'=4,'b'=4,'x'=4,'y'=4,'c'=2] {'b'}, dimensions={0}, use_global_device_ids=true | all-gather | bytes 655360 | tf_op jit(solution)/shard_map/all_gather | solution.py:248
  93.4 6.1 %collective-permute-start = (bf16[4,4,64,256]{3,2,1,0:T(8,128)(2,1)S(1)}, bf16[4,4,64,256]{3,2,1,0:T(8,128)(2,1)S(1)}, u32[]{:S(2)}, u32[]{:S(2)}) collective-permute-start(bf16[4,4,64,256]{3,2,1,0:T(8,128)(2,1)S(1)} %bitcast.9), channel_id=1, source_target_pairs={{0,8},{8,16},{16,24},{24,0},{1,9},{9,17},{17,25},{25,1},{2,10},{10... | collective-permute-start | bytes 1572872 | tf_op jit(solution)/shard_map/ppermute | solution.py:29
  99.5 2.0 collective-permute-start.1
  101.5 4.2 %collective-permute-start.2 = (bf16[4,4,64,256]{3,2,1,0:T(8,128)(2,1)S(1)}, bf16[4,4,64,256]{3,2,1,0:T(8,128)(2,1)S(1)}, u32[]{:S(2)}, u32[]{:S(2)}) collective-permute-start(bf16[4,4,64,256]{3,2,1,0:T(8,128)(2,1)S(1)} %bitcast.11), channel_id=1, source_target_pairs={{0,24},{8,0},{16,8},{24,16},{1,25},{9,1},{17,9},{25,17},{2,26},{10... | collective-permute-start | bytes 1572872 | tf_op jit(solution)/shard_map/ppermute | solution.py:29
  106.0 1.3 dynamic-slice
  108.2 15.9 %all-reduce = s32[64]{0:T(128)S(1)} all-reduce(s32[64]{0:T(128)S(1)} %dynamic-update-slice), channel_id=1, replica_groups=mesh['a'=4,'b'=4,'x'=4,'y'=4,'c'=2] {'x'}, use_global_device_ids=true, to_apply=%add | all-reduce | flops 64 | bytes 512
  125.0 3.5 %copy-done.1 = bf16[1024,4096]{1,0:T(8,128)(2,1)S(1)} copy-done((bf16[1024,4096]{1,0:T(8,128)(2,1)S(1)}, bf16[1024,4096]{1,0:T(8,128)(2,1)}, u32[]{:S(2)}) %copy-start.1) | copy-done | bytes 8388632
  128.4 3.1 %project.2.query = bf16[1024,256]{1,0:T(8,128)(2,1)S(1)} custom-call(s32[1]{0:T(128)} %bitcast.2.place, bf16[1024,4096]{1,0:T(8,128)(2,1)S(1)} %copy-done.1, bf16[4,4,64,256]{3,2,1,0:T(8,128)(2,1)S(1)} %bitcast.12, bf16[4,4,64,256]{3,2,1,0:T(8,128)(2,1)S(1)} %collective-permute-done.part1, bf16[4,4,64,256]{3,2,1,0:T(8,128)(2,1)S(1)} %collective-permute-done.1.part2, ...), custom_call_target="tpu_custom_call" | custom-call | flops 2147483648 | bytes 11010048 | tf_op jit(solution)/shard_map/project/pallas_call | solution.py:51
  131.5 3.9 %collective-permute-start.6 = (bf16[1024,256]{1,0:T(8,128)(2,1)S(1)}, bf16[1024,256]{1,0:T(8,128)(2,1)S(1)}, u32[]{:S(2)}, u32[]{:S(2)}) collective-permute-start(bf16[1024,256]{1,0:T(8,128)(2,1)S(1)} %project.2.query), channel_id=1, source_target_pairs={{0,8},{8,16},{16,24},{24,0},{1,9},{9,17},{17,25},{25,1},{2,10},{10... | collective-permute-start | bytes 1572872 | tf_op jit(solution)/shard_map/ppermute | solution.py:29
  136.0 1.9 collective-permute-start.8
  137.9 4.3 %collective-permute-start.10 = (bf16[1024,256]{1,0:T(8,128)(2,1)S(1)}, bf16[1024,256]{1,0:T(8,128)(2,1)S(1)}, u32[]{:S(2)}, u32[]{:S(2)}) collective-permute-start(bf16[1024,256]{1,0:T(8,128)(2,1)S(1)} %project.2.query), channel_id=1, source_target_pairs={{0,24},{8,0},{16,8},{24,16},{1,25},{9,1},{17,9},{25,17},{2,26},{10... | collective-permute-start | bytes 1572872 | tf_op jit(solution)/shard_map/ppermute | solution.py:29
  142.3 1.7 collective-permute-done.6.query
  143.9 41.9 %all-gather.5.cloned.1.call-done = bf16[16384,256]{1,0:T(8,128)(2,1)} async-done(((bf16[1024,256]{1,0:T(8,128)(2,1)}), bf16[16384,256]{1,0:T(8,128)(2,1)}) %all-gather.5.cloned.1.call-update) | async-done | bytes 8388624 | tf_op jit(solution)/shard_map/all_gather | solution.py:256
  185.9 3.4 %copy-done.3 = bf16[16384,256]{1,0:T(8,128)(2,1)S(1)} copy-done((bf16[16384,256]{1,0:T(8,128)(2,1)S(1)}, bf16[16384,256]{1,0:T(8,128)(2,1)}, u32[]{:S(2)}) %copy-start.3) | copy-done | bytes 8388632
  189.3 6.1 %partial_attention.5 = bf16[1088,256]{1,0:T(8,128)(2,1)S(1)} custom-call(s32[1]{0:T(128)} %bitcast.6.from_x, s32[640]{0:T(1024)S(1)} %reshape.195.index, s32[64]{0:T(128)S(1)} %get-tuple-element.9.counts, bf16[1024,256]{1,0:T(8,128)(2,1)S(1)} %collective-permute-done.6.query, bf16[256,64,256]{2,1,0:T(8,128)(2,1)S(1)} %bitcast.17), custom_call_target="tpu_custom_call" | custom-call | flops 10000000000 | bytes 4194304 | tf_op jit(solution)/shard_map/partial_attention/pallas_call | solution.py:153
  195.4 7.1 %collective-permute-start.7 = (bf16[1088,256]{1,0:T(8,128)(2,1)S(1)}, bf16[1088,256]{1,0:T(8,128)(2,1)S(1)}, u32[]{:S(2)}, u32[]{:S(2)}) collective-permute-start(bf16[1088,256]{1,0:T(8,128)(2,1)S(1)} %partial_attention.5), channel_id=1, source_target_pairs={{0,24},{8,0},{16,8},{24,16},{1,25},{9,1},{17,9},{25,17},{2,26},{10... | collective-permute-start | bytes 1671176 | tf_op jit(solution)/shard_map/ppermute | solution.py:29
  202.5 6.3 %partial_attention.6 = bf16[1088,256]{1,0:T(8,128)(2,1)S(1)} custom-call(s32[1]{0:T(128)} %bitcast.7.from_x, s32[640]{0:T(1024)S(1)} %reshape.195.index, s32[64]{0:T(128)S(1)} %get-tuple-element.9.counts, bf16[1024,256]{1,0:T(8,128)(2,1)S(1)} %collective-permute-done.8.query, bf16[256,64,256]{2,1,0:T(8,128)(2,1)S(1)} %bitcast.18), custom_call_target="tpu_custom_call" | custom-call | flops 10000000000 | bytes 4194304 | tf_op jit(solution)/shard_map/partial_attention/pallas_call | solution.py:153
  208.8 2.1 collective-permute-start.9
  210.9 6.1 %partial_attention.7 = bf16[1088,256]{1,0:T(8,128)(2,1)S(1)} custom-call(s32[1]{0:T(128)} %bitcast.8.from_x, s32[640]{0:T(1024)S(1)} %reshape.195.index, s32[64]{0:T(128)S(1)} %get-tuple-element.9.counts, bf16[1024,256]{1,0:T(8,128)(2,1)S(1)} %collective-permute-done.10.query, bf16[256,64,256]{2,1,0:T(8,128)(2,1)S(1)} %bitcast.19), custom_call_target="tpu_custom_call" | custom-call | flops 10000000000 | bytes 4194304 | tf_op jit(solution)/shard_map/partial_attention/pallas_call | solution.py:153
  217.0 5.8 %collective-permute-start.11 = (bf16[1088,256]{1,0:T(8,128)(2,1)S(1)}, bf16[1088,256]{1,0:T(8,128)(2,1)S(1)}, u32[]{:S(2)}, u32[]{:S(2)}) collective-permute-start(bf16[1088,256]{1,0:T(8,128)(2,1)S(1)} %partial_attention.7), channel_id=1, source_target_pairs={{0,8},{8,16},{16,24},{24,0},{1,9},{9,17},{17,25},{25,1},{2,10},{10... | collective-permute-start | bytes 1671176 | tf_op jit(solution)/shard_map/ppermute | solution.py:29
  222.8 11.2 %partial_attention.4.part0 = bf16[1088,256]{1,0:T(8,128)(2,1)S(1)} custom-call(s32[1]{0:T(128)} %bitcast.from_x, s32[640]{0:T(1024)S(1)} %reshape.195.index, s32[64]{0:T(128)S(1)} %get-tuple-element.9.counts, bf16[1024,256]{1,0:T(8,128)(2,1)S(1)} %project.2.query, bf16[256,64,256]{2,1,0:T(8,128)(2,1)S(1)} %bitcast.22), custom_call_target="tpu_custom_call" | custom-call | flops 10000000000 | bytes 4194304 | tf_op jit(solution)/shard_map/partial_attention/pallas_call | solution.py:153
  236.5 2.2 collective-permute-done.11.part3
  239.5 4.7 %combine.1 = bf16[1024,256]{1,0:T(8,128)(2,1)} custom-call(bf16[1088,256]{1,0:T(8,128)(2,1)} %copy-done.2, bf16[1088,256]{1,0:T(8,128)(2,1)} %copy-done.4, bf16[1088,256]{1,0:T(8,128)(2,1)} %copy-done.5, bf16[1088,256]{1,0:T(8,128)(2,1)} %copy-done.6), custom_call_target="tpu_custom_call" | custom-call | tf_op jit(solution)/shard_map/combine/pallas_call | solution.py:198
  (51 shorter events, 7.6 us)
Async XLA Ops:
  6.5 99.3 %copy-start.7 = (s32[2]{0:T(128)S(1)}, s32[2]{0:T(128)}, u32[]{:S(2)}) copy-start(s32[2]{0:T(128)} %param.10) | copy-start | bytes 28
  6.5 101.4 %copy-start.8 = (s32[16]{0:T(128)S(1)}, s32[16]{0:T(128)}, u32[]{:S(2)}) copy-start(s32[16]{0:T(128)} %param.9) | copy-start | bytes 196
  6.5 66.3 %all-gather.3.cloned.1.call-start = ((), (), s32[]{:S(2)}) async-start(), calls=%async_computation | async-start | bytes 9437184 | tf_op jit(solution)/shard_map/all_gather | solution.py:242
  7.3 178.6 %all-gather.5.cloned.1.call-start = ((), (), s32[]{:S(2)}) async-start(), calls=%async_computation.1 | async-start | bytes 8912896 | tf_op jit(solution)/shard_map/all_gather | solution.py:256
  46.1 11.5 %collective-permute-start.3 = (bf16[4,4,64,256]{3,2,1,0:T(8,128)(2,1)S(1)}, bf16[4,4,64,256]{3,2,1,0:T(8,128)(2,1)S(1)}, u32[]{:S(2)}, u32[]{:S(2)}) collective-permute-start(bf16[4,4,64,256]{3,2,1,0:T(8,128)(2,1)S(1)} %bitcast.13), channel_id=1, source_target_pairs={{0,8},{8,16},{16,24},{24,0},{1,9},{9,17},{17,25},{25,1},{2,10},{10... | collective-permute-start | bytes 1572872 | tf_op jit(solution)/shard_map/ppermute | solution.py:29
  49.2 19.4 %collective-permute-start.4 = (bf16[4,4,64,256]{3,2,1,0:T(8,128)(2,1)S(1)}, bf16[4,4,64,256]{3,2,1,0:T(8,128)(2,1)S(1)}, u32[]{:S(2)}, u32[]{:S(2)}) collective-permute-start(bf16[4,4,64,256]{3,2,1,0:T(8,128)(2,1)S(1)} %bitcast.14), channel_id=1, source_target_pairs={{0,16},{8,24},{16,0},{24,8},{1,17},{9,25},{17,1},{25,9},{2,18},{10... | collective-permute-start | bytes 1572872 | tf_op jit(solution)/shard_map/ppermute | solution.py:29
  53.6 19.2 %collective-permute-start.5 = (bf16[4,4,64,256]{3,2,1,0:T(8,128)(2,1)S(1)}, bf16[4,4,64,256]{3,2,1,0:T(8,128)(2,1)S(1)}, u32[]{:S(2)}, u32[]{:S(2)}) collective-permute-start(bf16[4,4,64,256]{3,2,1,0:T(8,128)(2,1)S(1)} %bitcast.15), channel_id=1, source_target_pairs={{0,24},{8,0},{16,8},{24,16},{1,25},{9,1},{17,9},{25,17},{2,26},{10... | collective-permute-start | bytes 1572872 | tf_op jit(solution)/shard_map/ppermute | solution.py:29
  72.8 3.4 %copy-start = (bf16[1024,4096]{1,0:T(8,128)(2,1)S(1)}, bf16[1024,4096]{1,0:T(8,128)(2,1)}, u32[]{:S(2)}) copy-start(bf16[1024,4096]{1,0:T(8,128)(2,1)} %all-gather.3.cloned.1.call-done.rows) | copy-start | bytes 25165828
  93.4 31.6 %collective-permute-start = (bf16[4,4,64,256]{3,2,1,0:T(8,128)(2,1)S(1)}, bf16[4,4,64,256]{3,2,1,0:T(8,128)(2,1)S(1)}, u32[]{:S(2)}, u32[]{:S(2)}) collective-permute-start(bf16[4,4,64,256]{3,2,1,0:T(8,128)(2,1)S(1)} %bitcast.9), channel_id=1, source_target_pairs={{0,8},{8,16},{16,24},{24,0},{1,9},{9,17},{17,25},{25,1},{2,10},{10... | collective-permute-start | bytes 1572872 | tf_op jit(solution)/shard_map/ppermute | solution.py:29
  99.5 25.4 %collective-permute-start.1 = (bf16[4,4,64,256]{3,2,1,0:T(8,128)(2,1)S(1)}, bf16[4,4,64,256]{3,2,1,0:T(8,128)(2,1)S(1)}, u32[]{:S(2)}, u32[]{:S(2)}) collective-permute-start(bf16[4,4,64,256]{3,2,1,0:T(8,128)(2,1)S(1)} %bitcast.10), channel_id=1, source_target_pairs={{0,16},{8,24},{16,0},{24,8},{1,17},{9,25},{17,1},{25,9},{2,18},{10... | collective-permute-start | bytes 1572872 | tf_op jit(solution)/shard_map/ppermute | solution.py:29
  101.5 23.4 %collective-permute-start.2 = (bf16[4,4,64,256]{3,2,1,0:T(8,128)(2,1)S(1)}, bf16[4,4,64,256]{3,2,1,0:T(8,128)(2,1)S(1)}, u32[]{:S(2)}, u32[]{:S(2)}) collective-permute-start(bf16[4,4,64,256]{3,2,1,0:T(8,128)(2,1)S(1)} %bitcast.11), channel_id=1, source_target_pairs={{0,24},{8,0},{16,8},{24,16},{1,25},{9,1},{17,9},{25,17},{2,26},{10... | collective-permute-start | bytes 1572872 | tf_op jit(solution)/shard_map/ppermute | solution.py:29
  125.0 3.5 %copy-start.1 = (bf16[1024,4096]{1,0:T(8,128)(2,1)S(1)}, bf16[1024,4096]{1,0:T(8,128)(2,1)}, u32[]{:S(2)}) copy-start(bf16[1024,4096]{1,0:T(8,128)(2,1)} %all-gather.3.cloned.1.call-done.rows) | copy-start | bytes 25165828
  131.5 12.4 %collective-permute-start.6 = (bf16[1024,256]{1,0:T(8,128)(2,1)S(1)}, bf16[1024,256]{1,0:T(8,128)(2,1)S(1)}, u32[]{:S(2)}, u32[]{:S(2)}) collective-permute-start(bf16[1024,256]{1,0:T(8,128)(2,1)S(1)} %project.2.query), channel_id=1, source_target_pairs={{0,8},{8,16},{16,24},{24,0},{1,9},{9,17},{17,25},{25,1},{2,10},{10... | collective-permute-start | bytes 1572872 | tf_op jit(solution)/shard_map/ppermute | solution.py:29
  136.0 66.4 %collective-permute-start.8 = (bf16[1024,256]{1,0:T(8,128)(2,1)S(1)}, bf16[1024,256]{1,0:T(8,128)(2,1)S(1)}, u32[]{:S(2)}, u32[]{:S(2)}) collective-permute-start(bf16[1024,256]{1,0:T(8,128)(2,1)S(1)} %project.2.query), channel_id=1, source_target_pairs={{0,16},{8,24},{16,0},{24,8},{1,17},{9,25},{17,1},{25,9},{2,18},{10... | collective-permute-start | bytes 1572872 | tf_op jit(solution)/shard_map/ppermute | solution.py:29
  137.9 72.9 %collective-permute-start.10 = (bf16[1024,256]{1,0:T(8,128)(2,1)S(1)}, bf16[1024,256]{1,0:T(8,128)(2,1)S(1)}, u32[]{:S(2)}, u32[]{:S(2)}) collective-permute-start(bf16[1024,256]{1,0:T(8,128)(2,1)S(1)} %project.2.query), channel_id=1, source_target_pairs={{0,24},{8,0},{16,8},{24,16},{1,25},{9,1},{17,9},{25,17},{2,26},{10... | collective-permute-start | bytes 1572872 | tf_op jit(solution)/shard_map/ppermute | solution.py:29
  185.9 3.4 %copy-start.3 = (bf16[16384,256]{1,0:T(8,128)(2,1)S(1)}, bf16[16384,256]{1,0:T(8,128)(2,1)}, u32[]{:S(2)}) copy-start(bf16[16384,256]{1,0:T(8,128)(2,1)} %all-gather.5.cloned.1.call-done) | copy-start | bytes 25165828
  195.4 39.5 %collective-permute-start.7 = (bf16[1088,256]{1,0:T(8,128)(2,1)S(1)}, bf16[1088,256]{1,0:T(8,128)(2,1)S(1)}, u32[]{:S(2)}, u32[]{:S(2)}) collective-permute-start(bf16[1088,256]{1,0:T(8,128)(2,1)S(1)} %partial_attention.5), channel_id=1, source_target_pairs={{0,24},{8,0},{16,8},{24,16},{1,25},{9,1},{17,9},{25,17},{2,26},{10... | collective-permute-start | bytes 1671176 | tf_op jit(solution)/shard_map/ppermute | solution.py:29
  202.4 20.3 %slice-start = ((s8[8388608]{0:T(1024)(128)(4,1)}), s8[4194304]{0:T(1024)(128)(4,1)S(1)}, s32[]{:S(2)}) async-start(s8[8388608]{0:T(1024)(128)(4,1)} %bitcast.20), calls=%async_computation.2 | async-start | bytes 8388608
  208.8 26.1 %collective-permute-start.9 = (bf16[1088,256]{1,0:T(8,128)(2,1)S(1)}, bf16[1088,256]{1,0:T(8,128)(2,1)S(1)}, u32[]{:S(2)}, u32[]{:S(2)}) collective-permute-start(bf16[1088,256]{1,0:T(8,128)(2,1)S(1)} %partial_attention.6), channel_id=1, source_target_pairs={{0,16},{8,24},{16,0},{24,8},{1,17},{9,25},{17,1},{25,9},{2,18},{10... | collective-permute-start | bytes 1671176 | tf_op jit(solution)/shard_map/ppermute | solution.py:29
  210.9 11.9 %slice-start.1 = ((s8[8388608]{0:T(1024)(128)(4,1)}), s8[4194304]{0:T(1024)(128)(4,1)S(1)}, s32[]{:S(2)}) async-start(s8[8388608]{0:T(1024)(128)(4,1)} %bitcast.20), calls=%async_computation.3 | async-start | bytes 8388608
  217.0 21.7 %collective-permute-start.11 = (bf16[1088,256]{1,0:T(8,128)(2,1)S(1)}, bf16[1088,256]{1,0:T(8,128)(2,1)S(1)}, u32[]{:S(2)}, u32[]{:S(2)}) collective-permute-start(bf16[1088,256]{1,0:T(8,128)(2,1)S(1)} %partial_attention.7), channel_id=1, source_target_pairs={{0,8},{8,16},{16,24},{24,0},{1,9},{9,17},{17,25},{25,1},{2,10},{10... | collective-permute-start | bytes 1671176 | tf_op jit(solution)/shard_map/ppermute | solution.py:29
  234.0 0.8 copy-start.2
  234.8 0.8 copy-start.4
  235.6 0.8 copy-start.5
  238.7 0.8 copy-start.6
Sparse Core Ops, SparseCore 0:
  9.5 63.1 all-gather.2
  80.1 105.7 all-gather.4

commit v2 on v1

--- a/solution.py
+++ b/solution.py
@@ -10,10 +10,9 @@
 HD = 128
 BS = 64
 WMAX = 2
-SLOTS = 10
-CHUNK = 4
+CHUNK = 2
 UNROLL = 4
-SLOT_ROOM = 12
+SLOT_ROOM = 8
 RUN_BLOCKS = 16
 PAD = 16
 LOG2E = 1.4426950408889634
@@ -58,7 +57,7 @@
             scratch_shapes=[pltpu.VMEM((16, 4, 64, width), BF16)],
         ),
         out_shape=jax.ShapeDtypeStruct((count, width), BF16),
-        compiler_params=pltpu.CompilerParams(vmem_limit_bytes=40 << 20),
+        compiler_params=pltpu.CompilerParams(vmem_limit_bytes=50 << 20),
         cost_estimate=pl.CostEstimate(
             flops=2 * count * depth * width,
             bytes_accessed=2 * (count * depth + depth * width + count * width),
@@ -72,7 +71,7 @@
     base = from_x[0] * RUN_BLOCKS
 
     def copy(j, p):
-        block = index[(base + j) * SLOTS + p]
+        block = index[(base + j) * SLOT_ROOM + p]
         return pltpu.make_async_copy(
             held.at[block], slabs.at[j, pl.ds(p * BS, BS)], sems.at[j, p]
         )
@@ -134,7 +133,7 @@
             out[pl.ds(row0 + UNROLL * BS, PAD), 0:HD] = stats.astype(BF16)
             out[pl.ds(row0 + UNROLL * BS, PAD), HD : 2 * HD] = jnp.zeros((PAD, HD), BF16)
 
-        for chunks in (1, 2, 3):
+        for chunks in (1, 2, 3, 4):
             low_edge = (chunks - 1) * CHUNK if chunks > 1 else -1
 
             @pl.when((most > low_edge) & (most <= chunks * CHUNK))
@@ -157,9 +156,9 @@
         out_shape=jax.ShapeDtypeStruct((rows, 2 * HD), BF16),
         scratch_shapes=[
             pltpu.VMEM((RUN_BLOCKS, SLOT_ROOM * BS, 2 * HD), BF16),
-            pltpu.SemaphoreType.DMA((RUN_BLOCKS, SLOTS)),
+            pltpu.SemaphoreType.DMA((RUN_BLOCKS, SLOT_ROOM)),
         ],
-        compiler_params=pltpu.CompilerParams(vmem_limit_bytes=40 << 20),
+        compiler_params=pltpu.CompilerParams(vmem_limit_bytes=50 << 20),
         cost_estimate=pl.CostEstimate(
             flops=10 * 10**9, bytes_accessed=4 << 20, transcendentals=0
         ),
@@ -167,55 +166,87 @@
     )(from_x, index, counts, query, held)
 
 
-def combine_kernel(part0, part1, part2, part3, out):
-    parts = (part0, part1, part2, part3)
+def combine_kernel(*refs):
+    parts, out = refs[:-1], refs[-1]
     spot = lax.broadcasted_iota(jnp.int32, (HD, HD), 0)
-    tail = [part[pl.ds(UNROLL * BS, PAD), 0:HD].astype(F32) for part in parts]
-    for u in range(UNROLL):
-        levels = [
-            t[3 * u : 3 * u + 1] + t[3 * u + 1 : 3 * u + 2] + t[3 * u + 2 : 3 * u + 3]
-            for t in tail
-        ]
-        top = functools.reduce(jnp.maximum, levels)
-        shares = [jnp.exp2(level - top) for level in levels]
-        norm = 1.0 / functools.reduce(jnp.add, shares)
-        table = jnp.zeros((HD, HD), F32)
-        for k, share in enumerate(shares):
-            table = jnp.where(spot == k, share * norm, table)
-        table = table.T
-        for h in range(2):
-            lanes = slice(h * HD, (h + 1) * HD)
-            mixed = jnp.zeros((BS, HD), F32)
-            for k, part in enumerate(parts):
-                scale = table[h * BS : (h + 1) * BS, k : k + 1]
-                mixed += scale * part[u * BS : (u + 1) * BS, lanes].astype(F32)
-            out[u * BS : (u + 1) * BS, lanes] = mixed.astype(BF16)
+
+    def group(g, carry):
+        row0 = g * (UNROLL * BS + PAD)
+        tail = [p[pl.ds(row0 + UNROLL * BS, PAD), 0:HD].astype(F32) for p in parts]
+        for u in range(UNROLL):
+            levels = [
+                t[3 * u : 3 * u + 1] + t[3 * u + 1 : 3 * u + 2] + t[3 * u + 2 : 3 * u + 3]
+                for t in tail
+            ]
+            top = functools.reduce(jnp.maximum, levels)
+            shares = [jnp.exp2(level - top) for level in levels]
+            norm = 1.0 / functools.reduce(jnp.add, shares)
+            table = jnp.zeros((HD, HD), F32)
+            for k, share in enumerate(shares):
+                table = jnp.where(spot == k, share * norm, table)
+            table = table.T
+            for h in range(2):
+                lanes = slice(h * HD, (h + 1) * HD)
+                mixed = jnp.zeros((BS, HD), F32)
+                for k, part in enumerate(parts):
+                    scale = table[h * BS : (h + 1) * BS, k : k + 1]
+                    mixed += scale * part[pl.ds(row0 + u * BS, BS), lanes].astype(F32)
+                out[pl.ds((g * UNROLL + u) * BS, BS), lanes] = mixed.astype(BF16)
+        return carry
+
+    lax.fori_loop(0, RUN_BLOCKS // UNROLL, group, 0)
 
 
 def combine(parts):
-    groups = RUN_BLOCKS // UNROLL
-    spec = pl.BlockSpec((UNROLL * BS + PAD, 2 * HD), lambda i: (i, 0))
+    vmem = pl.BlockSpec(memory_space=pltpu.VMEM)
     return pl.pallas_call(
         combine_kernel,
-        grid=(groups,),
-        in_specs=[spec] * 4,
-        out_specs=pl.BlockSpec((UNROLL * BS, 2 * HD), lambda i: (i, 0)),
+        in_specs=[vmem] * len(parts),
+        out_specs=vmem,
         out_shape=jax.ShapeDtypeStruct((RUN_BLOCKS * BS, 2 * HD), BF16),
+        compiler_params=pltpu.CompilerParams(vmem_limit_bytes=16 << 20),
         name="combine",
     )(*parts)
 
 
-def slot_lists(reach_plane, global_ids, rand_ids, plane, place):
+def pack(held, local):
+    slots = held.shape[1]
+    source, target = jnp.arange(slots), jnp.arange(SLOT_ROOM)
+    before = source[:, None] < source[None, :]
+    rank = jnp.sum(jnp.where(held[:, :, None] & before[None], 1, 0), axis=1)
+    at = held[:, :, None] & (rank[:, :, None] == target[None, None, :])
+    index = jnp.sum(jnp.where(at, local[:, :, None], 0), axis=1)
+    counts = jnp.sum(held.astype(jnp.int32), axis=1)
+    return index.reshape(-1).astype(jnp.int32), counts.astype(jnp.int32)
+
+
+def own_lists(reach):
+    offsets = jnp.arange(-WMAX, WMAX + 1, dtype=jnp.int32)
+    target = jnp.arange(RUN_BLOCKS, dtype=jnp.int32)[:, None] + offsets[None, :]
+    live = (
+        (jnp.abs(offsets)[None, :] <= reach[:, None]) & (target >= 0) & (target < RUN_BLOCKS)
+    )
+    return pack(live, target)
+
+
+def plane_lists(before, after, global_ids, rand_ids, plane, place):
     plane_blocks = 4 * RUN_BLOCKS
     block_total = rand_ids.shape[0]
     first = plane * plane_blocks
-    blocks = first + jnp.arange(plane_blocks, dtype=jnp.int32)
-    offsets = jnp.arange(-WMAX, WMAX + 1, dtype=jnp.int32)
-    target = blocks[:, None] + offsets[None, :]
+    blocks = jnp.arange(plane_blocks, dtype=jnp.int32)
+    run = blocks // RUN_BLOCKS
+    offsets = jnp.asarray([-2, -1, 1, 2], jnp.int32)
+    target = first + blocks[:, None] + offsets[None, :]
+    reach = jnp.where(
+        (run == (place + 3) % 4)[:, None],
+        jnp.tile(before, 4)[:, None],
+        jnp.tile(after, 4)[:, None],
+    )
     window_live = (
-        (jnp.abs(offsets)[None, :] <= reach_plane[:, None])
+        (jnp.abs(offsets)[None, :] <= reach)
         & (target >= 0)
         & (target < block_total)
+        & (target // RUN_BLOCKS != (first + blocks)[:, None] // RUN_BLOCKS)
     )
     listed = lax.dynamic_slice_in_dim(rand_ids, first, plane_blocks, 0)
     globals_all = jnp.broadcast_to(global_ids[None, :], (plane_blocks, global_ids.shape[0]))
@@ -224,14 +255,7 @@
         [window_live, jnp.ones(globals_all.shape, jnp.bool_), listed >= 0], axis=1
     )
     held = live & ((slots >> 4) % 4 == place)
-    local = (slots >> 6) * RUN_BLOCKS + (slots & (RUN_BLOCKS - 1))
-    order = jnp.arange(SLOTS)
-    before = order[:, None] < order[None, :]
-    rank = jnp.sum(jnp.where(held[:, :, None] & before[None], 1, 0), axis=1)
-    at = held[:, :, None] & (rank[:, :, None] == order[None, None, :])
-    index = jnp.sum(jnp.where(at, local[:, :, None], 0), axis=1)
-    counts = jnp.sum(held.astype(jnp.int32), axis=1)
-    return index.reshape(-1).astype(jnp.int32), counts.astype(jnp.int32)
+    return pack(held, (slots >> 6) * RUN_BLOCKS + (slots & (RUN_BLOCKS - 1)))
 
 
 def per_device(tokens, query_weight, kv_weight, reach, global_ids, rand_ids):
@@ -245,28 +269,40 @@
     both = lax.all_gather(both, "a", axis=0, tiled=True)
     kv_own = lax.all_gather(both[:, :width], "b", axis=0, tiled=True)
     query_own_in, kv_own = lax.optimization_barrier((both[:, width:], kv_own))
-    query_own = lax.all_gather(query_own_in, "b", axis=0, tiled=True)
 
     def spread(own):
         own = own.reshape(4, 4, 64, width)
         return [own] + [shift(own, "x", s) for s in (1, 2, 3)]
 
+    kv_parts = spread(kv_own)
+    query_own = lax.all_gather(query_own_in, "b", axis=0, tiled=True)
+    kv_parts, query_own = lax.optimization_barrier((kv_parts, query_own))
+
     place_1 = place.reshape(1)
-    kv_rows = project(place_1, rows, spread(kv_own))
+    kv_rows = project(place_1, rows, kv_parts)
     held = lax.all_gather(kv_rows, ("a", "b"), axis=0, tiled=True)
     held = held.reshape(-1, BS, 2 * HD)
+    query_own, reach, kv_rows = lax.optimization_barrier((query_own, reach, kv_rows))
     query_rows = project(place_1, rows, spread(query_own))
     queries = [query_rows] + [shift(query_rows, "x", s) for s in (1, 2, 3)]
 
-    reach_plane = lax.all_gather(reach, "x", axis=0, tiled=True)
-    index, counts = slot_lists(reach_plane, global_ids, rand_ids, plane, place)
+    own_index, own_counts = own_lists(reach)
+    zero = jnp.zeros((1,), jnp.int32)
+    own_held = kv_rows.reshape(-1, BS, 2 * HD)
+    windows = partial_attention(zero, own_index, own_counts, query_rows, own_held)
+
+    before, after = shift(reach, "x", 1), shift(reach, "x", 3)
+    index, counts = plane_lists(before, after, global_ids, rand_ids, plane, place)
+    held, windows, index, counts, queries = lax.optimization_barrier(
+        (held, windows, index, counts, queries)
+    )
 
     parts = [None] * 4
     for s in (2, 1, 3, 0):
         from_x = ((place + 4 - s) % 4).reshape(1)
         part = partial_attention(from_x, index, counts, queries[s], held)
         parts[s] = part if s == 0 else shift(part, "x", 4 - s)
-    return combine(parts)
+    return combine(parts + [windows])
 
 
 def solution(mesh):

time: 252 us -> 244 us (0.968)
  blocking collectives: 67.3 us -> 50.7 us
  local copies, waits for them, and re-layouts: 15.4 us -> 1.53 us
  waiting for transfers between devices: 62.7 us -> 72.8 us
  Pallas kernels: 41.2 us -> 51.1 us
    ppermute x12 -> x14, waiting for transfers between devices: 20 us -> 42.2 us  [shift(): lax.ppermute(value, axis, [(i, (i + by) % size) for i in range(size)])]
    unnamed x1 -> x0, blocking collectives: 15.9 us -> none
    unnamed x25 -> x12, local copies, waits for them, and re-layouts: 15 us -> 0.84 us
    all_gather x1, waiting for transfers between devices: 41.9 us -> 29.9 us  [per_device(): held = lax.all_gather(kv_rows, ('a', 'b'), axis=0, tiled=True)]
    pallas_call x4 -> x5, Pallas kernels: 29.7 us -> 35.6 us  [partial_attention(): pl.pallas_call(partial_kernel, in_specs=[smem, smem, smem, vmem, pl.Block...]
    pallas_call x2, Pallas kernels: 6.9 us -> 12 us  [project(): pl.pallas_call(project_kernel, grid_spec=pltpu.PrefetchScalarGridSpec(num...]
    ppermute x12 -> x14, starting transfers between devices: 48 us -> 49.7 us  [shift(): lax.ppermute(value, axis, [(i, (i + by) % size) for i in range(size)])]
  transfers between devices with their start and end apart: 14 -> 16, of which waited for: 6 -> 8; matrix products, arithmetic and copies ran while one was open for 2% -> 1% of each run, Pallas kernels for 13% -> 14%
where the time goes in v2:
time: 244 us; the launch traced here: 242 us
  waiting for transfers between devices  72.8 us (30%)
  Pallas kernels  51.1 us (21%)
  blocking collectives  50.7 us (21%)
  starting transfers between devices  49.7 us (20%)
  between operations  13.7 us (6%)
    ppermute x14, starting transfers between devices, shift(): lax.ppermute(value, axis, [(i, (i + by) % size) for i in range(size)])  49.7 us
    ppermute x14, waiting for transfers between devices, shift(): lax.ppermute(value, axis, [(i, (i + by) % size) for i in range(size)])  42.2 us
    pallas_call x5, Pallas kernels, partial_attention(): pl.pallas_call(partial_kernel, in_specs=[smem, smem, smem, vmem, pl.Block...  35.6 us
    all_gather x1, waiting for transfers between devices, per_device(): held = lax.all_gather(kv_rows, ('a', 'b'), axis=0, tiled=True)  29.9 us
    all_gather x1, blocking collectives, per_device(): both = lax.all_gather(both, 'a', axis=0, tiled=True)  25.2 us
    all_gather x1, blocking collectives, per_device(): kv_own = lax.all_gather(both[:, :width], 'b', axis=0, tiled=True)  12.8 us
    all_gather x1, blocking collectives, per_device(): query_own = lax.all_gather(query_own_in, 'b', axis=0, tiled=True)  12.6 us
    pallas_call x2, Pallas kernels, project(): pl.pallas_call(project_kernel, grid_spec=pltpu.PrefetchScalarGridSpec(num...  12 us
  transfers between devices with their start and end apart: 16, of which 8 were waited for; matrix products, arithmetic and copies ran while one was open for 1% of the time, Pallas kernels for 14%

profile of v2, /device:TPU:1, one launch (start us, length us, event | category | flops | bytes accessed | tf_op | source)
XLA Modules:
  0.0 241.6 jit_solution(1955735031006659206)
XLA Ops:
  8.1 25.2 %all_gather.16 = bf16[256,512]{1,0:T(8,128)(2,1)S(1)} all-gather(bf16[64,512]{1,0:T(8,128)(2,1)S(1)} %pad_maximum_fusion), channel_id=1, replica_groups=mesh['a'=4,'b'=4,'x'=4,'y'=4,'c'=2] {'a'}, dimensions={0}, use_global_device_ids=true | all-gather | bytes 327680 | tf_op jit(solution)/shard_map/all_gather | solution.py:269
  33.4 12.8 %all_gather.17 = bf16[1024,256]{1,0:T(8,128)(2,1)S(1)} all-gather(bf16[256,256]{1,0:T(8,128)(2,1)S(1)} %get-tuple-element.47), channel_id=1, replica_groups=mesh['a'=4,'b'=4,'x'=4,'y'=4,'c'=2] {'b'}, dimensions={0}, use_global_device_ids=true | all-gather | bytes 655360 | tf_op jit(solution)/shard_map/all_gather | solution.py:270
  46.1 3.1 %collective-permute-start = (bf16[4,4,64,256]{3,2,1,0:T(8,128)(2,1)S(1)}, bf16[4,4,64,256]{3,2,1,0:T(8,128)(2,1)S(1)}, u32[]{:S(2)}, u32[]{:S(2)}) collective-permute-start(bf16[4,4,64,256]{3,2,1,0:T(8,128)(2,1)S(1)} %bitcast.13), channel_id=1, source_target_pairs={{0,8},{8,16},{16,24},{24,0},{1,9},{9,17},{17,25},{25,1},{2,10},{10... | collective-permute-start | bytes 1572872 | tf_op jit(solution)/shard_map/ppermute | solution.py:28
  49.3 4.4 %collective-permute-start.1 = (bf16[4,4,64,256]{3,2,1,0:T(8,128)(2,1)S(1)}, bf16[4,4,64,256]{3,2,1,0:T(8,128)(2,1)S(1)}, u32[]{:S(2)}, u32[]{:S(2)}) collective-permute-start(bf16[4,4,64,256]{3,2,1,0:T(8,128)(2,1)S(1)} %bitcast.14), channel_id=1, source_target_pairs={{0,16},{8,24},{16,0},{24,8},{1,17},{9,25},{17,1},{25,9},{2,18},{10... | collective-permute-start | bytes 1572872 | tf_op jit(solution)/shard_map/ppermute | solution.py:28
  53.6 3.1 %collective-permute-start.2 = (bf16[4,4,64,256]{3,2,1,0:T(8,128)(2,1)S(1)}, bf16[4,4,64,256]{3,2,1,0:T(8,128)(2,1)S(1)}, u32[]{:S(2)}, u32[]{:S(2)}) collective-permute-start(bf16[4,4,64,256]{3,2,1,0:T(8,128)(2,1)S(1)} %bitcast.15), channel_id=1, source_target_pairs={{0,24},{8,0},{16,8},{24,16},{1,25},{9,1},{17,9},{25,17},{2,26},{10... | collective-permute-start | bytes 1572872 | tf_op jit(solution)/shard_map/ppermute | solution.py:28
  56.7 12.6 %all_gather.18 = bf16[1024,256]{1,0:T(8,128)(2,1)S(1)} all-gather(bf16[256,256]{1,0:T(8,128)(2,1)S(1)} %get-tuple-element.24), channel_id=1, replica_groups=mesh['a'=4,'b'=4,'x'=4,'y'=4,'c'=2] {'b'}, dimensions={0}, use_global_device_ids=true | all-gather | bytes 655360 | tf_op jit(solution)/shard_map/all_gather | solution.py:278
  69.3 3.5 %collective-permute-done.2.part3 = bf16[4,4,64,256]{3,2,1,0:T(8,128)(2,1)S(1)} collective-permute-done((bf16[4,4,64,256]{3,2,1,0:T(8,128)(2,1)S(1)}, bf16[4,4,64,256]{3,2,1,0:T(8,128)(2,1)S(1)}, u32[]{:S(2)}, u32[]{:S(2)}) %collective-permute-start.2) | collective-permute-done | bytes 524320 | tf_op jit(solution)/shard_map/ppermute | solution.py:28
  72.8 6.4 %project.2 = bf16[1024,256]{1,0:T(8,128)(2,1)} custom-call(s32[1]{0:T(128)} %bitcast.1.place, bf16[1024,4096]{1,0:T(8,128)(2,1)} %all-gather.3.cloned.1.call-done.rows, bf16[4,4,64,256]{3,2,1,0:T(8,128)(2,1)S(1)} %bitcast.16, bf16[4,4,64,256]{3,2,1,0:T(8,128)(2,1)S(1)} %collective-permute-done.part1, ...), custom_call_target="tpu_custom_call" | custom-call | flops 2147483648 | bytes 11010048 | tf_op jit(solution)/shard_map/project/pallas_call | solution.py:50
  80.3 6.3 %collective-permute-start.6 = (s32[16]{0:T(128)S(1)}, s32[16]{0:T(128)S(1)}, u32[]{:S(2)}, u32[]{:S(2)}) collective-permute-start(s32[16]{0:T(128)S(1)} %copy-done.3), channel_id=1, source_target_pairs={{0,8},{8,16},{16,24},{24,0},{1,9},{9,17},{17,25},{25,1},{2,10},{10... | collective-permute-start | bytes 200 | tf_op jit(solution)/shard_map/ppermute | solution.py:28
  86.6 1.9 collective-permute-start.7
  88.5 3.4 %collective-permute-start.3 = (bf16[4,4,64,256]{3,2,1,0:T(8,128)(2,1)S(1)}, bf16[4,4,64,256]{3,2,1,0:T(8,128)(2,1)S(1)}, u32[]{:S(2)}, u32[]{:S(2)}) collective-permute-start(bf16[4,4,64,256]{3,2,1,0:T(8,128)(2,1)S(1)} %bitcast.9), channel_id=1, source_target_pairs={{0,8},{8,16},{16,24},{24,0},{1,9},{9,17},{17,25},{25,1},{2,10},{10... | collective-permute-start | bytes 1572872 | tf_op jit(solution)/shard_map/ppermute | solution.py:28
  91.9 2.3 collective-permute-start.4
  94.2 4.0 %collective-permute-start.5 = (bf16[4,4,64,256]{3,2,1,0:T(8,128)(2,1)S(1)}, bf16[4,4,64,256]{3,2,1,0:T(8,128)(2,1)S(1)}, u32[]{:S(2)}, u32[]{:S(2)}) collective-permute-start(bf16[4,4,64,256]{3,2,1,0:T(8,128)(2,1)S(1)} %bitcast.11), channel_id=1, source_target_pairs={{0,24},{8,0},{16,8},{24,16},{1,25},{9,1},{17,9},{25,17},{2,26},{10... | collective-permute-start | bytes 1572872 | tf_op jit(solution)/shard_map/ppermute | solution.py:28
  101.0 10.6 %collective-permute-done.4.part2 = bf16[4,4,64,256]{3,2,1,0:T(8,128)(2,1)S(1)} collective-permute-done((bf16[4,4,64,256]{3,2,1,0:T(8,128)(2,1)S(1)}, bf16[4,4,64,256]{3,2,1,0:T(8,128)(2,1)S(1)}, u32[]{:S(2)}, u32[]{:S(2)}) %collective-permute-start.4) | collective-permute-done | bytes 524320 | tf_op jit(solution)/shard_map/ppermute | solution.py:28
  111.6 6.1 %collective-permute-done.5.part3 = bf16[4,4,64,256]{3,2,1,0:T(8,128)(2,1)S(1)} collective-permute-done((bf16[4,4,64,256]{3,2,1,0:T(8,128)(2,1)S(1)}, bf16[4,4,64,256]{3,2,1,0:T(8,128)(2,1)S(1)}, u32[]{:S(2)}, u32[]{:S(2)}) %collective-permute-start.5) | collective-permute-done | bytes 524320 | tf_op jit(solution)/shard_map/ppermute | solution.py:28
  117.7 5.7 %project.3.query = bf16[1024,256]{1,0:T(8,128)(2,1)S(1)} custom-call(s32[1]{0:T(128)} %bitcast.1.place, bf16[1024,4096]{1,0:T(8,128)(2,1)} %all-gather.3.cloned.1.call-done.rows, bf16[4,4,64,256]{3,2,1,0:T(8,128)(2,1)S(1)} %bitcast.12, bf16[4,4,64,256]{3,2,1,0:T(8,128)(2,1)S(1)} %collective-permute-done.3.part1, ...), custom_call_target="tpu_custom_call" | custom-call | flops 2147483648 | bytes 11010048 | tf_op jit(solution)/shard_map/project/pallas_call | solution.py:50
  123.4 5.4 %collective-permute-start.10 = (bf16[1024,256]{1,0:T(8,128)(2,1)S(1)}, bf16[1024,256]{1,0:T(8,128)(2,1)S(1)}, u32[]{:S(2)}, u32[]{:S(2)}) collective-permute-start(bf16[1024,256]{1,0:T(8,128)(2,1)S(1)} %project.3.query), channel_id=1, source_target_pairs={{0,24},{8,0},{16,8},{24,16},{1,25},{9,1},{17,9},{25,17},{2,26},{10... | collective-permute-start | bytes 1572872 | tf_op jit(solution)/shard_map/ppermute | solution.py:28
  128.9 1.9 collective-permute-start.8
  130.8 3.1 %collective-permute-start.9 = (bf16[1024,256]{1,0:T(8,128)(2,1)S(1)}, bf16[1024,256]{1,0:T(8,128)(2,1)S(1)}, u32[]{:S(2)}, u32[]{:S(2)}) collective-permute-start(bf16[1024,256]{1,0:T(8,128)(2,1)S(1)} %project.3.query), channel_id=1, source_target_pairs={{0,16},{8,24},{16,0},{24,8},{1,17},{9,25},{17,1},{25,9},{2,18},{10... | collective-permute-start | bytes 1572872 | tf_op jit(solution)/shard_map/ppermute | solution.py:28
  133.9 6.4 %partial_attention.5.refs_4_ = bf16[1088,256]{1,0:T(8,128)(2,1)S(1)} custom-call(s32[1]{0:T(128)} %constant.107.clone.1.from_x, s32[128]{0:T(128)S(1)} %reshape.358.index, s32[16]{0:T(128)S(1)} %get-tuple-element.45.counts, bf16[1024,256]{1,0:T(8,128)(2,1)S(1)} %project.3.query, bf16[16,64,256]{2,1,0:T(8,128)(2,1)} %bitcast.5.held), custom_call_target="tpu_custom_call" | custom-call | flops 10000000000 | bytes 4194304 | tf_op jit(solution)/shard_map/partial_attention/pallas_call | solution.py:152
  140.3 5.2 %collective-permute-done.8.query = bf16[1024,256]{1,0:T(8,128)(2,1)S(1)} collective-permute-done((bf16[1024,256]{1,0:T(8,128)(2,1)S(1)}, bf16[1024,256]{1,0:T(8,128)(2,1)S(1)}, u32[]{:S(2)}, u32[]{:S(2)}) %collective-permute-start.8) | collective-permute-done | bytes 524320 | tf_op jit(solution)/shard_map/ppermute | solution.py:28
  145.5 8.8 %collective-permute-done.9.query = bf16[1024,256]{1,0:T(8,128)(2,1)S(1)} collective-permute-done((bf16[1024,256]{1,0:T(8,128)(2,1)S(1)}, bf16[1024,256]{1,0:T(8,128)(2,1)S(1)}, u32[]{:S(2)}, u32[]{:S(2)}) %collective-permute-start.9) | collective-permute-done | bytes 524320 | tf_op jit(solution)/shard_map/ppermute | solution.py:28
  155.2 29.9 %all-gather.5.cloned.1.call-done = bf16[16384,256]{1,0:T(8,128)(2,1)} async-done(((bf16[1024,256]{1,0:T(8,128)(2,1)}), bf16[16384,256]{1,0:T(8,128)(2,1)}) %all-gather.5.cloned.1.call-update) | async-done | bytes 8388624 | tf_op jit(solution)/shard_map/all_gather | solution.py:283
  185.1 7.2 %partial_attention.9 = bf16[1088,256]{1,0:T(8,128)(2,1)S(1)} custom-call(s32[1]{0:T(128)} %bitcast.8.from_x, s32[512]{0:T(512)S(1)} %reshape.361.index, s32[64]{0:T(128)S(1)} %get-tuple-element.34.counts, bf16[1024,256]{1,0:T(8,128)(2,1)S(1)} %collective-permute-done.10.query, bf16[256,64,256]{2,1,0:T(8,128)(2,1)} %bitcast.17), custom_call_target="tpu_custom_call" | custom-call | flops 10000000000 | bytes 4194304 | tf_op jit(solution)/shard_map/partial_attention/pallas_call | solution.py:152
  192.3 3.4 %collective-permute-start.13 = (bf16[1088,256]{1,0:T(8,128)(2,1)S(1)}, bf16[1088,256]{1,0:T(8,128)(2,1)S(1)}, u32[]{:S(2)}, u32[]{:S(2)}) collective-permute-start(bf16[1088,256]{1,0:T(8,128)(2,1)S(1)} %partial_attention.9), channel_id=1, source_target_pairs={{0,8},{8,16},{16,24},{24,0},{1,9},{9,17},{17,25},{25,1},{2,10},{10... | collective-permute-start | bytes 1671176 | tf_op jit(solution)/shard_map/ppermute | solution.py:28
  195.7 7.5 %partial_attention.8 = bf16[1088,256]{1,0:T(8,128)(2,1)S(1)} custom-call(s32[1]{0:T(128)} %bitcast.7.from_x, s32[512]{0:T(512)S(1)} %reshape.361.index, s32[64]{0:T(128)S(1)} %get-tuple-element.34.counts, bf16[1024,256]{1,0:T(8,128)(2,1)S(1)} %copy-done.1, bf16[256,64,256]{2,1,0:T(8,128)(2,1)} %bitcast.18), custom_call_target="tpu_custom_call" | custom-call | flops 10000000000 | bytes 4194304 | tf_op jit(solution)/shard_map/partial_attention/pallas_call | solution.py:152
  203.2 5.0 %collective-permute-start.12 = (bf16[1088,256]{1,0:T(8,128)(2,1)S(1)}, bf16[1088,256]{1,0:T(8,128)(2,1)S(1)}, u32[]{:S(2)}, u32[]{:S(2)}) collective-permute-start(bf16[1088,256]{1,0:T(8,128)(2,1)S(1)} %partial_attention.8), channel_id=1, source_target_pairs={{0,16},{8,24},{16,0},{24,8},{1,17},{9,25},{17,1},{25,9},{2,18},{10... | collective-permute-start | bytes 1671176 | tf_op jit(solution)/shard_map/ppermute | solution.py:28
  208.2 6.9 %partial_attention.7 = bf16[1088,256]{1,0:T(8,128)(2,1)S(1)} custom-call(s32[1]{0:T(128)} %bitcast.6.from_x, s32[512]{0:T(512)S(1)} %reshape.361.index, s32[64]{0:T(128)S(1)} %get-tuple-element.34.counts, bf16[1024,256]{1,0:T(8,128)(2,1)S(1)} %collective-permute-done.8.query, bf16[256,64,256]{2,1,0:T(8,128)(2,1)} %bitcast.19), custom_call_target="tpu_custom_call" | custom-call | flops 10000000000 | bytes 4194304 | tf_op jit(solution)/shard_map/partial_attention/pallas_call | solution.py:152
  215.1 2.5 %collective-permute-start.11 = (bf16[1088,256]{1,0:T(8,128)(2,1)S(1)}, bf16[1088,256]{1,0:T(8,128)(2,1)S(1)}, u32[]{:S(2)}, u32[]{:S(2)}) collective-permute-start(bf16[1088,256]{1,0:T(8,128)(2,1)S(1)} %partial_attention.7), channel_id=1, source_target_pairs={{0,24},{8,0},{16,8},{24,16},{1,25},{9,1},{17,9},{25,17},{2,26},{10... | collective-permute-start | bytes 1671176 | tf_op jit(solution)/shard_map/ppermute | solution.py:28
  217.7 7.6 %partial_attention.6.refs_0_ = bf16[1088,256]{1,0:T(8,128)(2,1)S(1)} custom-call(s32[1]{0:T(128)} %bitcast.from_x, s32[512]{0:T(512)S(1)} %reshape.361.index, s32[64]{0:T(128)S(1)} %get-tuple-element.34.counts, bf16[1024,256]{1,0:T(8,128)(2,1)S(1)} %project.3.query, bf16[256,64,256]{2,1,0:T(8,128)(2,1)} %bitcast.20), custom_call_target="tpu_custom_call" | custom-call | flops 10000000000 | bytes 4194304 | tf_op jit(solution)/shard_map/partial_attention/pallas_call | solution.py:152
  225.2 6.1 %collective-permute-done.11.refs_1_ = bf16[1088,256]{1,0:T(8,128)(2,1)S(1)} collective-permute-done((bf16[1088,256]{1,0:T(8,128)(2,1)S(1)}, bf16[1088,256]{1,0:T(8,128)(2,1)S(1)}, u32[]{:S(2)}, u32[]{:S(2)}) %collective-permute-start.11) | collective-permute-done | bytes 557088 | tf_op jit(solution)/shard_map/ppermute | solution.py:28
  231.4 3.4 %combine.1 = bf16[1024,256]{1,0:T(8,128)(2,1)} custom-call(bf16[1088,256]{1,0:T(8,128)(2,1)S(1)} %partial_attention.6.refs_0_, bf16[1088,256]{1,0:T(8,128)(2,1)S(1)} %collective-permute-done.11.refs_1_, bf16[1088,256]{1,0:T(8,128)(2,1)S(1)} %collective-permute-done.12.refs_2_, bf16[1088,256]{1,0:T(8,128)(2,1)S(1)} %collective-permute-done.13.refs_3_, ...), custom_call_target="tpu_custom_call" | custom-call | tf_op jit(solution)/shard_map/combine/pallas_call | solution.py:202
  (52 shorter events, 6.2 us)
Async XLA Ops:
  6.5 73.7 %copy-start.2 = (s32[4]{0:T(128)S(1)}, s32[4]{0:T(128)}, u32[]{:S(2)}) copy-start(s32[4]{0:T(128)} %constant.120.clone) | copy-start | bytes 52
  6.5 92.2 %copy-start.4 = (s32[4]{0:T(128)S(1)}, s32[4]{0:T(128)}, u32[]{:S(2)}) copy-start(s32[4]{0:T(128)} %constant.123) | copy-start | bytes 52
  6.5 72.7 %copy-start.5 = (s32[2]{0:T(128)S(1)}, s32[2]{0:T(128)}, u32[]{:S(2)}) copy-start(s32[2]{0:T(128)} %param.11) | copy-start | bytes 28
  6.5 73.7 %copy-start.3 = (s32[16]{0:T(128)S(1)}, s32[16]{0:T(128)}, u32[]{:S(2)}) copy-start(s32[16]{0:T(128)} %param.10) | copy-start | bytes 196
  6.5 66.3 %all-gather.3.cloned.1.call-start = ((), (), s32[]{:S(2)}) async-start(), calls=%async_computation | async-start | bytes 9437184 | tf_op jit(solution)/shard_map/all_gather | solution.py:266
  7.3 177.8 %all-gather.5.cloned.1.call-start = ((), (), s32[]{:S(2)}) async-start(), calls=%async_computation.1 | async-start | bytes 8912896 | tf_op jit(solution)/shard_map/all_gather | solution.py:283
  46.1 23.2 %collective-permute-start = (bf16[4,4,64,256]{3,2,1,0:T(8,128)(2,1)S(1)}, bf16[4,4,64,256]{3,2,1,0:T(8,128)(2,1)S(1)}, u32[]{:S(2)}, u32[]{:S(2)}) collective-permute-start(bf16[4,4,64,256]{3,2,1,0:T(8,128)(2,1)S(1)} %bitcast.13), channel_id=1, source_target_pairs={{0,8},{8,16},{16,24},{24,0},{1,9},{9,17},{17,25},{25,1},{2,10},{10... | collective-permute-start | bytes 1572872 | tf_op jit(solution)/shard_map/ppermute | solution.py:28
  49.3 20.1 %collective-permute-start.1 = (bf16[4,4,64,256]{3,2,1,0:T(8,128)(2,1)S(1)}, bf16[4,4,64,256]{3,2,1,0:T(8,128)(2,1)S(1)}, u32[]{:S(2)}, u32[]{:S(2)}) collective-permute-start(bf16[4,4,64,256]{3,2,1,0:T(8,128)(2,1)S(1)} %bitcast.14), channel_id=1, source_target_pairs={{0,16},{8,24},{16,0},{24,8},{1,17},{9,25},{17,1},{25,9},{2,18},{10... | collective-permute-start | bytes 1572872 | tf_op jit(solution)/shard_map/ppermute | solution.py:28
  53.6 19.2 %collective-permute-start.2 = (bf16[4,4,64,256]{3,2,1,0:T(8,128)(2,1)S(1)}, bf16[4,4,64,256]{3,2,1,0:T(8,128)(2,1)S(1)}, u32[]{:S(2)}, u32[]{:S(2)}) collective-permute-start(bf16[4,4,64,256]{3,2,1,0:T(8,128)(2,1)S(1)} %bitcast.15), channel_id=1, source_target_pairs={{0,24},{8,0},{16,8},{24,16},{1,25},{9,1},{17,9},{25,17},{2,26},{10... | collective-permute-start | bytes 1572872 | tf_op jit(solution)/shard_map/ppermute | solution.py:28
  80.3 18.2 %collective-permute-start.6 = (s32[16]{0:T(128)S(1)}, s32[16]{0:T(128)S(1)}, u32[]{:S(2)}, u32[]{:S(2)}) collective-permute-start(s32[16]{0:T(128)S(1)} %copy-done.3), channel_id=1, source_target_pairs={{0,8},{8,16},{16,24},{24,0},{1,9},{9,17},{17,25},{25,1},{2,10},{10... | collective-permute-start | bytes 200 | tf_op jit(solution)/shard_map/ppermute | solution.py:28
  86.6 12.0 %collective-permute-start.7 = (s32[16]{0:T(128)S(1)}, s32[16]{0:T(128)S(1)}, u32[]{:S(2)}, u32[]{:S(2)}) collective-permute-start(s32[16]{0:T(128)S(1)} %copy-done.3), channel_id=1, source_target_pairs={{0,24},{8,0},{16,8},{24,16},{1,25},{9,1},{17,9},{25,17},{2,26},{10... | collective-permute-start | bytes 200 | tf_op jit(solution)/shard_map/ppermute | solution.py:28
  88.5 12.4 %collective-permute-start.3 = (bf16[4,4,64,256]{3,2,1,0:T(8,128)(2,1)S(1)}, bf16[4,4,64,256]{3,2,1,0:T(8,128)(2,1)S(1)}, u32[]{:S(2)}, u32[]{:S(2)}) collective-permute-start(bf16[4,4,64,256]{3,2,1,0:T(8,128)(2,1)S(1)} %bitcast.9), channel_id=1, source_target_pairs={{0,8},{8,16},{16,24},{24,0},{1,9},{9,17},{17,25},{25,1},{2,10},{10... | collective-permute-start | bytes 1572872 | tf_op jit(solution)/shard_map/ppermute | solution.py:28
  91.9 19.7 %collective-permute-start.4 = (bf16[4,4,64,256]{3,2,1,0:T(8,128)(2,1)S(1)}, bf16[4,4,64,256]{3,2,1,0:T(8,128)(2,1)S(1)}, u32[]{:S(2)}, u32[]{:S(2)}) collective-permute-start(bf16[4,4,64,256]{3,2,1,0:T(8,128)(2,1)S(1)} %bitcast.10), channel_id=1, source_target_pairs={{0,16},{8,24},{16,0},{24,8},{1,17},{9,25},{17,1},{25,9},{2,18},{10... | collective-permute-start | bytes 1572872 | tf_op jit(solution)/shard_map/ppermute | solution.py:28
  94.2 23.6 %collective-permute-start.5 = (bf16[4,4,64,256]{3,2,1,0:T(8,128)(2,1)S(1)}, bf16[4,4,64,256]{3,2,1,0:T(8,128)(2,1)S(1)}, u32[]{:S(2)}, u32[]{:S(2)}) collective-permute-start(bf16[4,4,64,256]{3,2,1,0:T(8,128)(2,1)S(1)} %bitcast.11), channel_id=1, source_target_pairs={{0,24},{8,0},{16,8},{24,16},{1,25},{9,1},{17,9},{25,17},{2,26},{10... | collective-permute-start | bytes 1572872 | tf_op jit(solution)/shard_map/ppermute | solution.py:28
  123.4 16.9 %collective-permute-start.10 = (bf16[1024,256]{1,0:T(8,128)(2,1)S(1)}, bf16[1024,256]{1,0:T(8,128)(2,1)S(1)}, u32[]{:S(2)}, u32[]{:S(2)}) collective-permute-start(bf16[1024,256]{1,0:T(8,128)(2,1)S(1)} %project.3.query), channel_id=1, source_target_pairs={{0,24},{8,0},{16,8},{24,16},{1,25},{9,1},{17,9},{25,17},{2,26},{10... | collective-permute-start | bytes 1572872 | tf_op jit(solution)/shard_map/ppermute | solution.py:28
  128.9 16.7 %collective-permute-start.8 = (bf16[1024,256]{1,0:T(8,128)(2,1)S(1)}, bf16[1024,256]{1,0:T(8,128)(2,1)S(1)}, u32[]{:S(2)}, u32[]{:S(2)}) collective-permute-start(bf16[1024,256]{1,0:T(8,128)(2,1)S(1)} %project.3.query), channel_id=1, source_target_pairs={{0,8},{8,16},{16,24},{24,0},{1,9},{9,17},{17,25},{25,1},{2,10},{10... | collective-permute-start | bytes 1572872 | tf_op jit(solution)/shard_map/ppermute | solution.py:28
  130.8 23.6 %collective-permute-start.9 = (bf16[1024,256]{1,0:T(8,128)(2,1)S(1)}, bf16[1024,256]{1,0:T(8,128)(2,1)S(1)}, u32[]{:S(2)}, u32[]{:S(2)}) collective-permute-start(bf16[1024,256]{1,0:T(8,128)(2,1)S(1)} %project.3.query), channel_id=1, source_target_pairs={{0,16},{8,24},{16,0},{24,8},{1,17},{9,25},{17,1},{25,9},{2,18},{10... | collective-permute-start | bytes 1572872 | tf_op jit(solution)/shard_map/ppermute | solution.py:28
  154.3 0.8 copy-start
  185.1 10.6 %copy-start.1 = (bf16[1024,256]{1,0:T(8,128)(2,1)S(1)}, bf16[1024,256]{1,0:T(8,128)(2,1)}, u32[]{:S(2)}) copy-start(bf16[1024,256]{1,0:T(8,128)(2,1)} %copy-done) | copy-start | bytes 1572868
  192.3 32.9 %collective-permute-start.13 = (bf16[1088,256]{1,0:T(8,128)(2,1)S(1)}, bf16[1088,256]{1,0:T(8,128)(2,1)S(1)}, u32[]{:S(2)}, u32[]{:S(2)}) collective-permute-start(bf16[1088,256]{1,0:T(8,128)(2,1)S(1)} %partial_attention.9), channel_id=1, source_target_pairs={{0,8},{8,16},{16,24},{24,0},{1,9},{9,17},{17,25},{25,1},{2,10},{10... | collective-permute-start | bytes 1671176 | tf_op jit(solution)/shard_map/ppermute | solution.py:28
  203.2 22.0 %collective-permute-start.12 = (bf16[1088,256]{1,0:T(8,128)(2,1)S(1)}, bf16[1088,256]{1,0:T(8,128)(2,1)S(1)}, u32[]{:S(2)}, u32[]{:S(2)}) collective-permute-start(bf16[1088,256]{1,0:T(8,128)(2,1)S(1)} %partial_attention.8), channel_id=1, source_target_pairs={{0,16},{8,24},{16,0},{24,8},{1,17},{9,25},{17,1},{25,9},{2,18},{10... | collective-permute-start | bytes 1671176 | tf_op jit(solution)/shard_map/ppermute | solution.py:28
  215.1 16.3 %collective-permute-start.11 = (bf16[1088,256]{1,0:T(8,128)(2,1)S(1)}, bf16[1088,256]{1,0:T(8,128)(2,1)S(1)}, u32[]{:S(2)}, u32[]{:S(2)}) collective-permute-start(bf16[1088,256]{1,0:T(8,128)(2,1)S(1)} %partial_attention.7), channel_id=1, source_target_pairs={{0,24},{8,0},{16,8},{24,16},{1,25},{9,1},{17,9},{25,17},{2,26},{10... | collective-permute-start | bytes 1671176 | tf_op jit(solution)/shard_map/ppermute | solution.py:28
Sparse Core Ops, SparseCore 0:
  9.5 63.1 all-gather.2
  79.3 105.7 all-gather.4

commit v3 on v2

--- a/solution.py
+++ b/solution.py
@@ -11,10 +11,10 @@
 BS = 64
 WMAX = 2
 CHUNK = 2
-UNROLL = 4
+UNROLL = 8
 SLOT_ROOM = 8
 RUN_BLOCKS = 16
-PAD = 16
+PAD = 32
 LOG2E = 1.4426950408889634
 MASKED = -1e30
 F32 = jnp.float32
@@ -45,8 +45,8 @@
 def project(place, rows, parts):
     count, depth = rows.shape
     width = parts[0].shape[-1]
-    tile = 256
-    whole = pl.BlockSpec(parts[0].shape, lambda i, p: (0, 0, 0, 0))
+    tile = 512
+    whole = pl.BlockSpec(memory_space=pltpu.VMEM)
     return pl.pallas_call(
         project_kernel,
         grid_spec=pltpu.PrefetchScalarGridSpec(
@@ -67,24 +67,34 @@
     )(place, rows, *parts)
 
 
-def partial_kernel(from_x, index, counts, query, held, out, slabs, sems):
-    base = from_x[0] * RUN_BLOCKS
-
-    def copy(j, p):
-        block = index[(base + j) * SLOT_ROOM + p]
+def partial_kernel(runs, from_x, index, counts, *refs):
+    queries, held, outs = refs[:runs], refs[runs], refs[runs + 1 : 2 * runs + 1]
+    slabs, sems = refs[-2:]
+
+    def copy(r, j, p):
+        row = (from_x[r] * RUN_BLOCKS + j) * SLOT_ROOM + p
         return pltpu.make_async_copy(
-            held.at[block], slabs.at[j, pl.ds(p * BS, BS)], sems.at[j, p]
+            held.at[index[row]],
+            slabs.at[r * RUN_BLOCKS + j, pl.ds(p * BS, BS)],
+            sems.at[r * RUN_BLOCKS + j, p],
         )
 
-    def start_block(j, carry):
-        def start(p, inner):
-            copy(j, p).start()
-            return inner
-
-        return lax.fori_loop(0, counts[base + j], start, carry)
-
-    lax.fori_loop(0, RUN_BLOCKS, start_block, 0)
-
+    for r in range(runs):
+
+        def start_block(j, carry, r=r):
+            def start(p, inner):
+                copy(r, j, p).start()
+                return inner
+
+            return lax.fori_loop(0, counts[from_x[r] * RUN_BLOCKS + j], start, carry)
+
+        lax.fori_loop(0, RUN_BLOCKS, start_block, 0)
+
+    for r in range(runs):
+        attend_run(r, from_x[r] * RUN_BLOCKS, counts, copy, queries[r], slabs, outs[r])
+
+
+def attend_run(r, base, counts, copy, query, slabs, out):
     def group(g, carry):
         first = g * UNROLL
         live = [counts[base + first + u] for u in range(UNROLL)]
@@ -92,7 +102,7 @@
         for u in range(UNROLL):
 
             def wait(p, inner, u=u):
-                copy(first + u, p).wait()
+                copy(r, first + u, p).wait()
                 return inner
 
             lax.fori_loop(0, live[u], wait, 0)
@@ -104,32 +114,43 @@
             keys = chunks * CHUNK * BS
             line = lax.broadcasted_iota(jnp.int32, (keys, HD), 0)
             spot = lax.broadcasted_iota(jnp.int32, (PAD, HD), 0)
-            stats = jnp.zeros((PAD, HD), F32)
-            for u in range(UNROLL):
+            each = range(UNROLL)
+            inside = [line < live[u] * BS for u in each]
+            scores = []
+            for u in each:
                 q_rows = query[pl.ds((first + u) * BS, BS), :]
                 q_both = jnp.concatenate([q_rows[:, :HD], q_rows[:, HD:]], axis=0)
-                key = slabs[first + u, 0:keys, 0:HD]
-                value = slabs[first + u, 0:keys, HD : 2 * HD]
-                inside = line < live[u] * BS
-                value = jnp.where(inside, value, jnp.zeros_like(value))
-                scores = lax.dot_general(key, q_both, NT, preferred_element_type=F32)
-                scores = jnp.where(inside, scores * (HD**-0.5 * LOG2E), MASKED)
-                top = jnp.max(scores, axis=0, keepdims=True)
-                power = jnp.where(inside, jnp.exp2(scores - top), 0.0)
-                total = jnp.sum(power, axis=0, keepdims=True)
-                some = total > 0.0
-                total = jnp.where(some, total, 1.0)
-                weights = (power * (1.0 / total)).astype(BF16)
-                mixed = lax.dot_general(weights, value, TN, preferred_element_type=F32)
-                mixed = mixed.astype(BF16)
+                key = slabs[r * RUN_BLOCKS + first + u, 0:keys, 0:HD]
+                scores.append(lax.dot_general(key, q_both, NT, preferred_element_type=F32))
+            scores = [
+                jnp.where(inside[u], scores[u] * (HD**-0.5 * LOG2E), MASKED) for u in each
+            ]
+            tops = [jnp.max(scores[u], axis=0, keepdims=True) for u in each]
+            powers = [
+                jnp.where(inside[u], jnp.exp2(scores[u] - tops[u]), 0.0) for u in each
+            ]
+            totals = [jnp.sum(powers[u], axis=0, keepdims=True) for u in each]
+            some = [totals[u] > 0.0 for u in each]
+            totals = [jnp.where(some[u], totals[u], 1.0) for u in each]
+            weights = [(powers[u] * (1.0 / totals[u])).astype(BF16) for u in each]
+            mixes = []
+            for u in each:
+                value = slabs[r * RUN_BLOCKS + first + u, 0:keys, HD : 2 * HD]
+                value = jnp.where(inside[u], value, jnp.zeros_like(value))
+                mixes.append(
+                    lax.dot_general(weights[u], value, TN, preferred_element_type=F32)
+                )
+            stats = jnp.zeros((PAD, HD), F32)
+            for u in each:
+                level = jnp.where(some[u], tops[u] + jnp.log2(totals[u]), MASKED)
+                high = level.astype(BF16).astype(F32)
+                middle = (level - high).astype(BF16).astype(F32)
+                for t, piece in enumerate((high, middle, level - high - middle)):
+                    stats = jnp.where(spot == 3 * u + t, piece, stats)
+            for u in each:
+                mixed = mixes[u].astype(BF16)
                 out[pl.ds(row0 + u * BS, BS), 0:HD] = mixed[:BS]
                 out[pl.ds(row0 + u * BS, BS), HD : 2 * HD] = mixed[BS:]
-                level = jnp.where(some, top + jnp.log2(total), MASKED)
-                high = level.astype(BF16).astype(F32)
-                middle = (level - high).astype(BF16).astype(F32)
-                low = level - high - middle
-                for t, piece in enumerate((high, middle, low)):
-                    stats = jnp.where(spot == 3 * u + t, piece, stats)
             out[pl.ds(row0 + UNROLL * BS, PAD), 0:HD] = stats.astype(BF16)
             out[pl.ds(row0 + UNROLL * BS, PAD), HD : 2 * HD] = jnp.zeros((PAD, HD), BF16)
 
@@ -145,25 +166,26 @@
     lax.fori_loop(0, RUN_BLOCKS // UNROLL, group, 0)
 
 
-def partial_attention(from_x, index, counts, query, held):
+def partial_attention(from_x, index, counts, queries, held):
+    runs = len(queries)
     rows = RUN_BLOCKS // UNROLL * (UNROLL * BS + PAD)
     smem = pl.BlockSpec(memory_space=pltpu.SMEM)
     vmem = pl.BlockSpec(memory_space=pltpu.VMEM)
     return pl.pallas_call(
-        partial_kernel,
-        in_specs=[smem, smem, smem, vmem, pl.BlockSpec(memory_space=pl.ANY)],
-        out_specs=vmem,
-        out_shape=jax.ShapeDtypeStruct((rows, 2 * HD), BF16),
+        functools.partial(partial_kernel, runs),
+        in_specs=[smem] * 3 + [vmem] * runs + [pl.BlockSpec(memory_space=pl.ANY)],
+        out_specs=[vmem] * runs,
+        out_shape=[jax.ShapeDtypeStruct((rows, 2 * HD), BF16)] * runs,
         scratch_shapes=[
-            pltpu.VMEM((RUN_BLOCKS, SLOT_ROOM * BS, 2 * HD), BF16),
-            pltpu.SemaphoreType.DMA((RUN_BLOCKS, SLOT_ROOM)),
+            pltpu.VMEM((runs * RUN_BLOCKS, SLOT_ROOM * BS, 2 * HD), BF16),
+            pltpu.SemaphoreType.DMA((runs * RUN_BLOCKS, SLOT_ROOM)),
         ],
         compiler_params=pltpu.CompilerParams(vmem_limit_bytes=50 << 20),
         cost_estimate=pl.CostEstimate(
-            flops=10 * 10**9, bytes_accessed=4 << 20, transcendentals=0
+            flops=runs * 5 * 10**9, bytes_accessed=4 << 20, transcendentals=0
         ),
         name="partial_attention",
-    )(from_x, index, counts, query, held)
+    )(from_x, index, counts, *queries, held)
 
 
 def combine_kernel(*refs):
@@ -173,6 +195,7 @@
     def group(g, carry):
         row0 = g * (UNROLL * BS + PAD)
         tail = [p[pl.ds(row0 + UNROLL * BS, PAD), 0:HD].astype(F32) for p in parts]
+        tables = []
         for u in range(UNROLL):
             levels = [
                 t[3 * u : 3 * u + 1] + t[3 * u + 1 : 3 * u + 2] + t[3 * u + 2 : 3 * u + 3]
@@ -184,12 +207,13 @@
             table = jnp.zeros((HD, HD), F32)
             for k, share in enumerate(shares):
                 table = jnp.where(spot == k, share * norm, table)
-            table = table.T
+            tables.append(table.T)
+        for u in range(UNROLL):
             for h in range(2):
                 lanes = slice(h * HD, (h + 1) * HD)
                 mixed = jnp.zeros((BS, HD), F32)
                 for k, part in enumerate(parts):
-                    scale = table[h * BS : (h + 1) * BS, k : k + 1]
+                    scale = tables[u][h * BS : (h + 1) * BS, k : k + 1]
                     mixed += scale * part[pl.ds(row0 + u * BS, BS), lanes].astype(F32)
                 out[pl.ds((g * UNROLL + u) * BS, BS), lanes] = mixed.astype(BF16)
         return carry
@@ -289,7 +313,7 @@
     own_index, own_counts = own_lists(reach)
     zero = jnp.zeros((1,), jnp.int32)
     own_held = kv_rows.reshape(-1, BS, 2 * HD)
-    windows = partial_attention(zero, own_index, own_counts, query_rows, own_held)
+    [windows] = partial_attention(zero, own_index, own_counts, [query_rows], own_held)
 
     before, after = shift(reach, "x", 1), shift(reach, "x", 3)
     index, counts = plane_lists(before, after, global_ids, rand_ids, plane, place)
@@ -298,10 +322,11 @@
     )
 
     parts = [None] * 4
-    for s in (2, 1, 3, 0):
-        from_x = ((place + 4 - s) % 4).reshape(1)
-        part = partial_attention(from_x, index, counts, queries[s], held)
-        parts[s] = part if s == 0 else shift(part, "x", 4 - s)
+    for steps in ((2,), (1,), (3,), (0,)):
+        from_x = jnp.stack([(place + 4 - k) % 4 for k in steps])
+        mine = partial_attention(from_x, index, counts, [queries[k] for k in steps], held)
+        for k, part in zip(steps, mine):
+            parts[k] = part if k == 0 else shift(part, "x", 4 - k)
     return combine(parts + [windows])
 
 

time: 244 us -> 238 us (0.975)
  Pallas kernels: 51.1 us -> 38 us
  waiting for transfers between devices: 72.8 us -> 77.4 us
    pallas_call x5, Pallas kernels: 35.6 us -> 24.5 us  [partial_attention(): pl.pallas_call(functools.partial(partial_kernel, runs), in_specs=[smem] *...]
    ppermute x14, waiting for transfers between devices: 42.2 us -> 46.1 us  [shift(): lax.ppermute(value, axis, [(i, (i + by) % size) for i in range(size)])]
  transfers between devices with their start and end apart: 16 -> 16, of which waited for: 8 -> 9; matrix products, arithmetic and copies ran while one was open for 1% -> 1% of each run, Pallas kernels for 14% -> 11%
where the time goes in v3:
time: 238 us; the launch traced here: 236 us
  waiting for transfers between devices  77.4 us (33%)
  starting transfers between devices  51.4 us (22%)
  blocking collectives  50.7 us (21%)
  Pallas kernels  38 us (16%)
  between operations  13.7 us (6%)
    ppermute x14, starting transfers between devices, shift(): lax.ppermute(value, axis, [(i, (i + by) % size) for i in range(size)])  51.3 us
    ppermute x14, waiting for transfers between devices, shift(): lax.ppermute(value, axis, [(i, (i + by) % size) for i in range(size)])  46.1 us
    all_gather x1, waiting for transfers between devices, per_device(): held = lax.all_gather(kv_rows, ('a', 'b'), axis=0, tiled=True)  30.7 us
    all_gather x1, blocking collectives, per_device(): both = lax.all_gather(both, 'a', axis=0, tiled=True)  25.2 us
    pallas_call x5, Pallas kernels, partial_attention(): pl.pallas_call(functools.partial(partial_kernel, runs), in_specs=[smem] *...  24.5 us
    all_gather x1, blocking collectives, per_device(): kv_own = lax.all_gather(both[:, :width], 'b', axis=0, tiled=True)  12.8 us
    all_gather x1, blocking collectives, per_device(): query_own = lax.all_gather(query_own_in, 'b', axis=0, tiled=True)  12.6 us
    pallas_call x2, Pallas kernels, project(): pl.pallas_call(project_kernel, grid_spec=pltpu.PrefetchScalarGridSpec(num...  10.5 us
  transfers between devices with their start and end apart: 16, of which 9 were waited for; matrix products, arithmetic and copies ran while one was open for 1% of the time, Pallas kernels for 11%

profile of v3, /device:TPU:1, one launch (start us, length us, event | category | flops | bytes accessed | tf_op | source)
XLA Modules:
  0.0 235.7 jit_solution(16784829319430640314)
XLA Ops:
  8.1 25.2 %all_gather.16 = bf16[256,512]{1,0:T(8,128)(2,1)S(1)} all-gather(bf16[64,512]{1,0:T(8,128)(2,1)S(1)} %pad_maximum_fusion), channel_id=1, replica_groups=mesh['a'=4,'b'=4,'x'=4,'y'=4,'c'=2] {'a'}, dimensions={0}, use_global_device_ids=true | all-gather | bytes 327680 | tf_op jit(solution)/shard_map/all_gather | solution.py:293
  33.4 12.8 %all_gather.17 = bf16[1024,256]{1,0:T(8,128)(2,1)S(1)} all-gather(bf16[256,256]{1,0:T(8,128)(2,1)S(1)} %get-tuple-element.47), channel_id=1, replica_groups=mesh['a'=4,'b'=4,'x'=4,'y'=4,'c'=2] {'b'}, dimensions={0}, use_global_device_ids=true | all-gather | bytes 655360 | tf_op jit(solution)/shard_map/all_gather | solution.py:294
  46.1 3.1 %collective-permute-start = (bf16[4,4,64,256]{3,2,1,0:T(8,128)(2,1)S(1)}, bf16[4,4,64,256]{3,2,1,0:T(8,128)(2,1)S(1)}, u32[]{:S(2)}, u32[]{:S(2)}) collective-permute-start(bf16[4,4,64,256]{3,2,1,0:T(8,128)(2,1)S(1)} %bitcast.13), channel_id=1, source_target_pairs={{0,8},{8,16},{16,24},{24,0},{1,9},{9,17},{17,25},{25,1},{2,10},{10... | collective-permute-start | bytes 1572872 | tf_op jit(solution)/shard_map/ppermute | solution.py:28
  49.3 4.4 %collective-permute-start.1 = (bf16[4,4,64,256]{3,2,1,0:T(8,128)(2,1)S(1)}, bf16[4,4,64,256]{3,2,1,0:T(8,128)(2,1)S(1)}, u32[]{:S(2)}, u32[]{:S(2)}) collective-permute-start(bf16[4,4,64,256]{3,2,1,0:T(8,128)(2,1)S(1)} %bitcast.14), channel_id=1, source_target_pairs={{0,16},{8,24},{16,0},{24,8},{1,17},{9,25},{17,1},{25,9},{2,18},{10... | collective-permute-start | bytes 1572872 | tf_op jit(solution)/shard_map/ppermute | solution.py:28
  53.6 3.1 %collective-permute-start.2 = (bf16[4,4,64,256]{3,2,1,0:T(8,128)(2,1)S(1)}, bf16[4,4,64,256]{3,2,1,0:T(8,128)(2,1)S(1)}, u32[]{:S(2)}, u32[]{:S(2)}) collective-permute-start(bf16[4,4,64,256]{3,2,1,0:T(8,128)(2,1)S(1)} %bitcast.15), channel_id=1, source_target_pairs={{0,24},{8,0},{16,8},{24,16},{1,25},{9,1},{17,9},{25,17},{2,26},{10... | collective-permute-start | bytes 1572872 | tf_op jit(solution)/shard_map/ppermute | solution.py:28
  56.7 12.6 %all_gather.18 = bf16[1024,256]{1,0:T(8,128)(2,1)S(1)} all-gather(bf16[256,256]{1,0:T(8,128)(2,1)S(1)} %get-tuple-element.24), channel_id=1, replica_groups=mesh['a'=4,'b'=4,'x'=4,'y'=4,'c'=2] {'b'}, dimensions={0}, use_global_device_ids=true | all-gather | bytes 655360 | tf_op jit(solution)/shard_map/all_gather | solution.py:302
  69.3 3.5 %collective-permute-done.2.part3 = bf16[4,4,64,256]{3,2,1,0:T(8,128)(2,1)S(1)} collective-permute-done((bf16[4,4,64,256]{3,2,1,0:T(8,128)(2,1)S(1)}, bf16[4,4,64,256]{3,2,1,0:T(8,128)(2,1)S(1)}, u32[]{:S(2)}, u32[]{:S(2)}) %collective-permute-start.2) | collective-permute-done | bytes 524320 | tf_op jit(solution)/shard_map/ppermute | solution.py:28
  72.8 5.6 %project.2 = bf16[1024,256]{1,0:T(8,128)(2,1)} custom-call(s32[1]{0:T(128)} %bitcast.1.place, bf16[1024,4096]{1,0:T(8,128)(2,1)} %all-gather.3.cloned.1.call-done.rows, bf16[4,4,64,256]{3,2,1,0:T(8,128)(2,1)S(1)} %bitcast.16, bf16[4,4,64,256]{3,2,1,0:T(8,128)(2,1)S(1)} %collective-permute-done.part1, ...), custom_call_target="tpu_custom_call" | custom-call | flops 2147483648 | bytes 11010048 | tf_op jit(solution)/shard_map/project/pallas_call | solution.py:50
  79.5 6.3 %collective-permute-start.6 = (s32[16]{0:T(128)S(1)}, s32[16]{0:T(128)S(1)}, u32[]{:S(2)}, u32[]{:S(2)}) collective-permute-start(s32[16]{0:T(128)S(1)} %copy-done.5), channel_id=1, source_target_pairs={{0,8},{8,16},{16,24},{24,0},{1,9},{9,17},{17,25},{25,1},{2,10},{10... | collective-permute-start | bytes 200 | tf_op jit(solution)/shard_map/ppermute | solution.py:28
  87.7 3.4 %collective-permute-start.3 = (bf16[4,4,64,256]{3,2,1,0:T(8,128)(2,1)S(1)}, bf16[4,4,64,256]{3,2,1,0:T(8,128)(2,1)S(1)}, u32[]{:S(2)}, u32[]{:S(2)}) collective-permute-start(bf16[4,4,64,256]{3,2,1,0:T(8,128)(2,1)S(1)} %bitcast.9), channel_id=1, source_target_pairs={{0,8},{8,16},{16,24},{24,0},{1,9},{9,17},{17,25},{25,1},{2,10},{10... | collective-permute-start | bytes 1572872 | tf_op jit(solution)/shard_map/ppermute | solution.py:28
  91.1 2.3 collective-permute-start.4
  93.4 4.0 %collective-permute-start.5 = (bf16[4,4,64,256]{3,2,1,0:T(8,128)(2,1)S(1)}, bf16[4,4,64,256]{3,2,1,0:T(8,128)(2,1)S(1)}, u32[]{:S(2)}, u32[]{:S(2)}) collective-permute-start(bf16[4,4,64,256]{3,2,1,0:T(8,128)(2,1)S(1)} %bitcast.11), channel_id=1, source_target_pairs={{0,24},{8,0},{16,8},{24,16},{1,25},{9,1},{17,9},{25,17},{2,26},{10... | collective-permute-start | bytes 1572872 | tf_op jit(solution)/shard_map/ppermute | solution.py:28
  98.2 2.0 collective-permute-done.3.part1
  100.2 10.7 %collective-permute-done.4.part2 = bf16[4,4,64,256]{3,2,1,0:T(8,128)(2,1)S(1)} collective-permute-done((bf16[4,4,64,256]{3,2,1,0:T(8,128)(2,1)S(1)}, bf16[4,4,64,256]{3,2,1,0:T(8,128)(2,1)S(1)}, u32[]{:S(2)}, u32[]{:S(2)}) %collective-permute-start.4) | collective-permute-done | bytes 524320 | tf_op jit(solution)/shard_map/ppermute | solution.py:28
  110.8 6.1 %collective-permute-done.5.part3 = bf16[4,4,64,256]{3,2,1,0:T(8,128)(2,1)S(1)} collective-permute-done((bf16[4,4,64,256]{3,2,1,0:T(8,128)(2,1)S(1)}, bf16[4,4,64,256]{3,2,1,0:T(8,128)(2,1)S(1)}, u32[]{:S(2)}, u32[]{:S(2)}) %collective-permute-start.5) | collective-permute-done | bytes 524320 | tf_op jit(solution)/shard_map/ppermute | solution.py:28
  116.9 4.9 %project.3.refs_0_ = bf16[1024,256]{1,0:T(8,128)(2,1)S(1)} custom-call(s32[1]{0:T(128)} %bitcast.1.place, bf16[1024,4096]{1,0:T(8,128)(2,1)} %all-gather.3.cloned.1.call-done.rows, bf16[4,4,64,256]{3,2,1,0:T(8,128)(2,1)S(1)} %bitcast.12, bf16[4,4,64,256]{3,2,1,0:T(8,128)(2,1)S(1)} %collective-permute-done.3.part1, ...), custom_call_target="tpu_custom_call" | custom-call | flops 2147483648 | bytes 11010048 | tf_op jit(solution)/shard_map/project/pallas_call | solution.py:50
  121.9 5.4 %collective-permute-start.10 = (bf16[1024,256]{1,0:T(8,128)(2,1)S(1)}, bf16[1024,256]{1,0:T(8,128)(2,1)S(1)}, u32[]{:S(2)}, u32[]{:S(2)}) collective-permute-start(bf16[1024,256]{1,0:T(8,128)(2,1)S(1)} %project.3.refs_0_), channel_id=1, source_target_pairs={{0,24},{8,0},{16,8},{24,16},{1,25},{9,1},{17,9},{25,17},{2,26},{10... | collective-permute-start | bytes 1572872 | tf_op jit(solution)/shard_map/ppermute | solution.py:28
  129.2 3.3 %collective-permute-start.9 = (bf16[1024,256]{1,0:T(8,128)(2,1)S(1)}, bf16[1024,256]{1,0:T(8,128)(2,1)S(1)}, u32[]{:S(2)}, u32[]{:S(2)}) collective-permute-start(bf16[1024,256]{1,0:T(8,128)(2,1)S(1)} %project.3.refs_0_), channel_id=1, source_target_pairs={{0,16},{8,24},{16,0},{24,8},{1,17},{9,25},{17,1},{25,9},{2,18},{10... | collective-permute-start | bytes 1572872 | tf_op jit(solution)/shard_map/ppermute | solution.py:28
  132.7 6.1 %partial_attention.5.refs_4_ = bf16[1088,256]{1,0:T(8,128)(2,1)S(1)} custom-call(s32[1]{0:T(128)} %constant.107.clone.1.from_x, s32[128]{0:T(128)S(1)} %reshape.345.index, s32[16]{0:T(128)S(1)} %get-tuple-element.45.counts, bf16[1024,256]{1,0:T(8,128)(2,1)S(1)} %project.3.refs_0_, bf16[16,64,256]{2,1,0:T(8,128)(2,1)} %bitcast.5.refs_1_), custom_call_target="tpu_custom_call" | custom-call | flops 5000000000 | bytes 4194304 | tf_op jit(solution)/shard_map/partial_attention/pallas_call | solution.py:174
  138.8 5.2 %collective-permute-done.8.refs_0_ = bf16[1024,256]{1,0:T(8,128)(2,1)S(1)} collective-permute-done((bf16[1024,256]{1,0:T(8,128)(2,1)S(1)}, bf16[1024,256]{1,0:T(8,128)(2,1)S(1)}, u32[]{:S(2)}, u32[]{:S(2)}) %collective-permute-start.8) | collective-permute-done | bytes 524320 | tf_op jit(solution)/shard_map/ppermute | solution.py:28
  144.8 8.0 %collective-permute-done.9.refs_0_ = bf16[1024,256]{1,0:T(8,128)(2,1)S(1)} collective-permute-done((bf16[1024,256]{1,0:T(8,128)(2,1)S(1)}, bf16[1024,256]{1,0:T(8,128)(2,1)S(1)}, u32[]{:S(2)}, u32[]{:S(2)}) %collective-permute-start.9) | collective-permute-done | bytes 524320 | tf_op jit(solution)/shard_map/ppermute | solution.py:28
  153.6 30.7 %all-gather.5.cloned.1.call-done = bf16[16384,256]{1,0:T(8,128)(2,1)} async-done(((bf16[1024,256]{1,0:T(8,128)(2,1)}), bf16[16384,256]{1,0:T(8,128)(2,1)}) %all-gather.5.cloned.1.call-update) | async-done | bytes 8388624 | tf_op jit(solution)/shard_map/all_gather | solution.py:307
  184.3 4.1 %partial_attention.9 = bf16[1088,256]{1,0:T(8,128)(2,1)S(1)} custom-call(s32[1]{0:T(128)} %bitcast.8.from_x, s32[512]{0:T(512)S(1)} %reshape.348.index, s32[64]{0:T(128)S(1)} %get-tuple-element.34.counts, bf16[1024,256]{1,0:T(8,128)(2,1)S(1)} %collective-permute-done.10.refs_0_, bf16[256,64,256]{2,1,0:T(8,128)(2,1)} %bitcast.17), custom_call_target="tpu_custom_call" | custom-call | flops 5000000000 | bytes 4194304 | tf_op jit(solution)/shard_map/partial_attention/pallas_call | solution.py:174
  188.4 3.7 %collective-permute-start.13 = (bf16[1088,256]{1,0:T(8,128)(2,1)S(1)}, bf16[1088,256]{1,0:T(8,128)(2,1)S(1)}, u32[]{:S(2)}, u32[]{:S(2)}) collective-permute-start(bf16[1088,256]{1,0:T(8,128)(2,1)S(1)} %partial_attention.9), channel_id=1, source_target_pairs={{0,8},{8,16},{16,24},{24,0},{1,9},{9,17},{17,25},{25,1},{2,10},{10... | collective-permute-start | bytes 1671176 | tf_op jit(solution)/shard_map/ppermute | solution.py:28
  192.1 5.0 %partial_attention.8 = bf16[1088,256]{1,0:T(8,128)(2,1)} custom-call(s32[1]{0:T(128)} %bitcast.7.from_x, s32[512]{0:T(512)S(1)} %reshape.348.index, s32[64]{0:T(128)S(1)} %get-tuple-element.34.counts, bf16[1024,256]{1,0:T(8,128)(2,1)S(1)} %copy-done.3, bf16[256,64,256]{2,1,0:T(8,128)(2,1)} %bitcast.18), custom_call_target="tpu_custom_call" | custom-call | flops 5000000000 | bytes 4194304 | tf_op jit(solution)/shard_map/partial_attention/pallas_call | solution.py:174
  197.1 5.6 %collective-permute-start.12 = (bf16[1088,256]{1,0:T(8,128)(2,1)}, bf16[1088,256]{1,0:T(8,128)(2,1)S(1)}, u32[]{:S(2)}, u32[]{:S(2)}) collective-permute-start(bf16[1088,256]{1,0:T(8,128)(2,1)} %partial_attention.8), channel_id=1, source_target_pairs={{0,16},{8,24},{16,0},{24,8},{1,17},{9,25},{17,1},{25,9},{2,18},{10... | collective-permute-start | bytes 1671176 | tf_op jit(solution)/shard_map/ppermute | solution.py:28
  202.8 5.2 %partial_attention.7 = bf16[1088,256]{1,0:T(8,128)(2,1)} custom-call(s32[1]{0:T(128)} %bitcast.6.from_x, s32[512]{0:T(512)S(1)} %reshape.348.index, s32[64]{0:T(128)S(1)} %get-tuple-element.34.counts, bf16[1024,256]{1,0:T(8,128)(2,1)S(1)} %copy-done.1, bf16[256,64,256]{2,1,0:T(8,128)(2,1)} %bitcast.19), custom_call_target="tpu_custom_call" | custom-call | flops 5000000000 | bytes 4194304 | tf_op jit(solution)/shard_map/partial_attention/pallas_call | solution.py:174
  208.0 3.1 %collective-permute-start.11 = (bf16[1088,256]{1,0:T(8,128)(2,1)}, bf16[1088,256]{1,0:T(8,128)(2,1)S(1)}, u32[]{:S(2)}, u32[]{:S(2)}) collective-permute-start(bf16[1088,256]{1,0:T(8,128)(2,1)} %partial_attention.7), channel_id=1, source_target_pairs={{0,24},{8,0},{16,8},{24,16},{1,25},{9,1},{17,9},{25,17},{2,26},{10... | collective-permute-start | bytes 1671176 | tf_op jit(solution)/shard_map/ppermute | solution.py:28
  211.1 4.1 %partial_attention.6.refs_0_ = bf16[1088,256]{1,0:T(8,128)(2,1)S(1)} custom-call(s32[1]{0:T(128)} %bitcast.from_x, s32[512]{0:T(512)S(1)} %reshape.348.index, s32[64]{0:T(128)S(1)} %get-tuple-element.34.counts, bf16[1024,256]{1,0:T(8,128)(2,1)S(1)} %project.3.refs_0_, bf16[256,64,256]{2,1,0:T(8,128)(2,1)} %bitcast.20), custom_call_target="tpu_custom_call" | custom-call | flops 5000000000 | bytes 4194304 | tf_op jit(solution)/shard_map/partial_attention/pallas_call | solution.py:174
  215.2 3.4 %collective-permute-done.12.refs_2_ = bf16[1088,256]{1,0:T(8,128)(2,1)S(1)} collective-permute-done((bf16[1088,256]{1,0:T(8,128)(2,1)}, bf16[1088,256]{1,0:T(8,128)(2,1)S(1)}, u32[]{:S(2)}, u32[]{:S(2)}) %collective-permute-start.12) | collective-permute-done | bytes 557088 | tf_op jit(solution)/shard_map/ppermute | solution.py:28
  218.6 7.2 %collective-permute-done.11.refs_1_ = bf16[1088,256]{1,0:T(8,128)(2,1)S(1)} collective-permute-done((bf16[1088,256]{1,0:T(8,128)(2,1)}, bf16[1088,256]{1,0:T(8,128)(2,1)S(1)}, u32[]{:S(2)}, u32[]{:S(2)}) %collective-permute-start.11) | collective-permute-done | bytes 557088 | tf_op jit(solution)/shard_map/ppermute | solution.py:28
  225.9 3.1 %combine.1 = bf16[1024,256]{1,0:T(8,128)(2,1)} custom-call(bf16[1088,256]{1,0:T(8,128)(2,1)S(1)} %partial_attention.6.refs_0_, bf16[1088,256]{1,0:T(8,128)(2,1)S(1)} %collective-permute-done.11.refs_1_, bf16[1088,256]{1,0:T(8,128)(2,1)S(1)} %collective-permute-done.12.refs_2_, bf16[1088,256]{1,0:T(8,128)(2,1)S(1)} %collective-permute-done.13.refs_3_, ...), custom_call_target="tpu_custom_call" | custom-call | tf_op jit(solution)/shard_map/combine/pallas_call | solution.py:226
  (56 shorter events, 9.1 us)
Async XLA Ops:
  6.5 72.9 %copy-start.4 = (s32[4]{0:T(128)S(1)}, s32[4]{0:T(128)}, u32[]{:S(2)}) copy-start(s32[4]{0:T(128)} %constant.120.clone) | copy-start | bytes 52
  6.5 91.4 %copy-start.6 = (s32[4]{0:T(128)S(1)}, s32[4]{0:T(128)}, u32[]{:S(2)}) copy-start(s32[4]{0:T(128)} %constant.123) | copy-start | bytes 52
  6.5 71.9 %copy-start.7 = (s32[2]{0:T(128)S(1)}, s32[2]{0:T(128)}, u32[]{:S(2)}) copy-start(s32[2]{0:T(128)} %param.11) | copy-start | bytes 28
  6.5 73.0 %copy-start.5 = (s32[16]{0:T(128)S(1)}, s32[16]{0:T(128)}, u32[]{:S(2)}) copy-start(s32[16]{0:T(128)} %param.10) | copy-start | bytes 196
  6.5 66.3 %all-gather.3.cloned.1.call-start = ((), (), s32[]{:S(2)}) async-start(), calls=%async_computation | async-start | bytes 9437184 | tf_op jit(solution)/shard_map/all_gather | solution.py:290
  7.3 177.0 %all-gather.5.cloned.1.call-start = ((), (), s32[]{:S(2)}) async-start(), calls=%async_computation.1 | async-start | bytes 8912896 | tf_op jit(solution)/shard_map/all_gather | solution.py:307
  46.1 23.2 %collective-permute-start = (bf16[4,4,64,256]{3,2,1,0:T(8,128)(2,1)S(1)}, bf16[4,4,64,256]{3,2,1,0:T(8,128)(2,1)S(1)}, u32[]{:S(2)}, u32[]{:S(2)}) collective-permute-start(bf16[4,4,64,256]{3,2,1,0:T(8,128)(2,1)S(1)} %bitcast.13), channel_id=1, source_target_pairs={{0,8},{8,16},{16,24},{24,0},{1,9},{9,17},{17,25},{25,1},{2,10},{10... | collective-permute-start | bytes 1572872 | tf_op jit(solution)/shard_map/ppermute | solution.py:28
  49.3 20.1 %collective-permute-start.1 = (bf16[4,4,64,256]{3,2,1,0:T(8,128)(2,1)S(1)}, bf16[4,4,64,256]{3,2,1,0:T(8,128)(2,1)S(1)}, u32[]{:S(2)}, u32[]{:S(2)}) collective-permute-start(bf16[4,4,64,256]{3,2,1,0:T(8,128)(2,1)S(1)} %bitcast.14), channel_id=1, source_target_pairs={{0,16},{8,24},{16,0},{24,8},{1,17},{9,25},{17,1},{25,9},{2,18},{10... | collective-permute-start | bytes 1572872 | tf_op jit(solution)/shard_map/ppermute | solution.py:28
  53.6 19.2 %collective-permute-start.2 = (bf16[4,4,64,256]{3,2,1,0:T(8,128)(2,1)S(1)}, bf16[4,4,64,256]{3,2,1,0:T(8,128)(2,1)S(1)}, u32[]{:S(2)}, u32[]{:S(2)}) collective-permute-start(bf16[4,4,64,256]{3,2,1,0:T(8,128)(2,1)S(1)} %bitcast.15), channel_id=1, source_target_pairs={{0,24},{8,0},{16,8},{24,16},{1,25},{9,1},{17,9},{25,17},{2,26},{10... | collective-permute-start | bytes 1572872 | tf_op jit(solution)/shard_map/ppermute | solution.py:28
  79.5 18.2 %collective-permute-start.6 = (s32[16]{0:T(128)S(1)}, s32[16]{0:T(128)S(1)}, u32[]{:S(2)}, u32[]{:S(2)}) collective-permute-start(s32[16]{0:T(128)S(1)} %copy-done.5), channel_id=1, source_target_pairs={{0,8},{8,16},{16,24},{24,0},{1,9},{9,17},{17,25},{25,1},{2,10},{10... | collective-permute-start | bytes 200 | tf_op jit(solution)/shard_map/ppermute | solution.py:28
  85.8 12.0 %collective-permute-start.7 = (s32[16]{0:T(128)S(1)}, s32[16]{0:T(128)S(1)}, u32[]{:S(2)}, u32[]{:S(2)}) collective-permute-start(s32[16]{0:T(128)S(1)} %copy-done.5), channel_id=1, source_target_pairs={{0,24},{8,0},{16,8},{24,16},{1,25},{9,1},{17,9},{25,17},{2,26},{10... | collective-permute-start | bytes 200 | tf_op jit(solution)/shard_map/ppermute | solution.py:28
  87.7 12.4 %collective-permute-start.3 = (bf16[4,4,64,256]{3,2,1,0:T(8,128)(2,1)S(1)}, bf16[4,4,64,256]{3,2,1,0:T(8,128)(2,1)S(1)}, u32[]{:S(2)}, u32[]{:S(2)}) collective-permute-start(bf16[4,4,64,256]{3,2,1,0:T(8,128)(2,1)S(1)} %bitcast.9), channel_id=1, source_target_pairs={{0,8},{8,16},{16,24},{24,0},{1,9},{9,17},{17,25},{25,1},{2,10},{10... | collective-permute-start | bytes 1572872 | tf_op jit(solution)/shard_map/ppermute | solution.py:28
  91.1 19.7 %collective-permute-start.4 = (bf16[4,4,64,256]{3,2,1,0:T(8,128)(2,1)S(1)}, bf16[4,4,64,256]{3,2,1,0:T(8,128)(2,1)S(1)}, u32[]{:S(2)}, u32[]{:S(2)}) collective-permute-start(bf16[4,4,64,256]{3,2,1,0:T(8,128)(2,1)S(1)} %bitcast.10), channel_id=1, source_target_pairs={{0,16},{8,24},{16,0},{24,8},{1,17},{9,25},{17,1},{25,9},{2,18},{10... | collective-permute-start | bytes 1572872 | tf_op jit(solution)/shard_map/ppermute | solution.py:28
  93.4 23.6 %collective-permute-start.5 = (bf16[4,4,64,256]{3,2,1,0:T(8,128)(2,1)S(1)}, bf16[4,4,64,256]{3,2,1,0:T(8,128)(2,1)S(1)}, u32[]{:S(2)}, u32[]{:S(2)}) collective-permute-start(bf16[4,4,64,256]{3,2,1,0:T(8,128)(2,1)S(1)} %bitcast.11), channel_id=1, source_target_pairs={{0,24},{8,0},{16,8},{24,16},{1,25},{9,1},{17,9},{25,17},{2,26},{10... | collective-permute-start | bytes 1572872 | tf_op jit(solution)/shard_map/ppermute | solution.py:28
  121.9 16.9 %collective-permute-start.10 = (bf16[1024,256]{1,0:T(8,128)(2,1)S(1)}, bf16[1024,256]{1,0:T(8,128)(2,1)S(1)}, u32[]{:S(2)}, u32[]{:S(2)}) collective-permute-start(bf16[1024,256]{1,0:T(8,128)(2,1)S(1)} %project.3.refs_0_), channel_id=1, source_target_pairs={{0,24},{8,0},{16,8},{24,16},{1,25},{9,1},{17,9},{25,17},{2,26},{10... | collective-permute-start | bytes 1572872 | tf_op jit(solution)/shard_map/ppermute | solution.py:28
  127.3 16.7 %collective-permute-start.8 = (bf16[1024,256]{1,0:T(8,128)(2,1)S(1)}, bf16[1024,256]{1,0:T(8,128)(2,1)S(1)}, u32[]{:S(2)}, u32[]{:S(2)}) collective-permute-start(bf16[1024,256]{1,0:T(8,128)(2,1)S(1)} %project.3.refs_0_), channel_id=1, source_target_pairs={{0,8},{8,16},{16,24},{24,0},{1,9},{9,17},{17,25},{25,1},{2,10},{10... | collective-permute-start | bytes 1572872 | tf_op jit(solution)/shard_map/ppermute | solution.py:28
  129.2 23.6 %collective-permute-start.9 = (bf16[1024,256]{1,0:T(8,128)(2,1)S(1)}, bf16[1024,256]{1,0:T(8,128)(2,1)S(1)}, u32[]{:S(2)}, u32[]{:S(2)}) collective-permute-start(bf16[1024,256]{1,0:T(8,128)(2,1)S(1)} %project.3.refs_0_), channel_id=1, source_target_pairs={{0,16},{8,24},{16,0},{24,8},{1,17},{9,25},{17,1},{25,9},{2,18},{10... | collective-permute-start | bytes 1572872 | tf_op jit(solution)/shard_map/ppermute | solution.py:28
  144.0 0.8 copy-start
  152.8 0.8 copy-start.2
  184.3 7.8 %copy-start.3 = (bf16[1024,256]{1,0:T(8,128)(2,1)S(1)}, bf16[1024,256]{1,0:T(8,128)(2,1)}, u32[]{:S(2)}) copy-start(bf16[1024,256]{1,0:T(8,128)(2,1)} %copy-done.2) | copy-start | bytes 1572868
  188.4 26.7 %collective-permute-start.13 = (bf16[1088,256]{1,0:T(8,128)(2,1)S(1)}, bf16[1088,256]{1,0:T(8,128)(2,1)S(1)}, u32[]{:S(2)}, u32[]{:S(2)}) collective-permute-start(bf16[1088,256]{1,0:T(8,128)(2,1)S(1)} %partial_attention.9), channel_id=1, source_target_pairs={{0,8},{8,16},{16,24},{24,0},{1,9},{9,17},{17,25},{25,1},{2,10},{10... | collective-permute-start | bytes 1671176 | tf_op jit(solution)/shard_map/ppermute | solution.py:28
  192.1 10.7 %copy-start.1 = (bf16[1024,256]{1,0:T(8,128)(2,1)S(1)}, bf16[1024,256]{1,0:T(8,128)(2,1)}, u32[]{:S(2)}) copy-start(bf16[1024,256]{1,0:T(8,128)(2,1)} %copy-done) | copy-start | bytes 1572868
  197.1 21.5 %collective-permute-start.12 = (bf16[1088,256]{1,0:T(8,128)(2,1)}, bf16[1088,256]{1,0:T(8,128)(2,1)S(1)}, u32[]{:S(2)}, u32[]{:S(2)}) collective-permute-start(bf16[1088,256]{1,0:T(8,128)(2,1)} %partial_attention.8), channel_id=1, source_target_pairs={{0,16},{8,24},{16,0},{24,8},{1,17},{9,25},{17,1},{25,9},{2,18},{10... | collective-permute-start | bytes 1671176 | tf_op jit(solution)/shard_map/ppermute | solution.py:28
  208.0 17.9 %collective-permute-start.11 = (bf16[1088,256]{1,0:T(8,128)(2,1)}, bf16[1088,256]{1,0:T(8,128)(2,1)S(1)}, u32[]{:S(2)}, u32[]{:S(2)}) collective-permute-start(bf16[1088,256]{1,0:T(8,128)(2,1)} %partial_attention.7), channel_id=1, source_target_pairs={{0,24},{8,0},{16,8},{24,16},{1,25},{9,1},{17,9},{25,17},{2,26},{10... | collective-permute-start | bytes 1671176 | tf_op jit(solution)/shard_map/ppermute | solution.py:28
Sparse Core Ops, SparseCore 0:
  9.5 63.1 all-gather.2
  78.5 105.7 all-gather.4

commit v4 on v3

--- a/solution.py
+++ b/solution.py
@@ -15,6 +15,7 @@
 SLOT_ROOM = 8
 RUN_BLOCKS = 16
 PAD = 32
+ROW_TILE = 256
 LOG2E = 1.4426950408889634
 MASKED = -1e30
 F32 = jnp.float32
@@ -28,35 +29,48 @@
     return lax.ppermute(value, axis, [(i, (i + by) % size) for i in range(size)])
 
 
-def project_kernel(place, rows, part0, part1, part2, part3, out, weight):
-    @pl.when(pl.program_id(0) == 0)
-    def _():
-        for s, part in enumerate((part0, part1, part2, part3)):
-            owner = lax.rem(place[0] + 4 - s, 4)
-            for za in range(4):
-                for zb in range(4):
-                    weight[za * 4 + zb, owner] = part[zb, za]
-
-    depth = rows.shape[1]
-    flat = weight[...].reshape(depth, out.shape[1])
-    out[...] = jnp.dot(rows[...], flat, preferred_element_type=F32).astype(BF16)
+def project_kernel(place, rows, part0, part1, part2, part3, out, buffer, weight, sems):
+    count, depth = rows.shape
+
+    def copy(t):
+        tile = pl.ds(pl.multiple_of(t * ROW_TILE, ROW_TILE), ROW_TILE)
+        return pltpu.make_async_copy(rows.at[tile], buffer.at[tile], sems.at[t])
+
+    for t in range(count // ROW_TILE):
+        copy(t).start()
+    for s, part in enumerate((part0, part1, part2, part3)):
+        owner = lax.rem(place[0] + 4 - s, 4)
+        for za in range(4):
+            for zb in range(4):
+                weight[za * 4 + zb, owner] = part[zb, za]
+
+    def step(t, carry):
+        copy(t).wait()
+        tile = pl.ds(pl.multiple_of(t * ROW_TILE, ROW_TILE), ROW_TILE)
+        flat = weight[...].reshape(depth, out.shape[1])
+        out[tile, :] = jnp.dot(
+            buffer[tile, :], flat, preferred_element_type=F32
+        ).astype(BF16)
+        return carry
+
+    lax.fori_loop(0, count // ROW_TILE, step, 0)
 
 
 def project(place, rows, parts):
     count, depth = rows.shape
     width = parts[0].shape[-1]
-    tile = 512
-    whole = pl.BlockSpec(memory_space=pltpu.VMEM)
+    vmem = pl.BlockSpec(memory_space=pltpu.VMEM)
     return pl.pallas_call(
         project_kernel,
-        grid_spec=pltpu.PrefetchScalarGridSpec(
-            num_scalar_prefetch=1,
-            grid=(count // tile,),
-            in_specs=[pl.BlockSpec((tile, depth), lambda i, p: (i, 0))] + [whole] * 4,
-            out_specs=pl.BlockSpec((tile, width), lambda i, p: (i, 0)),
-            scratch_shapes=[pltpu.VMEM((16, 4, 64, width), BF16)],
-        ),
+        in_specs=[pl.BlockSpec(memory_space=pltpu.SMEM), pl.BlockSpec(memory_space=pl.ANY)]
+        + [vmem] * 4,
+        out_specs=vmem,
         out_shape=jax.ShapeDtypeStruct((count, width), BF16),
+        scratch_shapes=[
+            pltpu.VMEM((count, depth), BF16),
+            pltpu.VMEM((16, 4, 64, width), BF16),
+            pltpu.SemaphoreType.DMA((count // ROW_TILE,)),
+        ],
         compiler_params=pltpu.CompilerParams(vmem_limit_bytes=50 << 20),
         cost_estimate=pl.CostEstimate(
             flops=2 * count * depth * width,
@@ -69,7 +83,16 @@
 
 def partial_kernel(runs, from_x, index, counts, *refs):
     queries, held, outs = refs[:runs], refs[runs], refs[runs + 1 : 2 * runs + 1]
-    slabs, sems = refs[-2:]
+    slabs, near, far, sems, near_sems, far_sems = refs[-6:]
+
+    def fetch(r):
+        return pltpu.make_async_copy(queries[r], near.at[r], near_sems.at[r])
+
+    def give(r):
+        return pltpu.make_async_copy(far.at[r], outs[r], far_sems.at[r])
+
+    for r in range(runs):
+        fetch(r).start()
 
     def copy(r, j, p):
         row = (from_x[r] * RUN_BLOCKS + j) * SLOT_ROOM + p
@@ -79,19 +102,34 @@
             sems.at[r * RUN_BLOCKS + j, p],
         )
 
+    def start_block(i, carry):
+        r, j = i // RUN_BLOCKS, lax.rem(i, RUN_BLOCKS)
+
+        def start(p, inner):
+            copy(r, j, p).start()
+            return inner
+
+        return lax.fori_loop(0, counts[from_x[r] * RUN_BLOCKS + j], start, carry)
+
+    lax.fori_loop(0, runs * RUN_BLOCKS, start_block, 0)
+
     for r in range(runs):
-
-        def start_block(j, carry, r=r):
-            def start(p, inner):
-                copy(r, j, p).start()
-                return inner
-
-            return lax.fori_loop(0, counts[from_x[r] * RUN_BLOCKS + j], start, carry)
-
-        lax.fori_loop(0, RUN_BLOCKS, start_block, 0)
-
+        fetch(r).wait()
+
+    def run(r, carry):
+        base = from_x[r] * RUN_BLOCKS
+        attend_run(r, base, counts, copy, near.at[r], slabs, far.at[r])
+        for fixed in range(runs):
+
+            @pl.when(r == fixed)
+            def _(fixed=fixed):
+                give(fixed).start()
+
+        return carry
+
+    lax.fori_loop(0, runs, run, 0)
     for r in range(runs):
-        attend_run(r, from_x[r] * RUN_BLOCKS, counts, copy, queries[r], slabs, outs[r])
+        give(r).wait()
 
 
 def attend_run(r, base, counts, copy, query, slabs, out):
@@ -170,15 +208,18 @@
     runs = len(queries)
     rows = RUN_BLOCKS // UNROLL * (UNROLL * BS + PAD)
     smem = pl.BlockSpec(memory_space=pltpu.SMEM)
-    vmem = pl.BlockSpec(memory_space=pltpu.VMEM)
     return pl.pallas_call(
         functools.partial(partial_kernel, runs),
-        in_specs=[smem] * 3 + [vmem] * runs + [pl.BlockSpec(memory_space=pl.ANY)],
-        out_specs=[vmem] * runs,
+        in_specs=[smem] * 3 + [pl.BlockSpec(memory_space=pl.ANY)] * (runs + 1),
+        out_specs=[pl.BlockSpec(memory_space=pl.ANY)] * runs,
         out_shape=[jax.ShapeDtypeStruct((rows, 2 * HD), BF16)] * runs,
         scratch_shapes=[
             pltpu.VMEM((runs * RUN_BLOCKS, SLOT_ROOM * BS, 2 * HD), BF16),
+            pltpu.VMEM((runs, RUN_BLOCKS * BS, 2 * HD), BF16),
+            pltpu.VMEM((runs, rows, 2 * HD), BF16),
             pltpu.SemaphoreType.DMA((runs * RUN_BLOCKS, SLOT_ROOM)),
+            pltpu.SemaphoreType.DMA((runs,)),
+            pltpu.SemaphoreType.DMA((runs,)),
         ],
         compiler_params=pltpu.CompilerParams(vmem_limit_bytes=50 << 20),
         cost_estimate=pl.CostEstimate(
@@ -322,7 +363,7 @@
     )
 
     parts = [None] * 4
-    for steps in ((2,), (1,), (3,), (0,)):
+    for steps in ((2, 1, 3), (0,)):
         from_x = jnp.stack([(place + 4 - k) % 4 for k in steps])
         mine = partial_attention(from_x, index, counts, [queries[k] for k in steps], held)
         for k, part in zip(steps, mine):

time: 238 us -> 242 us (1.017)
  waiting for transfers between devices: 77.4 us -> 87 us
  Pallas kernels: 38 us -> 33.8 us
    ppermute x14, waiting for transfers between devices: 46.1 us -> 55.3 us  [shift(): lax.ppermute(value, axis, [(i, (i + by) % size) for i in range(size)])]
    pallas_call x5 -> x3, Pallas kernels: 24.5 us -> 21 us  [partial_attention(): pl.pallas_call(functools.partial(partial_kernel, runs), in_specs=[smem] *...]
  transfers between devices with their start and end apart: 16 -> 16, of which waited for: 9 -> 9; matrix products, arithmetic and copies ran while one was open for 1% -> 1% of each run, Pallas kernels for 11% -> 6%
where the time goes in v4:
time: 242 us; the launch traced here: 241 us
  waiting for transfers between devices  87 us (36%)
  starting transfers between devices  51.1 us (21%)
  blocking collectives  50.7 us (21%)
  Pallas kernels  33.8 us (14%)
  between operations  13.7 us (6%)
  local copies, waits for them, and re-layouts  2.58 us (1%)
    ppermute x14, waiting for transfers between devices, shift(): lax.ppermute(value, axis, [(i, (i + by) % size) for i in range(size)])  55.3 us
    ppermute x14, starting transfers between devices, shift(): lax.ppermute(value, axis, [(i, (i + by) % size) for i in range(size)])  51 us
    all_gather x1, waiting for transfers between devices, per_device(): held = lax.all_gather(kv_rows, ('a', 'b'), axis=0, tiled=True)  31 us
    all_gather x1, blocking collectives, per_device(): both = lax.all_gather(both, 'a', axis=0, tiled=True)  25.2 us
    pallas_call x3, Pallas kernels, partial_attention(): pl.pallas_call(functools.partial(partial_kernel, runs), in_specs=[smem] *...  21 us
    all_gather x1, blocking collectives, per_device(): kv_own = lax.all_gather(both[:, :width], 'b', axis=0, tiled=True)  12.8 us
    all_gather x1, blocking collectives, per_device(): query_own = lax.all_gather(query_own_in, 'b', axis=0, tiled=True)  12.6 us
    pallas_call x2, Pallas kernels, project(): pl.pallas_call(project_kernel, in_specs=[pl.BlockSpec(memory_space=pltpu....  9.75 us
  transfers between devices with their start and end apart: 16, of which 9 were waited for; matrix products, arithmetic and copies ran while one was open for 1% of the time, Pallas kernels for 6%

profile of v4, /device:TPU:1, one launch (start us, length us, event | category | flops | bytes accessed | tf_op | source)
XLA Modules:
  0.0 241.1 jit_solution(3380840833154625981)
XLA Ops:
  8.1 25.2 %all_gather.16 = bf16[256,512]{1,0:T(8,128)(2,1)S(1)} all-gather(bf16[64,512]{1,0:T(8,128)(2,1)S(1)} %pad_maximum_fusion), channel_id=1, replica_groups=mesh['a'=4,'b'=4,'x'=4,'y'=4,'c'=2] {'a'}, dimensions={0}, use_global_device_ids=true | all-gather | bytes 327680 | tf_op jit(solution)/shard_map/all_gather | solution.py:334
  33.4 12.8 %all_gather.17 = bf16[1024,256]{1,0:T(8,128)(2,1)S(1)} all-gather(bf16[256,256]{1,0:T(8,128)(2,1)S(1)} %get-tuple-element.53), channel_id=1, replica_groups=mesh['a'=4,'b'=4,'x'=4,'y'=4,'c'=2] {'b'}, dimensions={0}, use_global_device_ids=true | all-gather | bytes 655360 | tf_op jit(solution)/shard_map/all_gather | solution.py:335
  46.1 3.1 %collective-permute-start = (bf16[4,4,64,256]{3,2,1,0:T(8,128)(2,1)S(1)}, bf16[4,4,64,256]{3,2,1,0:T(8,128)(2,1)S(1)}, u32[]{:S(2)}, u32[]{:S(2)}) collective-permute-start(bf16[4,4,64,256]{3,2,1,0:T(8,128)(2,1)S(1)} %bitcast.13), channel_id=1, source_target_pairs={{0,8},{8,16},{16,24},{24,0},{1,9},{9,17},{17,25},{25,1},{2,10},{10... | collective-permute-start | bytes 1572872 | tf_op jit(solution)/shard_map/ppermute | solution.py:29
  49.3 4.4 %collective-permute-start.1 = (bf16[4,4,64,256]{3,2,1,0:T(8,128)(2,1)S(1)}, bf16[4,4,64,256]{3,2,1,0:T(8,128)(2,1)S(1)}, u32[]{:S(2)}, u32[]{:S(2)}) collective-permute-start(bf16[4,4,64,256]{3,2,1,0:T(8,128)(2,1)S(1)} %bitcast.14), channel_id=1, source_target_pairs={{0,16},{8,24},{16,0},{24,8},{1,17},{9,25},{17,1},{25,9},{2,18},{10... | collective-permute-start | bytes 1572872 | tf_op jit(solution)/shard_map/ppermute | solution.py:29
  53.6 3.1 %collective-permute-start.2 = (bf16[4,4,64,256]{3,2,1,0:T(8,128)(2,1)S(1)}, bf16[4,4,64,256]{3,2,1,0:T(8,128)(2,1)S(1)}, u32[]{:S(2)}, u32[]{:S(2)}) collective-permute-start(bf16[4,4,64,256]{3,2,1,0:T(8,128)(2,1)S(1)} %bitcast.15), channel_id=1, source_target_pairs={{0,24},{8,0},{16,8},{24,16},{1,25},{9,1},{17,9},{25,17},{2,26},{10... | collective-permute-start | bytes 1572872 | tf_op jit(solution)/shard_map/ppermute | solution.py:29
  56.7 12.6 %all_gather.18 = bf16[1024,256]{1,0:T(8,128)(2,1)S(1)} all-gather(bf16[256,256]{1,0:T(8,128)(2,1)S(1)} %get-tuple-element.27), channel_id=1, replica_groups=mesh['a'=4,'b'=4,'x'=4,'y'=4,'c'=2] {'b'}, dimensions={0}, use_global_device_ids=true | all-gather | bytes 655360 | tf_op jit(solution)/shard_map/all_gather | solution.py:343
  69.3 3.5 %collective-permute-done.2.part3 = bf16[4,4,64,256]{3,2,1,0:T(8,128)(2,1)S(1)} collective-permute-done((bf16[4,4,64,256]{3,2,1,0:T(8,128)(2,1)S(1)}, bf16[4,4,64,256]{3,2,1,0:T(8,128)(2,1)S(1)}, u32[]{:S(2)}, u32[]{:S(2)}) %collective-permute-start.2) | collective-permute-done | bytes 524320 | tf_op jit(solution)/shard_map/ppermute | solution.py:29
  72.8 5.3 %project.2 = bf16[1024,256]{1,0:T(8,128)(2,1)} custom-call(s32[1]{0:T(128)} %bitcast.1.place, bf16[1024,4096]{1,0:T(8,128)(2,1)} %all-gather.3.cloned.1.call-done.rows, bf16[4,4,64,256]{3,2,1,0:T(8,128)(2,1)S(1)} %bitcast.16, bf16[4,4,64,256]{3,2,1,0:T(8,128)(2,1)S(1)} %collective-permute-done.part1, ...), custom_call_target="tpu_custom_call" | custom-call | flops 2147483648 | bytes 11010048 | tf_op jit(solution)/shard_map/project/pallas_call | solution.py:63
  79.3 6.3 %collective-permute-start.6 = (s32[16]{0:T(128)S(1)}, s32[16]{0:T(128)S(1)}, u32[]{:S(2)}, u32[]{:S(2)}) collective-permute-start(s32[16]{0:T(128)S(1)} %copy-done.3), channel_id=1, source_target_pairs={{0,8},{8,16},{16,24},{24,0},{1,9},{9,17},{17,25},{25,1},{2,10},{10... | collective-permute-start | bytes 200 | tf_op jit(solution)/shard_map/ppermute | solution.py:29
  85.6 1.9 collective-permute-start.7
  87.5 3.4 %collective-permute-start.3 = (bf16[4,4,64,256]{3,2,1,0:T(8,128)(2,1)S(1)}, bf16[4,4,64,256]{3,2,1,0:T(8,128)(2,1)S(1)}, u32[]{:S(2)}, u32[]{:S(2)}) collective-permute-start(bf16[4,4,64,256]{3,2,1,0:T(8,128)(2,1)S(1)} %bitcast.9), channel_id=1, source_target_pairs={{0,8},{8,16},{16,24},{24,0},{1,9},{9,17},{17,25},{25,1},{2,10},{10... | collective-permute-start | bytes 1572872 | tf_op jit(solution)/shard_map/ppermute | solution.py:29
  90.9 2.3 collective-permute-start.4
  93.2 4.0 %collective-permute-start.5 = (bf16[4,4,64,256]{3,2,1,0:T(8,128)(2,1)S(1)}, bf16[4,4,64,256]{3,2,1,0:T(8,128)(2,1)S(1)}, u32[]{:S(2)}, u32[]{:S(2)}) collective-permute-start(bf16[4,4,64,256]{3,2,1,0:T(8,128)(2,1)S(1)} %bitcast.11), channel_id=1, source_target_pairs={{0,24},{8,0},{16,8},{24,16},{1,25},{9,1},{17,9},{25,17},{2,26},{10... | collective-permute-start | bytes 1572872 | tf_op jit(solution)/shard_map/ppermute | solution.py:29
  98.0 2.0 collective-permute-done.3.part1
  100.0 10.6 %collective-permute-done.4.part2 = bf16[4,4,64,256]{3,2,1,0:T(8,128)(2,1)S(1)} collective-permute-done((bf16[4,4,64,256]{3,2,1,0:T(8,128)(2,1)S(1)}, bf16[4,4,64,256]{3,2,1,0:T(8,128)(2,1)S(1)}, u32[]{:S(2)}, u32[]{:S(2)}) %collective-permute-start.4) | collective-permute-done | bytes 524320 | tf_op jit(solution)/shard_map/ppermute | solution.py:29
  110.6 6.1 %collective-permute-done.5.part3 = bf16[4,4,64,256]{3,2,1,0:T(8,128)(2,1)S(1)} collective-permute-done((bf16[4,4,64,256]{3,2,1,0:T(8,128)(2,1)S(1)}, bf16[4,4,64,256]{3,2,1,0:T(8,128)(2,1)S(1)}, u32[]{:S(2)}, u32[]{:S(2)}) %collective-permute-start.5) | collective-permute-done | bytes 524320 | tf_op jit(solution)/shard_map/ppermute | solution.py:29
  116.7 4.5 %project.3.refs_0_ = bf16[1024,256]{1,0:T(8,128)(2,1)S(1)} custom-call(s32[1]{0:T(128)} %bitcast.1.place, bf16[1024,4096]{1,0:T(8,128)(2,1)} %all-gather.3.cloned.1.call-done.rows, bf16[4,4,64,256]{3,2,1,0:T(8,128)(2,1)S(1)} %bitcast.12, bf16[4,4,64,256]{3,2,1,0:T(8,128)(2,1)S(1)} %collective-permute-done.3.part1, ...), custom_call_target="tpu_custom_call" | custom-call | flops 2147483648 | bytes 11010048 | tf_op jit(solution)/shard_map/project/pallas_call | solution.py:63
  121.2 5.4 %collective-permute-start.10 = (bf16[1024,256]{1,0:T(8,128)(2,1)S(1)}, bf16[1024,256]{1,0:T(8,128)(2,1)S(1)}, u32[]{:S(2)}, u32[]{:S(2)}) collective-permute-start(bf16[1024,256]{1,0:T(8,128)(2,1)S(1)} %project.3.refs_0_), channel_id=1, source_target_pairs={{0,24},{8,0},{16,8},{24,16},{1,25},{9,1},{17,9},{25,17},{2,26},{10... | collective-permute-start | bytes 1572872 | tf_op jit(solution)/shard_map/ppermute | solution.py:29
  126.7 1.9 collective-permute-start.8
  128.6 3.3 %collective-permute-start.9 = (bf16[1024,256]{1,0:T(8,128)(2,1)S(1)}, bf16[1024,256]{1,0:T(8,128)(2,1)S(1)}, u32[]{:S(2)}, u32[]{:S(2)}) collective-permute-start(bf16[1024,256]{1,0:T(8,128)(2,1)S(1)} %project.3.refs_0_), channel_id=1, source_target_pairs={{0,16},{8,24},{16,0},{24,8},{1,17},{9,25},{17,1},{25,9},{2,18},{10... | collective-permute-start | bytes 1572872 | tf_op jit(solution)/shard_map/ppermute | solution.py:29
  132.1 6.1 %partial_attention.3.refs_4_ = bf16[1088,256]{1,0:T(8,128)(2,1)S(1)} custom-call(s32[1]{0:T(128)} %constant.107.clone.1.from_x, s32[128]{0:T(128)S(1)} %reshape.345.index, s32[16]{0:T(128)S(1)} %get-tuple-element.51.counts, bf16[1024,256]{1,0:T(8,128)(2,1)S(1)} %project.3.refs_0_, bf16[16,64,256]{2,1,0:T(8,128)(2,1)} %bitcast.5.refs_1_), custom_call_target="tpu_custom_call" | custom-call | flops 5000000000 | bytes 4194304 | tf_op jit(solution)/shard_map/partial_attention/pallas_call | solution.py:211
  138.2 5.1 %collective-permute-done.8.refs_1_ = bf16[1024,256]{1,0:T(8,128)(2,1)S(1)} collective-permute-done((bf16[1024,256]{1,0:T(8,128)(2,1)S(1)}, bf16[1024,256]{1,0:T(8,128)(2,1)S(1)}, u32[]{:S(2)}, u32[]{:S(2)}) %collective-permute-start.8) | collective-permute-done | bytes 524320 | tf_op jit(solution)/shard_map/ppermute | solution.py:29
  143.3 8.8 %collective-permute-done.9.refs_0_ = bf16[1024,256]{1,0:T(8,128)(2,1)S(1)} collective-permute-done((bf16[1024,256]{1,0:T(8,128)(2,1)S(1)}, bf16[1024,256]{1,0:T(8,128)(2,1)S(1)}, u32[]{:S(2)}, u32[]{:S(2)}) %collective-permute-start.9) | collective-permute-done | bytes 524320 | tf_op jit(solution)/shard_map/ppermute | solution.py:29
  153.0 31.0 %all-gather.5.cloned.1.call-done = bf16[16384,256]{1,0:T(8,128)(2,1)} async-done(((bf16[1024,256]{1,0:T(8,128)(2,1)}), bf16[16384,256]{1,0:T(8,128)(2,1)}) %all-gather.5.cloned.1.call-update) | async-done | bytes 8388624 | tf_op jit(solution)/shard_map/all_gather | solution.py:348
  185.0 10.6 %partial_attention.5 = (bf16[1088,256]{1,0:T(8,128)(2,1)}, bf16[1088,256]{1,0:T(8,128)(2,1)}, bf16[1088,256]{1,0:T(8,128)(2,1)S(1)}) custom-call(s32[3]{0:T(128)S(1)} %pad_add_fusion.1.from_x, s32[512]{0:T(512)S(1)} %reshape.348.index, s32[64]{0:T(128)S(1)} %get-tuple-element.37.counts, bf16[1024,256]{1,0:T(8,128)(2,1)S(1)} %copy-done.1, ...), custom_call_target="tpu_custom_call" | custom-call | flops 15000000512 | bytes 4194304 | tf_op jit(solution)/shard_map/partial_attention/pallas_call | solution.py:211
  195.7 5.4 %collective-permute-start.11 = (bf16[1088,256]{1,0:T(8,128)(2,1)}, bf16[1088,256]{1,0:T(8,128)(2,1)S(1)}, u32[]{:S(2)}, u32[]{:S(2)}) collective-permute-start(bf16[1088,256]{1,0:T(8,128)(2,1)} %get-tuple-element.43), channel_id=1, source_target_pairs={{0,24},{8,0},{16,8},{24,16},{1,25},{9,1},{17,9},{25,17},{2,26},{10... | collective-permute-start | bytes 1671176 | tf_op jit(solution)/shard_map/ppermute | solution.py:29
  201.1 3.7 %collective-permute-start.12 = (bf16[1088,256]{1,0:T(8,128)(2,1)}, bf16[1088,256]{1,0:T(8,128)(2,1)S(1)}, u32[]{:S(2)}, u32[]{:S(2)}) collective-permute-start(bf16[1088,256]{1,0:T(8,128)(2,1)} %get-tuple-element.44), channel_id=1, source_target_pairs={{0,16},{8,24},{16,0},{24,8},{1,17},{9,25},{17,1},{25,9},{2,18},{10... | collective-permute-start | bytes 1671176 | tf_op jit(solution)/shard_map/ppermute | solution.py:29
  204.7 3.0 %collective-permute-start.13 = (bf16[1088,256]{1,0:T(8,128)(2,1)S(1)}, bf16[1088,256]{1,0:T(8,128)(2,1)S(1)}, u32[]{:S(2)}, u32[]{:S(2)}) collective-permute-start(bf16[1088,256]{1,0:T(8,128)(2,1)S(1)} %get-tuple-element.45), channel_id=1, source_target_pairs={{0,8},{8,16},{16,24},{24,0},{1,9},{9,17},{17,25},{25,1},{2,10},{10... | collective-permute-start | bytes 1671176 | tf_op jit(solution)/shard_map/ppermute | solution.py:29
  207.7 4.3 %partial_attention.4.refs_0_ = bf16[1088,256]{1,0:T(8,128)(2,1)S(1)} custom-call(s32[1]{0:T(128)} %bitcast.from_x, s32[512]{0:T(512)S(1)} %reshape.348.index, s32[64]{0:T(128)S(1)} %get-tuple-element.37.counts, bf16[1024,256]{1,0:T(8,128)(2,1)S(1)} %project.3.refs_0_, bf16[256,64,256]{2,1,0:T(8,128)(2,1)} %bitcast.18), custom_call_target="tpu_custom_call" | custom-call | flops 5000000000 | bytes 4194304 | tf_op jit(solution)/shard_map/partial_attention/pallas_call | solution.py:211
  212.0 12.4 %collective-permute-done.11.refs_1_ = bf16[1088,256]{1,0:T(8,128)(2,1)S(1)} collective-permute-done((bf16[1088,256]{1,0:T(8,128)(2,1)}, bf16[1088,256]{1,0:T(8,128)(2,1)S(1)}, u32[]{:S(2)}, u32[]{:S(2)}) %collective-permute-start.11) | collective-permute-done | bytes 557088 | tf_op jit(solution)/shard_map/ppermute | solution.py:29
  224.5 6.7 %collective-permute-done.13.refs_3_ = bf16[1088,256]{1,0:T(8,128)(2,1)S(1)} collective-permute-done((bf16[1088,256]{1,0:T(8,128)(2,1)S(1)}, bf16[1088,256]{1,0:T(8,128)(2,1)S(1)}, u32[]{:S(2)}, u32[]{:S(2)}) %collective-permute-start.13) | collective-permute-done | bytes 557088 | tf_op jit(solution)/shard_map/ppermute | solution.py:29
  231.2 3.1 %combine.1 = bf16[1024,256]{1,0:T(8,128)(2,1)} custom-call(bf16[1088,256]{1,0:T(8,128)(2,1)S(1)} %partial_attention.4.refs_0_, bf16[1088,256]{1,0:T(8,128)(2,1)S(1)} %collective-permute-done.11.refs_1_, bf16[1088,256]{1,0:T(8,128)(2,1)S(1)} %collective-permute-done.12.refs_2_, bf16[1088,256]{1,0:T(8,128)(2,1)S(1)} %collective-permute-done.13.refs_3_, ...), custom_call_target="tpu_custom_call" | custom-call | tf_op jit(solution)/shard_map/combine/pallas_call | solution.py:267
  (51 shorter events, 5.6 us)
Async XLA Ops:
  6.5 72.7 %copy-start.2 = (s32[4]{0:T(128)S(1)}, s32[4]{0:T(128)}, u32[]{:S(2)}) copy-start(s32[4]{0:T(128)} %constant.120.clone) | copy-start | bytes 52
  6.5 91.2 %copy-start.4 = (s32[4]{0:T(128)S(1)}, s32[4]{0:T(128)}, u32[]{:S(2)}) copy-start(s32[4]{0:T(128)} %constant.123) | copy-start | bytes 52
  6.5 71.6 %copy-start.5 = (s32[2]{0:T(128)S(1)}, s32[2]{0:T(128)}, u32[]{:S(2)}) copy-start(s32[2]{0:T(128)} %param.11) | copy-start | bytes 28
  6.5 72.7 %copy-start.3 = (s32[16]{0:T(128)S(1)}, s32[16]{0:T(128)}, u32[]{:S(2)}) copy-start(s32[16]{0:T(128)} %param.10) | copy-start | bytes 196
  6.5 66.3 %all-gather.3.cloned.1.call-start = ((), (), s32[]{:S(2)}) async-start(), calls=%async_computation | async-start | bytes 9437184 | tf_op jit(solution)/shard_map/all_gather | solution.py:331
  7.3 176.7 %all-gather.5.cloned.1.call-start = ((), (), s32[]{:S(2)}) async-start(), calls=%async_computation.1 | async-start | bytes 8912896 | tf_op jit(solution)/shard_map/all_gather | solution.py:348
  46.1 23.2 %collective-permute-start = (bf16[4,4,64,256]{3,2,1,0:T(8,128)(2,1)S(1)}, bf16[4,4,64,256]{3,2,1,0:T(8,128)(2,1)S(1)}, u32[]{:S(2)}, u32[]{:S(2)}) collective-permute-start(bf16[4,4,64,256]{3,2,1,0:T(8,128)(2,1)S(1)} %bitcast.13), channel_id=1, source_target_pairs={{0,8},{8,16},{16,24},{24,0},{1,9},{9,17},{17,25},{25,1},{2,10},{10... | collective-permute-start | bytes 1572872 | tf_op jit(solution)/shard_map/ppermute | solution.py:29
  49.3 20.1 %collective-permute-start.1 = (bf16[4,4,64,256]{3,2,1,0:T(8,128)(2,1)S(1)}, bf16[4,4,64,256]{3,2,1,0:T(8,128)(2,1)S(1)}, u32[]{:S(2)}, u32[]{:S(2)}) collective-permute-start(bf16[4,4,64,256]{3,2,1,0:T(8,128)(2,1)S(1)} %bitcast.14), channel_id=1, source_target_pairs={{0,16},{8,24},{16,0},{24,8},{1,17},{9,25},{17,1},{25,9},{2,18},{10... | collective-permute-start | bytes 1572872 | tf_op jit(solution)/shard_map/ppermute | solution.py:29
  53.6 19.2 %collective-permute-start.2 = (bf16[4,4,64,256]{3,2,1,0:T(8,128)(2,1)S(1)}, bf16[4,4,64,256]{3,2,1,0:T(8,128)(2,1)S(1)}, u32[]{:S(2)}, u32[]{:S(2)}) collective-permute-start(bf16[4,4,64,256]{3,2,1,0:T(8,128)(2,1)S(1)} %bitcast.15), channel_id=1, source_target_pairs={{0,24},{8,0},{16,8},{24,16},{1,25},{9,1},{17,9},{25,17},{2,26},{10... | collective-permute-start | bytes 1572872 | tf_op jit(solution)/shard_map/ppermute | solution.py:29
  79.3 18.2 %collective-permute-start.6 = (s32[16]{0:T(128)S(1)}, s32[16]{0:T(128)S(1)}, u32[]{:S(2)}, u32[]{:S(2)}) collective-permute-start(s32[16]{0:T(128)S(1)} %copy-done.3), channel_id=1, source_target_pairs={{0,8},{8,16},{16,24},{24,0},{1,9},{9,17},{17,25},{25,1},{2,10},{10... | collective-permute-start | bytes 200 | tf_op jit(solution)/shard_map/ppermute | solution.py:29
  85.6 12.0 %collective-permute-start.7 = (s32[16]{0:T(128)S(1)}, s32[16]{0:T(128)S(1)}, u32[]{:S(2)}, u32[]{:S(2)}) collective-permute-start(s32[16]{0:T(128)S(1)} %copy-done.3), channel_id=1, source_target_pairs={{0,24},{8,0},{16,8},{24,16},{1,25},{9,1},{17,9},{25,17},{2,26},{10... | collective-permute-start | bytes 200 | tf_op jit(solution)/shard_map/ppermute | solution.py:29
  87.5 12.4 %collective-permute-start.3 = (bf16[4,4,64,256]{3,2,1,0:T(8,128)(2,1)S(1)}, bf16[4,4,64,256]{3,2,1,0:T(8,128)(2,1)S(1)}, u32[]{:S(2)}, u32[]{:S(2)}) collective-permute-start(bf16[4,4,64,256]{3,2,1,0:T(8,128)(2,1)S(1)} %bitcast.9), channel_id=1, source_target_pairs={{0,8},{8,16},{16,24},{24,0},{1,9},{9,17},{17,25},{25,1},{2,10},{10... | collective-permute-start | bytes 1572872 | tf_op jit(solution)/shard_map/ppermute | solution.py:29
  90.9 19.7 %collective-permute-start.4 = (bf16[4,4,64,256]{3,2,1,0:T(8,128)(2,1)S(1)}, bf16[4,4,64,256]{3,2,1,0:T(8,128)(2,1)S(1)}, u32[]{:S(2)}, u32[]{:S(2)}) collective-permute-start(bf16[4,4,64,256]{3,2,1,0:T(8,128)(2,1)S(1)} %bitcast.10), channel_id=1, source_target_pairs={{0,16},{8,24},{16,0},{24,8},{1,17},{9,25},{17,1},{25,9},{2,18},{10... | collective-permute-start | bytes 1572872 | tf_op jit(solution)/shard_map/ppermute | solution.py:29
  93.2 23.6 %collective-permute-start.5 = (bf16[4,4,64,256]{3,2,1,0:T(8,128)(2,1)S(1)}, bf16[4,4,64,256]{3,2,1,0:T(8,128)(2,1)S(1)}, u32[]{:S(2)}, u32[]{:S(2)}) collective-permute-start(bf16[4,4,64,256]{3,2,1,0:T(8,128)(2,1)S(1)} %bitcast.11), channel_id=1, source_target_pairs={{0,24},{8,0},{16,8},{24,16},{1,25},{9,1},{17,9},{25,17},{2,26},{10... | collective-permute-start | bytes 1572872 | tf_op jit(solution)/shard_map/ppermute | solution.py:29
  121.2 17.0 %collective-permute-start.10 = (bf16[1024,256]{1,0:T(8,128)(2,1)S(1)}, bf16[1024,256]{1,0:T(8,128)(2,1)S(1)}, u32[]{:S(2)}, u32[]{:S(2)}) collective-permute-start(bf16[1024,256]{1,0:T(8,128)(2,1)S(1)} %project.3.refs_0_), channel_id=1, source_target_pairs={{0,24},{8,0},{16,8},{24,16},{1,25},{9,1},{17,9},{25,17},{2,26},{10... | collective-permute-start | bytes 1572872 | tf_op jit(solution)/shard_map/ppermute | solution.py:29
  126.7 16.7 %collective-permute-start.8 = (bf16[1024,256]{1,0:T(8,128)(2,1)S(1)}, bf16[1024,256]{1,0:T(8,128)(2,1)S(1)}, u32[]{:S(2)}, u32[]{:S(2)}) collective-permute-start(bf16[1024,256]{1,0:T(8,128)(2,1)S(1)} %project.3.refs_0_), channel_id=1, source_target_pairs={{0,8},{8,16},{16,24},{24,0},{1,9},{9,17},{17,25},{25,1},{2,10},{10... | collective-permute-start | bytes 1572872 | tf_op jit(solution)/shard_map/ppermute | solution.py:29
  128.6 23.6 %collective-permute-start.9 = (bf16[1024,256]{1,0:T(8,128)(2,1)S(1)}, bf16[1024,256]{1,0:T(8,128)(2,1)S(1)}, u32[]{:S(2)}, u32[]{:S(2)}) collective-permute-start(bf16[1024,256]{1,0:T(8,128)(2,1)S(1)} %project.3.refs_0_), channel_id=1, source_target_pairs={{0,16},{8,24},{16,0},{24,8},{1,17},{9,25},{17,1},{25,9},{2,18},{10... | collective-permute-start | bytes 1572872 | tf_op jit(solution)/shard_map/ppermute | solution.py:29
  152.2 0.8 copy-start
  184.0 1.0 copy-start.1
  195.7 28.8 %collective-permute-start.11 = (bf16[1088,256]{1,0:T(8,128)(2,1)}, bf16[1088,256]{1,0:T(8,128)(2,1)S(1)}, u32[]{:S(2)}, u32[]{:S(2)}) collective-permute-start(bf16[1088,256]{1,0:T(8,128)(2,1)} %get-tuple-element.43), channel_id=1, source_target_pairs={{0,24},{8,0},{16,8},{24,16},{1,25},{9,1},{17,9},{25,17},{2,26},{10... | collective-permute-start | bytes 1671176 | tf_op jit(solution)/shard_map/ppermute | solution.py:29
  201.1 23.4 %collective-permute-start.12 = (bf16[1088,256]{1,0:T(8,128)(2,1)}, bf16[1088,256]{1,0:T(8,128)(2,1)S(1)}, u32[]{:S(2)}, u32[]{:S(2)}) collective-permute-start(bf16[1088,256]{1,0:T(8,128)(2,1)} %get-tuple-element.44), channel_id=1, source_target_pairs={{0,16},{8,24},{16,0},{24,8},{1,17},{9,25},{17,1},{25,9},{2,18},{10... | collective-permute-start | bytes 1671176 | tf_op jit(solution)/shard_map/ppermute | solution.py:29
  204.7 26.4 %collective-permute-start.13 = (bf16[1088,256]{1,0:T(8,128)(2,1)S(1)}, bf16[1088,256]{1,0:T(8,128)(2,1)S(1)}, u32[]{:S(2)}, u32[]{:S(2)}) collective-permute-start(bf16[1088,256]{1,0:T(8,128)(2,1)S(1)} %get-tuple-element.45), channel_id=1, source_target_pairs={{0,8},{8,16},{16,24},{24,0},{1,9},{9,17},{17,25},{25,1},{2,10},{10... | collective-permute-start | bytes 1671176 | tf_op jit(solution)/shard_map/ppermute | solution.py:29
Sparse Core Ops, SparseCore 0:
  9.5 63.1 all-gather.2
  78.2 105.7 all-gather.4

commit v5 on v2

--- a/solution.py
+++ b/solution.py
@@ -11,16 +11,16 @@
 BS = 64
 WMAX = 2
 CHUNK = 2
-UNROLL = 4
+UNROLL = 8
 SLOT_ROOM = 8
 RUN_BLOCKS = 16
-PAD = 16
+PAD = 64
+ROW_TILE = 256
 LOG2E = 1.4426950408889634
 MASKED = -1e30
 F32 = jnp.float32
 BF16 = jnp.bfloat16
 NT = (((1,), (1,)), ((), ()))
-TN = (((0,), (0,)), ((), ()))
 
 
 def shift(value, axis, by):
@@ -28,35 +28,48 @@
     return lax.ppermute(value, axis, [(i, (i + by) % size) for i in range(size)])
 
 
-def project_kernel(place, rows, part0, part1, part2, part3, out, weight):
-    @pl.when(pl.program_id(0) == 0)
-    def _():
-        for s, part in enumerate((part0, part1, part2, part3)):
-            owner = lax.rem(place[0] + 4 - s, 4)
-            for za in range(4):
-                for zb in range(4):
-                    weight[za * 4 + zb, owner] = part[zb, za]
-
-    depth = rows.shape[1]
-    flat = weight[...].reshape(depth, out.shape[1])
-    out[...] = jnp.dot(rows[...], flat, preferred_element_type=F32).astype(BF16)
+def project_kernel(place, rows, part0, part1, part2, part3, out, buffer, weight, sems):
+    count, depth = rows.shape
+
+    def copy(t):
+        tile = pl.ds(pl.multiple_of(t * ROW_TILE, ROW_TILE), ROW_TILE)
+        return pltpu.make_async_copy(rows.at[tile], buffer.at[tile], sems.at[t])
+
+    for t in range(count // ROW_TILE):
+        copy(t).start()
+    for s, part in enumerate((part0, part1, part2, part3)):
+        owner = lax.rem(place[0] + 4 - s, 4)
+        for za in range(4):
+            for zb in range(4):
+                weight[za * 4 + zb, owner] = part[zb, za]
+
+    def step(t, carry):
+        copy(t).wait()
+        tile = pl.ds(pl.multiple_of(t * ROW_TILE, ROW_TILE), ROW_TILE)
+        flat = weight[...].reshape(depth, out.shape[1])
+        out[tile, :] = jnp.dot(
+            buffer[tile, :], flat, preferred_element_type=F32
+        ).astype(BF16)
+        return carry
+
+    lax.fori_loop(0, count // ROW_TILE, step, 0)
 
 
 def project(place, rows, parts):
     count, depth = rows.shape
     width = parts[0].shape[-1]
-    tile = 256
-    whole = pl.BlockSpec(parts[0].shape, lambda i, p: (0, 0, 0, 0))
+    vmem = pl.BlockSpec(memory_space=pltpu.VMEM)
     return pl.pallas_call(
         project_kernel,
-        grid_spec=pltpu.PrefetchScalarGridSpec(
-            num_scalar_prefetch=1,
-            grid=(count // tile,),
-            in_specs=[pl.BlockSpec((tile, depth), lambda i, p: (i, 0))] + [whole] * 4,
-            out_specs=pl.BlockSpec((tile, width), lambda i, p: (i, 0)),
-            scratch_shapes=[pltpu.VMEM((16, 4, 64, width), BF16)],
-        ),
+        in_specs=[pl.BlockSpec(memory_space=pltpu.SMEM), pl.BlockSpec(memory_space=pl.ANY)]
+        + [vmem] * 4,
+        out_specs=vmem,
         out_shape=jax.ShapeDtypeStruct((count, width), BF16),
+        scratch_shapes=[
+            pltpu.VMEM((count, depth), BF16),
+            pltpu.VMEM((16, 4, 64, width), BF16),
+            pltpu.SemaphoreType.DMA((count // ROW_TILE,)),
+        ],
         compiler_params=pltpu.CompilerParams(vmem_limit_bytes=50 << 20),
         cost_estimate=pl.CostEstimate(
             flops=2 * count * depth * width,
@@ -67,13 +80,14 @@
     )(place, rows, *parts)
 
 
-def partial_kernel(from_x, index, counts, query, held, out, slabs, sems):
+def partial_kernel(from_x, index, counts, query, held, out, slabs, tops_at, sums_at, sems):
     base = from_x[0] * RUN_BLOCKS
 
     def copy(j, p):
-        block = index[(base + j) * SLOT_ROOM + p]
         return pltpu.make_async_copy(
-            held.at[block], slabs.at[j, pl.ds(p * BS, BS)], sems.at[j, p]
+            held.at[index[(base + j) * SLOT_ROOM + p]],
+            slabs.at[j, pl.ds(p * BS, BS)],
+            sems.at[j, p],
         )
 
     def start_block(j, carry):
@@ -98,40 +112,42 @@
             lax.fori_loop(0, live[u], wait, 0)
 
         most = functools.reduce(jnp.maximum, live)
-        row0 = g * (UNROLL * BS + PAD)
 
         def attend(chunks):
             keys = chunks * CHUNK * BS
+            each = range(UNROLL)
+            lane = lax.broadcasted_iota(jnp.int32, (2 * BS, keys), 1)
             line = lax.broadcasted_iota(jnp.int32, (keys, HD), 0)
-            spot = lax.broadcasted_iota(jnp.int32, (PAD, HD), 0)
-            stats = jnp.zeros((PAD, HD), F32)
-            for u in range(UNROLL):
+            spot = lax.broadcasted_iota(jnp.int32, (2 * BS, HD), 1)
+            ones = jnp.ones((keys, HD), BF16)
+            scores = []
+            for u in each:
                 q_rows = query[pl.ds((first + u) * BS, BS), :]
                 q_both = jnp.concatenate([q_rows[:, :HD], q_rows[:, HD:]], axis=0)
                 key = slabs[first + u, 0:keys, 0:HD]
+                scores.append(lax.dot_general(q_both, key, NT, preferred_element_type=F32))
+            scores = [
+                jnp.where(lane < live[u] * BS, scores[u] * (HD**-0.5 * LOG2E), MASKED)
+                for u in each
+            ]
+            tops = [jnp.max(scores[u], axis=1, keepdims=True) for u in each]
+            powers = [jnp.exp2(scores[u] - tops[u]).astype(BF16) for u in each]
+            mixes = []
+            for u in each:
                 value = slabs[first + u, 0:keys, HD : 2 * HD]
-                inside = line < live[u] * BS
-                value = jnp.where(inside, value, jnp.zeros_like(value))
-                scores = lax.dot_general(key, q_both, NT, preferred_element_type=F32)
-                scores = jnp.where(inside, scores * (HD**-0.5 * LOG2E), MASKED)
-                top = jnp.max(scores, axis=0, keepdims=True)
-                power = jnp.where(inside, jnp.exp2(scores - top), 0.0)
-                total = jnp.sum(power, axis=0, keepdims=True)
-                some = total > 0.0
-                total = jnp.where(some, total, 1.0)
-                weights = (power * (1.0 / total)).astype(BF16)
-                mixed = lax.dot_general(weights, value, TN, preferred_element_type=F32)
-                mixed = mixed.astype(BF16)
-                out[pl.ds(row0 + u * BS, BS), 0:HD] = mixed[:BS]
-                out[pl.ds(row0 + u * BS, BS), HD : 2 * HD] = mixed[BS:]
-                level = jnp.where(some, top + jnp.log2(total), MASKED)
-                high = level.astype(BF16).astype(F32)
-                middle = (level - high).astype(BF16).astype(F32)
-                low = level - high - middle
-                for t, piece in enumerate((high, middle, low)):
-                    stats = jnp.where(spot == 3 * u + t, piece, stats)
-            out[pl.ds(row0 + UNROLL * BS, PAD), 0:HD] = stats.astype(BF16)
-            out[pl.ds(row0 + UNROLL * BS, PAD), HD : 2 * HD] = jnp.zeros((PAD, HD), BF16)
+                value = jnp.where(line < live[u] * BS, value, jnp.zeros_like(value))
+                value = jnp.concatenate([value, ones], axis=1)
+                mixes.append(jnp.dot(powers[u], value, preferred_element_type=F32))
+            top_table, sum_table = tops_at[...], sums_at[...]
+            for u in each:
+                here = spot == first + u
+                top_table = jnp.where(here, tops[u], top_table)
+                sum_table = jnp.where(here, mixes[u][:, HD:], sum_table)
+            tops_at[...], sums_at[...] = top_table, sum_table
+            for u in each:
+                mixed = (mixes[u][:, :HD] * (1.0 / mixes[u][:, HD:])).astype(BF16)
+                out[pl.ds((first + u) * BS, BS), 0:HD] = mixed[:BS]
+                out[pl.ds((first + u) * BS, BS), HD : 2 * HD] = mixed[BS:]
 
         for chunks in (1, 2, 3, 4):
             low_edge = (chunks - 1) * CHUNK if chunks > 1 else -1
@@ -142,25 +158,39 @@
 
         return carry
 
+    tops_at[...] = jnp.zeros_like(tops_at)
+    sums_at[...] = jnp.ones_like(sums_at)
     lax.fori_loop(0, RUN_BLOCKS // UNROLL, group, 0)
+    spot = lax.broadcasted_iota(jnp.int32, (2 * BS, HD), 1)
+    level = jnp.where(spot < RUN_BLOCKS, tops_at[...] + jnp.log2(sums_at[...]), 0.0)
+    high = level.astype(BF16).astype(F32)
+    middle = (level - high).astype(BF16).astype(F32)
+    low = level - high - middle
+    packed = (
+        high + pltpu.roll(middle, RUN_BLOCKS, 1) + pltpu.roll(low, 2 * RUN_BLOCKS, 1)
+    ).astype(BF16)
+    out[pl.ds(RUN_BLOCKS * BS, PAD), 0:HD] = packed[:BS]
+    out[pl.ds(RUN_BLOCKS * BS, PAD), HD : 2 * HD] = packed[BS:]
 
 
 def partial_attention(from_x, index, counts, query, held):
-    rows = RUN_BLOCKS // UNROLL * (UNROLL * BS + PAD)
+    rows = RUN_BLOCKS * BS + PAD
     smem = pl.BlockSpec(memory_space=pltpu.SMEM)
     vmem = pl.BlockSpec(memory_space=pltpu.VMEM)
     return pl.pallas_call(
         partial_kernel,
-        in_specs=[smem, smem, smem, vmem, pl.BlockSpec(memory_space=pl.ANY)],
+        in_specs=[smem] * 3 + [vmem, pl.BlockSpec(memory_space=pl.ANY)],
         out_specs=vmem,
         out_shape=jax.ShapeDtypeStruct((rows, 2 * HD), BF16),
         scratch_shapes=[
             pltpu.VMEM((RUN_BLOCKS, SLOT_ROOM * BS, 2 * HD), BF16),
+            pltpu.VMEM((2 * BS, HD), F32),
+            pltpu.VMEM((2 * BS, HD), F32),
             pltpu.SemaphoreType.DMA((RUN_BLOCKS, SLOT_ROOM)),
         ],
         compiler_params=pltpu.CompilerParams(vmem_limit_bytes=50 << 20),
         cost_estimate=pl.CostEstimate(
-            flops=10 * 10**9, bytes_accessed=4 << 20, transcendentals=0
+            flops=2 * 10**9, bytes_accessed=1 << 16, transcendentals=0
         ),
         name="partial_attention",
     )(from_x, index, counts, query, held)
@@ -168,33 +198,31 @@
 
 def combine_kernel(*refs):
     parts, out = refs[:-1], refs[-1]
-    spot = lax.broadcasted_iota(jnp.int32, (HD, HD), 0)
-
-    def group(g, carry):
-        row0 = g * (UNROLL * BS + PAD)
-        tail = [p[pl.ds(row0 + UNROLL * BS, PAD), 0:HD].astype(F32) for p in parts]
-        for u in range(UNROLL):
-            levels = [
-                t[3 * u : 3 * u + 1] + t[3 * u + 1 : 3 * u + 2] + t[3 * u + 2 : 3 * u + 3]
-                for t in tail
+    rows = pl.ds(RUN_BLOCKS * BS, PAD)
+    scales = []
+    for h in range(2):
+        lanes = slice(h * HD, (h + 1) * HD)
+        levels = []
+        for part in parts:
+            packed = part[rows, lanes].astype(F32)
+            levels.append(
+                packed
+                + pltpu.roll(packed, HD - RUN_BLOCKS, 1)
+                + pltpu.roll(packed, HD - 2 * RUN_BLOCKS, 1)
+            )
+        top = functools.reduce(jnp.maximum, levels)
+        shares = [jnp.exp2(level - top) for level in levels]
+        norm = 1.0 / functools.reduce(jnp.add, shares)
+        scales.append([share * norm for share in shares])
+    for j in range(RUN_BLOCKS):
+        block = slice(j * BS, (j + 1) * BS)
+        for h in range(2):
+            lanes = slice(h * HD, (h + 1) * HD)
+            terms = [
+                scales[h][k][:, j : j + 1] * part[block, lanes].astype(F32)
+                for k, part in enumerate(parts)
             ]
-            top = functools.reduce(jnp.maximum, levels)
-            shares = [jnp.exp2(level - top) for level in levels]
-            norm = 1.0 / functools.reduce(jnp.add, shares)
-            table = jnp.zeros((HD, HD), F32)
-            for k, share in enumerate(shares):
-                table = jnp.where(spot == k, share * norm, table)
-            table = table.T
-            for h in range(2):
-                lanes = slice(h * HD, (h + 1) * HD)
-                mixed = jnp.zeros((BS, HD), F32)
-                for k, part in enumerate(parts):
-                    scale = table[h * BS : (h + 1) * BS, k : k + 1]
-                    mixed += scale * part[pl.ds(row0 + u * BS, BS), lanes].astype(F32)
-                out[pl.ds((g * UNROLL + u) * BS, BS), lanes] = mixed.astype(BF16)
-        return carry
-
-    lax.fori_loop(0, RUN_BLOCKS // UNROLL, group, 0)
+            out[block, lanes] = functools.reduce(jnp.add, terms).astype(BF16)
 
 
 def combine(parts):
@@ -298,11 +326,12 @@
     )
 
     parts = [None] * 4
+    turn = place
     for s in (2, 1, 3, 0):
-        from_x = ((place + 4 - s) % 4).reshape(1)
+        from_x = ((turn + 4 - s) % 4).reshape(1)
         part = partial_attention(from_x, index, counts, queries[s], held)
         parts[s] = part if s == 0 else shift(part, "x", 4 - s)
-    return combine(parts + [windows])
+    return combine([parts[0], parts[3], parts[1], parts[2], windows])
 
 
 def solution(mesh):

time: 244 us -> 236 us (0.967)
  Pallas kernels: 51.1 us -> 36.7 us
  waiting for transfers between devices: 72.8 us -> 79.7 us
    pallas_call x7, Pallas kernels: 47.7 us -> 33.3 us  [the longest x5 23.5 us: partial_attention(): pl.pallas_call(partial_kernel, in_specs=[smem] * 3 + [vmem, pl.BlockSpec(...]
    ppermute x14, waiting for transfers between devices: 42.2 us -> 47.1 us  [shift(): lax.ppermute(value, axis, [(i, (i + by) % size) for i in range(size)])]
  transfers between devices with their start and end apart: 16 -> 16, of which waited for: 8 -> 9; matrix products, arithmetic and copies ran while one was open for 1% -> 1% of each run, Pallas kernels for 14% -> 10%
where the time goes in v5:
time: 236 us; the launch traced here: 234 us
  waiting for transfers between devices  79.7 us (34%)
  blocking collectives  50.7 us (21%)
  starting transfers between devices  49.9 us (21%)
  Pallas kernels  36.7 us (16%)
  between operations  13.7 us (6%)
    ppermute x14, starting transfers between devices, shift(): lax.ppermute(value, axis, [(i, (i + by) % size) for i in range(size)])  49.8 us
    ppermute x14, waiting for transfers between devices, shift(): lax.ppermute(value, axis, [(i, (i + by) % size) for i in range(size)])  47.1 us
    all_gather x1, waiting for transfers between devices, per_device(): held = lax.all_gather(kv_rows, ('a', 'b'), axis=0, tiled=True)  31.9 us
    all_gather x1, blocking collectives, per_device(): both = lax.all_gather(both, 'a', axis=0, tiled=True)  25.2 us
    pallas_call x5, Pallas kernels, partial_attention(): pl.pallas_call(partial_kernel, in_specs=[smem] * 3 + [vmem, pl.BlockSpec(...  23.5 us
    all_gather x1, blocking collectives, per_device(): kv_own = lax.all_gather(both[:, :width], 'b', axis=0, tiled=True)  12.8 us
    all_gather x1, blocking collectives, per_device(): query_own = lax.all_gather(query_own_in, 'b', axis=0, tiled=True)  12.6 us
    pallas_call x2, Pallas kernels, project(): pl.pallas_call(project_kernel, in_specs=[pl.BlockSpec(memory_space=pltpu....  9.76 us
  transfers between devices with their start and end apart: 16, of which 9 were waited for; matrix products, arithmetic and copies ran while one was open for 1% of the time, Pallas kernels for 10%

profile of v5, /device:TPU:1, one launch (start us, length us, event | category | flops | bytes accessed | tf_op | source)
XLA Modules:
  0.0 233.5 jit_solution(16412150063589058484)
XLA Ops:
  8.1 25.2 %all_gather.16 = bf16[256,512]{1,0:T(8,128)(2,1)S(1)} all-gather(bf16[64,512]{1,0:T(8,128)(2,1)S(1)} %pad_maximum_fusion), channel_id=1, replica_groups=mesh['a'=4,'b'=4,'x'=4,'y'=4,'c'=2] {'a'}, dimensions={0}, use_global_device_ids=true | all-gather | bytes 327680 | tf_op jit(solution)/shard_map/all_gather | solution.py:297
  33.4 12.8 %all_gather.17 = bf16[1024,256]{1,0:T(8,128)(2,1)S(1)} all-gather(bf16[256,256]{1,0:T(8,128)(2,1)S(1)} %get-tuple-element.47), channel_id=1, replica_groups=mesh['a'=4,'b'=4,'x'=4,'y'=4,'c'=2] {'b'}, dimensions={0}, use_global_device_ids=true | all-gather | bytes 655360 | tf_op jit(solution)/shard_map/all_gather | solution.py:298
  46.1 3.1 %collective-permute-start = (bf16[4,4,64,256]{3,2,1,0:T(8,128)(2,1)S(1)}, bf16[4,4,64,256]{3,2,1,0:T(8,128)(2,1)S(1)}, u32[]{:S(2)}, u32[]{:S(2)}) collective-permute-start(bf16[4,4,64,256]{3,2,1,0:T(8,128)(2,1)S(1)} %bitcast.13), channel_id=1, source_target_pairs={{0,8},{8,16},{16,24},{24,0},{1,9},{9,17},{17,25},{25,1},{2,10},{10... | collective-permute-start | bytes 1572872 | tf_op jit(solution)/shard_map/ppermute | solution.py:28
  49.3 4.4 %collective-permute-start.1 = (bf16[4,4,64,256]{3,2,1,0:T(8,128)(2,1)S(1)}, bf16[4,4,64,256]{3,2,1,0:T(8,128)(2,1)S(1)}, u32[]{:S(2)}, u32[]{:S(2)}) collective-permute-start(bf16[4,4,64,256]{3,2,1,0:T(8,128)(2,1)S(1)} %bitcast.14), channel_id=1, source_target_pairs={{0,16},{8,24},{16,0},{24,8},{1,17},{9,25},{17,1},{25,9},{2,18},{10... | collective-permute-start | bytes 1572872 | tf_op jit(solution)/shard_map/ppermute | solution.py:28
  53.6 3.1 %collective-permute-start.2 = (bf16[4,4,64,256]{3,2,1,0:T(8,128)(2,1)S(1)}, bf16[4,4,64,256]{3,2,1,0:T(8,128)(2,1)S(1)}, u32[]{:S(2)}, u32[]{:S(2)}) collective-permute-start(bf16[4,4,64,256]{3,2,1,0:T(8,128)(2,1)S(1)} %bitcast.15), channel_id=1, source_target_pairs={{0,24},{8,0},{16,8},{24,16},{1,25},{9,1},{17,9},{25,17},{2,26},{10... | collective-permute-start | bytes 1572872 | tf_op jit(solution)/shard_map/ppermute | solution.py:28
  56.7 12.6 %all_gather.18 = bf16[1024,256]{1,0:T(8,128)(2,1)S(1)} all-gather(bf16[256,256]{1,0:T(8,128)(2,1)S(1)} %get-tuple-element.24), channel_id=1, replica_groups=mesh['a'=4,'b'=4,'x'=4,'y'=4,'c'=2] {'b'}, dimensions={0}, use_global_device_ids=true | all-gather | bytes 655360 | tf_op jit(solution)/shard_map/all_gather | solution.py:306
  69.3 3.5 %collective-permute-done.2.part3 = bf16[4,4,64,256]{3,2,1,0:T(8,128)(2,1)S(1)} collective-permute-done((bf16[4,4,64,256]{3,2,1,0:T(8,128)(2,1)S(1)}, bf16[4,4,64,256]{3,2,1,0:T(8,128)(2,1)S(1)}, u32[]{:S(2)}, u32[]{:S(2)}) %collective-permute-start.2) | collective-permute-done | bytes 524320 | tf_op jit(solution)/shard_map/ppermute | solution.py:28
  72.8 5.3 %project.2 = bf16[1024,256]{1,0:T(8,128)(2,1)} custom-call(s32[1]{0:T(128)} %bitcast.1.place, bf16[1024,4096]{1,0:T(8,128)(2,1)} %all-gather.3.cloned.1.call-done.rows, bf16[4,4,64,256]{3,2,1,0:T(8,128)(2,1)S(1)} %bitcast.16, bf16[4,4,64,256]{3,2,1,0:T(8,128)(2,1)S(1)} %collective-permute-done.part1, ...), custom_call_target="tpu_custom_call" | custom-call | flops 2147483648 | bytes 11010048 | tf_op jit(solution)/shard_map/project/pallas_call | solution.py:62
  79.2 6.3 %collective-permute-start.6 = (s32[16]{0:T(128)S(1)}, s32[16]{0:T(128)S(1)}, u32[]{:S(2)}, u32[]{:S(2)}) collective-permute-start(s32[16]{0:T(128)S(1)} %copy-done.1), channel_id=1, source_target_pairs={{0,8},{8,16},{16,24},{24,0},{1,9},{9,17},{17,25},{25,1},{2,10},{10... | collective-permute-start | bytes 200 | tf_op jit(solution)/shard_map/ppermute | solution.py:28
  87.5 3.4 %collective-permute-start.3 = (bf16[4,4,64,256]{3,2,1,0:T(8,128)(2,1)S(1)}, bf16[4,4,64,256]{3,2,1,0:T(8,128)(2,1)S(1)}, u32[]{:S(2)}, u32[]{:S(2)}) collective-permute-start(bf16[4,4,64,256]{3,2,1,0:T(8,128)(2,1)S(1)} %bitcast.9), channel_id=1, source_target_pairs={{0,8},{8,16},{16,24},{24,0},{1,9},{9,17},{17,25},{25,1},{2,10},{10... | collective-permute-start | bytes 1572872 | tf_op jit(solution)/shard_map/ppermute | solution.py:28
  90.8 2.3 collective-permute-start.4
  93.1 4.0 %collective-permute-start.5 = (bf16[4,4,64,256]{3,2,1,0:T(8,128)(2,1)S(1)}, bf16[4,4,64,256]{3,2,1,0:T(8,128)(2,1)S(1)}, u32[]{:S(2)}, u32[]{:S(2)}) collective-permute-start(bf16[4,4,64,256]{3,2,1,0:T(8,128)(2,1)S(1)} %bitcast.11), channel_id=1, source_target_pairs={{0,24},{8,0},{16,8},{24,16},{1,25},{9,1},{17,9},{25,17},{2,26},{10... | collective-permute-start | bytes 1572872 | tf_op jit(solution)/shard_map/ppermute | solution.py:28
  97.7 2.2 collective-permute-done.3.part1
  99.9 10.6 %collective-permute-done.4.part2 = bf16[4,4,64,256]{3,2,1,0:T(8,128)(2,1)S(1)} collective-permute-done((bf16[4,4,64,256]{3,2,1,0:T(8,128)(2,1)S(1)}, bf16[4,4,64,256]{3,2,1,0:T(8,128)(2,1)S(1)}, u32[]{:S(2)}, u32[]{:S(2)}) %collective-permute-start.4) | collective-permute-done | bytes 524320 | tf_op jit(solution)/shard_map/ppermute | solution.py:28
  110.5 6.1 %collective-permute-done.5.part3 = bf16[4,4,64,256]{3,2,1,0:T(8,128)(2,1)S(1)} collective-permute-done((bf16[4,4,64,256]{3,2,1,0:T(8,128)(2,1)S(1)}, bf16[4,4,64,256]{3,2,1,0:T(8,128)(2,1)S(1)}, u32[]{:S(2)}, u32[]{:S(2)}) %collective-permute-start.5) | collective-permute-done | bytes 524320 | tf_op jit(solution)/shard_map/ppermute | solution.py:28
  116.7 4.5 %project.3.query = bf16[1024,256]{1,0:T(8,128)(2,1)S(1)} custom-call(s32[1]{0:T(128)} %bitcast.1.place, bf16[1024,4096]{1,0:T(8,128)(2,1)} %all-gather.3.cloned.1.call-done.rows, bf16[4,4,64,256]{3,2,1,0:T(8,128)(2,1)S(1)} %bitcast.12, bf16[4,4,64,256]{3,2,1,0:T(8,128)(2,1)S(1)} %collective-permute-done.3.part1, ...), custom_call_target="tpu_custom_call" | custom-call | flops 2147483648 | bytes 11010048 | tf_op jit(solution)/shard_map/project/pallas_call | solution.py:62
  121.1 5.4 %collective-permute-start.10 = (bf16[1024,256]{1,0:T(8,128)(2,1)S(1)}, bf16[1024,256]{1,0:T(8,128)(2,1)S(1)}, u32[]{:S(2)}, u32[]{:S(2)}) collective-permute-start(bf16[1024,256]{1,0:T(8,128)(2,1)S(1)} %project.3.query), channel_id=1, source_target_pairs={{0,24},{8,0},{16,8},{24,16},{1,25},{9,1},{17,9},{25,17},{2,26},{10... | collective-permute-start | bytes 1572872 | tf_op jit(solution)/shard_map/ppermute | solution.py:28
  128.5 3.1 %collective-permute-start.9 = (bf16[1024,256]{1,0:T(8,128)(2,1)S(1)}, bf16[1024,256]{1,0:T(8,128)(2,1)S(1)}, u32[]{:S(2)}, u32[]{:S(2)}) collective-permute-start(bf16[1024,256]{1,0:T(8,128)(2,1)S(1)} %project.3.query), channel_id=1, source_target_pairs={{0,16},{8,24},{16,0},{24,8},{1,17},{9,25},{17,1},{25,9},{2,18},{10... | collective-permute-start | bytes 1572872 | tf_op jit(solution)/shard_map/ppermute | solution.py:28
  132.0 5.7 %partial_attention.5.refs_4_ = bf16[1088,256]{1,0:T(8,128)(2,1)S(1)} custom-call(s32[1]{0:T(128)} %constant.107.clone.1.from_x, s32[128]{0:T(128)S(1)} %reshape.358.index, s32[16]{0:T(128)S(1)} %get-tuple-element.45.counts, bf16[1024,256]{1,0:T(8,128)(2,1)S(1)} %project.3.query, bf16[16,64,256]{2,1,0:T(8,128)(2,1)} %bitcast.5.held), custom_call_target="tpu_custom_call" | custom-call | flops 2000000000 | bytes 65536 | tf_op jit(solution)/shard_map/partial_attention/pallas_call | solution.py:180
  137.8 5.5 %collective-permute-done.8.query = bf16[1024,256]{1,0:T(8,128)(2,1)S(1)} collective-permute-done((bf16[1024,256]{1,0:T(8,128)(2,1)S(1)}, bf16[1024,256]{1,0:T(8,128)(2,1)S(1)}, u32[]{:S(2)}, u32[]{:S(2)}) %collective-permute-start.8) | collective-permute-done | bytes 524320 | tf_op jit(solution)/shard_map/ppermute | solution.py:28
  143.3 8.8 %collective-permute-done.9.query = bf16[1024,256]{1,0:T(8,128)(2,1)S(1)} collective-permute-done((bf16[1024,256]{1,0:T(8,128)(2,1)S(1)}, bf16[1024,256]{1,0:T(8,128)(2,1)S(1)}, u32[]{:S(2)}, u32[]{:S(2)}) %collective-permute-start.9) | collective-permute-done | bytes 524320 | tf_op jit(solution)/shard_map/ppermute | solution.py:28
  152.1 31.9 %all-gather.5.cloned.1.call-done = bf16[16384,256]{1,0:T(8,128)(2,1)} async-done(((bf16[1024,256]{1,0:T(8,128)(2,1)}), bf16[16384,256]{1,0:T(8,128)(2,1)}) %all-gather.5.cloned.1.call-update) | async-done | bytes 8388624 | tf_op jit(solution)/shard_map/all_gather | solution.py:311
  184.0 4.0 %partial_attention.9 = bf16[1088,256]{1,0:T(8,128)(2,1)S(1)} custom-call(s32[1]{0:T(128)} %bitcast.8.from_x, s32[512]{0:T(512)S(1)} %reshape.361.index, s32[64]{0:T(128)S(1)} %get-tuple-element.34.counts, bf16[1024,256]{1,0:T(8,128)(2,1)S(1)} %collective-permute-done.9.query, bf16[256,64,256]{2,1,0:T(8,128)(2,1)} %bitcast.17), custom_call_target="tpu_custom_call" | custom-call | flops 2000000000 | bytes 65536 | tf_op jit(solution)/shard_map/partial_attention/pallas_call | solution.py:180
  188.0 4.8 %collective-permute-start.13 = (bf16[1088,256]{1,0:T(8,128)(2,1)S(1)}, bf16[1088,256]{1,0:T(8,128)(2,1)S(1)}, u32[]{:S(2)}, u32[]{:S(2)}) collective-permute-start(bf16[1088,256]{1,0:T(8,128)(2,1)S(1)} %partial_attention.9), channel_id=1, source_target_pairs={{0,16},{8,24},{16,0},{24,8},{1,17},{9,25},{17,1},{25,9},{2,18},{10... | collective-permute-start | bytes 1671176 | tf_op jit(solution)/shard_map/ppermute | solution.py:28
  192.7 4.8 %partial_attention.8 = bf16[1088,256]{1,0:T(8,128)(2,1)} custom-call(s32[1]{0:T(128)} %bitcast.7.from_x, s32[512]{0:T(512)S(1)} %reshape.361.index, s32[64]{0:T(128)S(1)} %get-tuple-element.34.counts, bf16[1024,256]{1,0:T(8,128)(2,1)S(1)} %collective-permute-done.8.query, bf16[256,64,256]{2,1,0:T(8,128)(2,1)} %bitcast.18), custom_call_target="tpu_custom_call" | custom-call | flops 2000000000 | bytes 65536 | tf_op jit(solution)/shard_map/partial_attention/pallas_call | solution.py:180
  197.6 4.3 %collective-permute-start.12 = (bf16[1088,256]{1,0:T(8,128)(2,1)}, bf16[1088,256]{1,0:T(8,128)(2,1)S(1)}, u32[]{:S(2)}, u32[]{:S(2)}) collective-permute-start(bf16[1088,256]{1,0:T(8,128)(2,1)} %partial_attention.8), channel_id=1, source_target_pairs={{0,24},{8,0},{16,8},{24,16},{1,25},{9,1},{17,9},{25,17},{2,26},{10... | collective-permute-start | bytes 1671176 | tf_op jit(solution)/shard_map/ppermute | solution.py:28
  201.9 5.0 %partial_attention.7 = bf16[1088,256]{1,0:T(8,128)(2,1)} custom-call(s32[1]{0:T(128)} %bitcast.6.from_x, s32[512]{0:T(512)S(1)} %reshape.361.index, s32[64]{0:T(128)S(1)} %get-tuple-element.34.counts, bf16[1024,256]{1,0:T(8,128)(2,1)S(1)} %collective-permute-done.10.query, bf16[256,64,256]{2,1,0:T(8,128)(2,1)} %bitcast.19), custom_call_target="tpu_custom_call" | custom-call | flops 2000000000 | bytes 65536 | tf_op jit(solution)/shard_map/partial_attention/pallas_call | solution.py:180
  206.9 1.9 collective-permute-start.11
  208.9 4.0 %partial_attention.6.refs_0_ = bf16[1088,256]{1,0:T(8,128)(2,1)S(1)} custom-call(s32[1]{0:T(128)} %bitcast.from_x, s32[512]{0:T(512)S(1)} %reshape.361.index, s32[64]{0:T(128)S(1)} %get-tuple-element.34.counts, bf16[1024,256]{1,0:T(8,128)(2,1)S(1)} %project.3.query, bf16[256,64,256]{2,1,0:T(8,128)(2,1)} %bitcast.20), custom_call_target="tpu_custom_call" | custom-call | flops 2000000000 | bytes 65536 | tf_op jit(solution)/shard_map/partial_attention/pallas_call | solution.py:180
  212.9 5.2 %collective-permute-done.12.refs_2_ = bf16[1088,256]{1,0:T(8,128)(2,1)S(1)} collective-permute-done((bf16[1088,256]{1,0:T(8,128)(2,1)}, bf16[1088,256]{1,0:T(8,128)(2,1)S(1)}, u32[]{:S(2)}, u32[]{:S(2)}) %collective-permute-start.12) | collective-permute-done | bytes 557088 | tf_op jit(solution)/shard_map/ppermute | solution.py:28
  218.0 5.2 %collective-permute-done.11.refs_1_ = bf16[1088,256]{1,0:T(8,128)(2,1)} collective-permute-done((bf16[1088,256]{1,0:T(8,128)(2,1)}, bf16[1088,256]{1,0:T(8,128)(2,1)}, u32[]{:S(2)}, u32[]{:S(2)}) %collective-permute-start.11) | collective-permute-done | bytes 557088 | tf_op jit(solution)/shard_map/ppermute | solution.py:28
  223.3 3.5 %combine.1 = bf16[1024,256]{1,0:T(8,128)(2,1)} custom-call(bf16[1088,256]{1,0:T(8,128)(2,1)S(1)} %partial_attention.6.refs_0_, bf16[1088,256]{1,0:T(8,128)(2,1)} %collective-permute-done.11.refs_1_, bf16[1088,256]{1,0:T(8,128)(2,1)S(1)} %collective-permute-done.12.refs_2_, bf16[1088,256]{1,0:T(8,128)(2,1)S(1)} %collective-permute-done.13.refs_3_, ...), custom_call_target="tpu_custom_call" | custom-call | tf_op jit(solution)/shard_map/combine/pallas_call | solution.py:230
  (48 shorter events, 7.5 us)
Async XLA Ops:
  6.5 72.6 %copy-start = (s32[4]{0:T(128)S(1)}, s32[4]{0:T(128)}, u32[]{:S(2)}) copy-start(s32[4]{0:T(128)} %constant.120.clone) | copy-start | bytes 52
  6.5 91.1 %copy-start.2 = (s32[4]{0:T(128)S(1)}, s32[4]{0:T(128)}, u32[]{:S(2)}) copy-start(s32[4]{0:T(128)} %constant.123) | copy-start | bytes 52
  6.5 71.6 %copy-start.3 = (s32[2]{0:T(128)S(1)}, s32[2]{0:T(128)}, u32[]{:S(2)}) copy-start(s32[2]{0:T(128)} %param.11) | copy-start | bytes 28
  6.5 72.7 %copy-start.1 = (s32[16]{0:T(128)S(1)}, s32[16]{0:T(128)}, u32[]{:S(2)}) copy-start(s32[16]{0:T(128)} %param.10) | copy-start | bytes 196
  6.5 66.3 %all-gather.3.cloned.1.call-start = ((), (), s32[]{:S(2)}) async-start(), calls=%async_computation | async-start | bytes 9437184 | tf_op jit(solution)/shard_map/all_gather | solution.py:294
  7.3 176.7 %all-gather.5.cloned.1.call-start = ((), (), s32[]{:S(2)}) async-start(), calls=%async_computation.1 | async-start | bytes 8912896 | tf_op jit(solution)/shard_map/all_gather | solution.py:311
  46.1 23.2 %collective-permute-start = (bf16[4,4,64,256]{3,2,1,0:T(8,128)(2,1)S(1)}, bf16[4,4,64,256]{3,2,1,0:T(8,128)(2,1)S(1)}, u32[]{:S(2)}, u32[]{:S(2)}) collective-permute-start(bf16[4,4,64,256]{3,2,1,0:T(8,128)(2,1)S(1)} %bitcast.13), channel_id=1, source_target_pairs={{0,8},{8,16},{16,24},{24,0},{1,9},{9,17},{17,25},{25,1},{2,10},{10... | collective-permute-start | bytes 1572872 | tf_op jit(solution)/shard_map/ppermute | solution.py:28
  49.3 20.1 %collective-permute-start.1 = (bf16[4,4,64,256]{3,2,1,0:T(8,128)(2,1)S(1)}, bf16[4,4,64,256]{3,2,1,0:T(8,128)(2,1)S(1)}, u32[]{:S(2)}, u32[]{:S(2)}) collective-permute-start(bf16[4,4,64,256]{3,2,1,0:T(8,128)(2,1)S(1)} %bitcast.14), channel_id=1, source_target_pairs={{0,16},{8,24},{16,0},{24,8},{1,17},{9,25},{17,1},{25,9},{2,18},{10... | collective-permute-start | bytes 1572872 | tf_op jit(solution)/shard_map/ppermute | solution.py:28
  53.6 19.2 %collective-permute-start.2 = (bf16[4,4,64,256]{3,2,1,0:T(8,128)(2,1)S(1)}, bf16[4,4,64,256]{3,2,1,0:T(8,128)(2,1)S(1)}, u32[]{:S(2)}, u32[]{:S(2)}) collective-permute-start(bf16[4,4,64,256]{3,2,1,0:T(8,128)(2,1)S(1)} %bitcast.15), channel_id=1, source_target_pairs={{0,24},{8,0},{16,8},{24,16},{1,25},{9,1},{17,9},{25,17},{2,26},{10... | collective-permute-start | bytes 1572872 | tf_op jit(solution)/shard_map/ppermute | solution.py:28
  79.2 18.2 %collective-permute-start.6 = (s32[16]{0:T(128)S(1)}, s32[16]{0:T(128)S(1)}, u32[]{:S(2)}, u32[]{:S(2)}) collective-permute-start(s32[16]{0:T(128)S(1)} %copy-done.1), channel_id=1, source_target_pairs={{0,8},{8,16},{16,24},{24,0},{1,9},{9,17},{17,25},{25,1},{2,10},{10... | collective-permute-start | bytes 200 | tf_op jit(solution)/shard_map/ppermute | solution.py:28
  85.5 12.0 %collective-permute-start.7 = (s32[16]{0:T(128)S(1)}, s32[16]{0:T(128)S(1)}, u32[]{:S(2)}, u32[]{:S(2)}) collective-permute-start(s32[16]{0:T(128)S(1)} %copy-done.1), channel_id=1, source_target_pairs={{0,24},{8,0},{16,8},{24,16},{1,25},{9,1},{17,9},{25,17},{2,26},{10... | collective-permute-start | bytes 200 | tf_op jit(solution)/shard_map/ppermute | solution.py:28
  87.5 12.4 %collective-permute-start.3 = (bf16[4,4,64,256]{3,2,1,0:T(8,128)(2,1)S(1)}, bf16[4,4,64,256]{3,2,1,0:T(8,128)(2,1)S(1)}, u32[]{:S(2)}, u32[]{:S(2)}) collective-permute-start(bf16[4,4,64,256]{3,2,1,0:T(8,128)(2,1)S(1)} %bitcast.9), channel_id=1, source_target_pairs={{0,8},{8,16},{16,24},{24,0},{1,9},{9,17},{17,25},{25,1},{2,10},{10... | collective-permute-start | bytes 1572872 | tf_op jit(solution)/shard_map/ppermute | solution.py:28
  90.8 19.7 %collective-permute-start.4 = (bf16[4,4,64,256]{3,2,1,0:T(8,128)(2,1)S(1)}, bf16[4,4,64,256]{3,2,1,0:T(8,128)(2,1)S(1)}, u32[]{:S(2)}, u32[]{:S(2)}) collective-permute-start(bf16[4,4,64,256]{3,2,1,0:T(8,128)(2,1)S(1)} %bitcast.10), channel_id=1, source_target_pairs={{0,16},{8,24},{16,0},{24,8},{1,17},{9,25},{17,1},{25,9},{2,18},{10... | collective-permute-start | bytes 1572872 | tf_op jit(solution)/shard_map/ppermute | solution.py:28
  93.1 23.6 %collective-permute-start.5 = (bf16[4,4,64,256]{3,2,1,0:T(8,128)(2,1)S(1)}, bf16[4,4,64,256]{3,2,1,0:T(8,128)(2,1)S(1)}, u32[]{:S(2)}, u32[]{:S(2)}) collective-permute-start(bf16[4,4,64,256]{3,2,1,0:T(8,128)(2,1)S(1)} %bitcast.11), channel_id=1, source_target_pairs={{0,24},{8,0},{16,8},{24,16},{1,25},{9,1},{17,9},{25,17},{2,26},{10... | collective-permute-start | bytes 1572872 | tf_op jit(solution)/shard_map/ppermute | solution.py:28
  121.1 16.6 %collective-permute-start.10 = (bf16[1024,256]{1,0:T(8,128)(2,1)S(1)}, bf16[1024,256]{1,0:T(8,128)(2,1)S(1)}, u32[]{:S(2)}, u32[]{:S(2)}) collective-permute-start(bf16[1024,256]{1,0:T(8,128)(2,1)S(1)} %project.3.query), channel_id=1, source_target_pairs={{0,24},{8,0},{16,8},{24,16},{1,25},{9,1},{17,9},{25,17},{2,26},{10... | collective-permute-start | bytes 1572872 | tf_op jit(solution)/shard_map/ppermute | solution.py:28
  126.6 16.7 %collective-permute-start.8 = (bf16[1024,256]{1,0:T(8,128)(2,1)S(1)}, bf16[1024,256]{1,0:T(8,128)(2,1)S(1)}, u32[]{:S(2)}, u32[]{:S(2)}) collective-permute-start(bf16[1024,256]{1,0:T(8,128)(2,1)S(1)} %project.3.query), channel_id=1, source_target_pairs={{0,8},{8,16},{16,24},{24,0},{1,9},{9,17},{17,25},{25,1},{2,10},{10... | collective-permute-start | bytes 1572872 | tf_op jit(solution)/shard_map/ppermute | solution.py:28
  128.5 23.6 %collective-permute-start.9 = (bf16[1024,256]{1,0:T(8,128)(2,1)S(1)}, bf16[1024,256]{1,0:T(8,128)(2,1)S(1)}, u32[]{:S(2)}, u32[]{:S(2)}) collective-permute-start(bf16[1024,256]{1,0:T(8,128)(2,1)S(1)} %project.3.query), channel_id=1, source_target_pairs={{0,16},{8,24},{16,0},{24,8},{1,17},{9,25},{17,1},{25,9},{2,18},{10... | collective-permute-start | bytes 1572872 | tf_op jit(solution)/shard_map/ppermute | solution.py:28
  188.0 24.9 %collective-permute-start.13 = (bf16[1088,256]{1,0:T(8,128)(2,1)S(1)}, bf16[1088,256]{1,0:T(8,128)(2,1)S(1)}, u32[]{:S(2)}, u32[]{:S(2)}) collective-permute-start(bf16[1088,256]{1,0:T(8,128)(2,1)S(1)} %partial_attention.9), channel_id=1, source_target_pairs={{0,16},{8,24},{16,0},{24,8},{1,17},{9,25},{17,1},{25,9},{2,18},{10... | collective-permute-start | bytes 1671176 | tf_op jit(solution)/shard_map/ppermute | solution.py:28
  197.6 20.4 %collective-permute-start.12 = (bf16[1088,256]{1,0:T(8,128)(2,1)}, bf16[1088,256]{1,0:T(8,128)(2,1)S(1)}, u32[]{:S(2)}, u32[]{:S(2)}) collective-permute-start(bf16[1088,256]{1,0:T(8,128)(2,1)} %partial_attention.8), channel_id=1, source_target_pairs={{0,24},{8,0},{16,8},{24,16},{1,25},{9,1},{17,9},{25,17},{2,26},{10... | collective-permute-start | bytes 1671176 | tf_op jit(solution)/shard_map/ppermute | solution.py:28
  206.9 16.3 %collective-permute-start.11 = (bf16[1088,256]{1,0:T(8,128)(2,1)}, bf16[1088,256]{1,0:T(8,128)(2,1)}, u32[]{:S(2)}, u32[]{:S(2)}) collective-permute-start(bf16[1088,256]{1,0:T(8,128)(2,1)} %partial_attention.7), channel_id=1, source_target_pairs={{0,8},{8,16},{16,24},{24,0},{1,9},{9,17},{17,25},{25,1},{2,10},{10... | collective-permute-start | bytes 1671176 | tf_op jit(solution)/shard_map/ppermute | solution.py:28
Sparse Core Ops, SparseCore 0:
  9.5 63.1 all-gather.2
  78.2 105.7 all-gather.4

commit v6 on v5

--- a/solution.py
+++ b/solution.py
@@ -16,6 +16,7 @@
 RUN_BLOCKS = 16
 PAD = 64
 ROW_TILE = 256
+ORDER = (0, 2, 1, 3)
 LOG2E = 1.4426950408889634
 MASKED = -1e30
 F32 = jnp.float32
@@ -37,7 +38,7 @@
 
     for t in range(count // ROW_TILE):
         copy(t).start()
-    for s, part in enumerate((part0, part1, part2, part3)):
+    for s, part in zip(ORDER, (part0, part1, part2, part3)):
         owner = lax.rem(place[0] + 4 - s, 4)
         for za in range(4):
             for zb in range(4):
@@ -293,17 +294,16 @@
 
     rows = lax.all_gather(tokens, ("y", "c"), axis=0, tiled=True)
 
-    both = jnp.concatenate([kv_weight, query_weight], axis=1)
-    both = lax.all_gather(both, "a", axis=0, tiled=True)
-    kv_own = lax.all_gather(both[:, :width], "b", axis=0, tiled=True)
-    query_own_in, kv_own = lax.optimization_barrier((both[:, width:], kv_own))
+    kv_own = lax.all_gather(kv_weight, "a", axis=0, tiled=True)
+    kv_own = lax.all_gather(kv_own, "b", axis=0, tiled=True)
+    query_weight, kv_own = lax.optimization_barrier((query_weight, kv_own))
 
     def spread(own):
         own = own.reshape(4, 4, 64, width)
-        return [own] + [shift(own, "x", s) for s in (1, 2, 3)]
+        return [shift(own, "x", s) if s else own for s in ORDER]
 
     kv_parts = spread(kv_own)
-    query_own = lax.all_gather(query_own_in, "b", axis=0, tiled=True)
+    query_own = lax.all_gather(query_weight, "a", axis=0, tiled=True)
     kv_parts, query_own = lax.optimization_barrier((kv_parts, query_own))
 
     place_1 = place.reshape(1)
@@ -311,6 +311,7 @@
     held = lax.all_gather(kv_rows, ("a", "b"), axis=0, tiled=True)
     held = held.reshape(-1, BS, 2 * HD)
     query_own, reach, kv_rows = lax.optimization_barrier((query_own, reach, kv_rows))
+    query_own = lax.all_gather(query_own, "b", axis=0, tiled=True)
     query_rows = project(place_1, rows, spread(query_own))
     queries = [query_rows] + [shift(query_rows, "x", s) for s in (1, 2, 3)]
 

time: 236 us -> 236 us (level)
  waiting for transfers between devices: 79.7 us -> 63.1 us
  blocking collectives: 50.7 us -> 66.5 us
    ppermute x14, waiting for transfers between devices: 47.1 us -> 23.2 us  [shift(): lax.ppermute(value, axis, [(i, (i + by) % size) for i in range(size)])]
    all_gather x3 -> x4, blocking collectives: 50.7 us -> 66.5 us  [the longest x1 24.1 us: per_device(): kv_own = lax.all_gather(kv_weight, 'a', axis=0, tiled=True)]
    all_gather x1, waiting for transfers between devices: 31.9 us -> 37.5 us  [per_device(): held = lax.all_gather(kv_rows, ('a', 'b'), axis=0, tiled=True)]
  transfers between devices with their start and end apart: 16 -> 16, of which waited for: 9 -> 7; matrix products, arithmetic and copies ran while one was open for 1% -> 1% of each run, Pallas kernels for 10% -> 10%
where the time goes in v6:
time: 236 us; the launch traced here: 234 us
  blocking collectives  66.5 us (28%)
  waiting for transfers between devices  63.1 us (27%)
  starting transfers between devices  51.8 us (22%)
  Pallas kernels  36.1 us (15%)
  between operations  13.7 us (6%)
    ppermute x14, starting transfers between devices, shift(): lax.ppermute(value, axis, [(i, (i + by) % size) for i in range(size)])  51.7 us
    all_gather x1, waiting for transfers between devices, per_device(): held = lax.all_gather(kv_rows, ('a', 'b'), axis=0, tiled=True)  37.5 us
    all_gather x1, blocking collectives, per_device(): kv_own = lax.all_gather(kv_weight, 'a', axis=0, tiled=True)  24.1 us
    ppermute x14, waiting for transfers between devices, shift(): lax.ppermute(value, axis, [(i, (i + by) % size) for i in range(size)])  23.2 us
    pallas_call x5, Pallas kernels, partial_attention(): pl.pallas_call(partial_kernel, in_specs=[smem] * 3 + [vmem, pl.BlockSpec(...  22.9 us
    all_gather x1, blocking collectives, per_device(): query_own = lax.all_gather(query_weight, 'a', axis=0, tiled=True)  15.7 us
    all_gather x1, blocking collectives, per_device(): query_own = lax.all_gather(query_own, 'b', axis=0, tiled=True)  14 us
    all_gather x1, blocking collectives, per_device(): kv_own = lax.all_gather(kv_own, 'b', axis=0, tiled=True)  12.7 us
  transfers between devices with their start and end apart: 16, of which 7 were waited for; matrix products, arithmetic and copies ran while one was open for 1% of the time, Pallas kernels for 10%

profile of v6, /device:TPU:1, one launch (start us, length us, event | category | flops | bytes accessed | tf_op | source)
XLA Modules:
  0.0 234.2 jit_solution(13302489085621131916)
XLA Ops:
  7.3 24.1 %all_gather.19 = bf16[256,256]{1,0:T(8,128)(2,1)S(1)} all-gather(bf16[64,256]{1,0:T(8,128)(2,1)} %param.9), channel_id=1, replica_groups=mesh['a'=4,'b'=4,'x'=4,'y'=4,'c'=2] {'a'}, dimensions={0}, use_global_device_ids=true | all-gather | bytes 163840 | tf_op jit(solution)/shard_map/all_gather | solution.py:297
  31.4 12.7 %all_gather.20 = bf16[1024,256]{1,0:T(8,128)(2,1)S(1)} all-gather(bf16[256,256]{1,0:T(8,128)(2,1)S(1)} %all_gather.19), channel_id=1, replica_groups=mesh['a'=4,'b'=4,'x'=4,'y'=4,'c'=2] {'b'}, dimensions={0}, use_global_device_ids=true | all-gather | bytes 655360 | tf_op jit(solution)/shard_map/all_gather | solution.py:298
  44.1 4.6 %collective-permute-start = (bf16[4,4,64,256]{3,2,1,0:T(8,128)(2,1)S(1)}, bf16[4,4,64,256]{3,2,1,0:T(8,128)(2,1)S(1)}, u32[]{:S(2)}, u32[]{:S(2)}) collective-permute-start(bf16[4,4,64,256]{3,2,1,0:T(8,128)(2,1)S(1)} %bitcast.13), channel_id=1, source_target_pairs={{0,16},{8,24},{16,0},{24,8},{1,17},{9,25},{17,1},{25,9},{2,18},{10... | collective-permute-start | bytes 1572872 | tf_op jit(solution)/shard_map/ppermute | solution.py:29
  48.8 2.2 collective-permute-start.1
  51.0 4.3 %collective-permute-start.2 = (bf16[4,4,64,256]{3,2,1,0:T(8,128)(2,1)S(1)}, bf16[4,4,64,256]{3,2,1,0:T(8,128)(2,1)S(1)}, u32[]{:S(2)}, u32[]{:S(2)}) collective-permute-start(bf16[4,4,64,256]{3,2,1,0:T(8,128)(2,1)S(1)} %bitcast.15), channel_id=1, source_target_pairs={{0,24},{8,0},{16,8},{24,16},{1,25},{9,1},{17,9},{25,17},{2,26},{10... | collective-permute-start | bytes 1572872 | tf_op jit(solution)/shard_map/ppermute | solution.py:29
  55.3 15.7 %all_gather.21 = bf16[256,256]{1,0:T(8,128)(2,1)S(1)} all-gather(bf16[64,256]{1,0:T(8,128)(2,1)} %param.8), channel_id=1, replica_groups=mesh['a'=4,'b'=4,'x'=4,'y'=4,'c'=2] {'a'}, dimensions={0}, use_global_device_ids=true | all-gather | bytes 163840 | tf_op jit(solution)/shard_map/all_gather | solution.py:306
  71.0 1.7 all-gather.3.cloned.1.call-done.rows
  72.7 5.3 %project.2 = bf16[1024,256]{1,0:T(8,128)(2,1)} custom-call(s32[1]{0:T(128)} %bitcast.1.place, bf16[1024,4096]{1,0:T(8,128)(2,1)} %all-gather.3.cloned.1.call-done.rows, bf16[4,4,64,256]{3,2,1,0:T(8,128)(2,1)S(1)} %bitcast.16, bf16[4,4,64,256]{3,2,1,0:T(8,128)(2,1)S(1)} %collective-permute-done.part1, ...), custom_call_target="tpu_custom_call" | custom-call | flops 2147483648 | bytes 11010048 | tf_op jit(solution)/shard_map/project/pallas_call | solution.py:63
  79.1 3.1 %collective-permute-start.6 = (s32[16]{0:T(128)S(1)}, s32[16]{0:T(128)S(1)}, u32[]{:S(2)}, u32[]{:S(2)}) collective-permute-start(s32[16]{0:T(128)S(1)} %copy-done.3), channel_id=1, source_target_pairs={{0,8},{8,16},{16,24},{24,0},{1,9},{9,17},{17,25},{25,1},{2,10},{10... | collective-permute-start | bytes 200 | tf_op jit(solution)/shard_map/ppermute | solution.py:29
  82.2 3.4 %collective-permute-start.7 = (s32[16]{0:T(128)S(1)}, s32[16]{0:T(128)S(1)}, u32[]{:S(2)}, u32[]{:S(2)}) collective-permute-start(s32[16]{0:T(128)S(1)} %copy-done.3), channel_id=1, source_target_pairs={{0,24},{8,0},{16,8},{24,16},{1,25},{9,1},{17,9},{25,17},{2,26},{10... | collective-permute-start | bytes 200 | tf_op jit(solution)/shard_map/ppermute | solution.py:29
  85.6 14.0 %all_gather.23 = bf16[1024,256]{1,0:T(8,128)(2,1)S(1)} all-gather(bf16[256,256]{1,0:T(8,128)(2,1)S(1)} %all_gather.21), channel_id=1, replica_groups=mesh['a'=4,'b'=4,'x'=4,'y'=4,'c'=2] {'b'}, dimensions={0}, use_global_device_ids=true | all-gather | bytes 655360 | tf_op jit(solution)/shard_map/all_gather | solution.py:314
  99.6 3.5 %collective-permute-start.3 = (bf16[4,4,64,256]{3,2,1,0:T(8,128)(2,1)S(1)}, bf16[4,4,64,256]{3,2,1,0:T(8,128)(2,1)S(1)}, u32[]{:S(2)}, u32[]{:S(2)}) collective-permute-start(bf16[4,4,64,256]{3,2,1,0:T(8,128)(2,1)S(1)} %bitcast.9), channel_id=1, source_target_pairs={{0,16},{8,24},{16,0},{24,8},{1,17},{9,25},{17,1},{25,9},{2,18},{10... | collective-permute-start | bytes 1572872 | tf_op jit(solution)/shard_map/ppermute | solution.py:29
  103.2 2.3 collective-permute-start.4
  105.5 4.2 %collective-permute-start.5 = (bf16[4,4,64,256]{3,2,1,0:T(8,128)(2,1)S(1)}, bf16[4,4,64,256]{3,2,1,0:T(8,128)(2,1)S(1)}, u32[]{:S(2)}, u32[]{:S(2)}) collective-permute-start(bf16[4,4,64,256]{3,2,1,0:T(8,128)(2,1)S(1)} %bitcast.11), channel_id=1, source_target_pairs={{0,24},{8,0},{16,8},{24,16},{1,25},{9,1},{17,9},{25,17},{2,26},{10... | collective-permute-start | bytes 1572872 | tf_op jit(solution)/shard_map/ppermute | solution.py:29
  111.2 5.6 %collective-permute-done.4.part2 = bf16[4,4,64,256]{3,2,1,0:T(8,128)(2,1)S(1)} collective-permute-done((bf16[4,4,64,256]{3,2,1,0:T(8,128)(2,1)S(1)}, bf16[4,4,64,256]{3,2,1,0:T(8,128)(2,1)S(1)}, u32[]{:S(2)}, u32[]{:S(2)}) %collective-permute-start.4) | collective-permute-done | bytes 524320 | tf_op jit(solution)/shard_map/ppermute | solution.py:29
  116.8 4.5 %project.3.query = bf16[1024,256]{1,0:T(8,128)(2,1)S(1)} custom-call(s32[1]{0:T(128)} %bitcast.1.place, bf16[1024,4096]{1,0:T(8,128)(2,1)} %all-gather.3.cloned.1.call-done.rows, bf16[4,4,64,256]{3,2,1,0:T(8,128)(2,1)S(1)} %bitcast.12, bf16[4,4,64,256]{3,2,1,0:T(8,128)(2,1)S(1)} %collective-permute-done.3.part1, ...), custom_call_target="tpu_custom_call" | custom-call | flops 2147483648 | bytes 11010048 | tf_op jit(solution)/shard_map/project/pallas_call | solution.py:63
  121.3 9.8 %collective-permute-start.10 = (bf16[1024,256]{1,0:T(8,128)(2,1)S(1)}, bf16[1024,256]{1,0:T(8,128)(2,1)S(1)}, u32[]{:S(2)}, u32[]{:S(2)}) collective-permute-start(bf16[1024,256]{1,0:T(8,128)(2,1)S(1)} %project.3.query), channel_id=1, source_target_pairs={{0,24},{8,0},{16,8},{24,16},{1,25},{9,1},{17,9},{25,17},{2,26},{10... | collective-permute-start | bytes 1572872 | tf_op jit(solution)/shard_map/ppermute | solution.py:29
  131.1 1.9 collective-permute-start.8
  133.1 3.1 %collective-permute-start.9 = (bf16[1024,256]{1,0:T(8,128)(2,1)S(1)}, bf16[1024,256]{1,0:T(8,128)(2,1)S(1)}, u32[]{:S(2)}, u32[]{:S(2)}) collective-permute-start(bf16[1024,256]{1,0:T(8,128)(2,1)S(1)} %project.3.query), channel_id=1, source_target_pairs={{0,16},{8,24},{16,0},{24,8},{1,17},{9,25},{17,1},{25,9},{2,18},{10... | collective-permute-start | bytes 1572872 | tf_op jit(solution)/shard_map/ppermute | solution.py:29
  136.6 5.8 %partial_attention.5.refs_4_ = bf16[1088,256]{1,0:T(8,128)(2,1)S(1)} custom-call(s32[1]{0:T(128)} %constant.107.clone.1.from_x, s32[128]{0:T(128)S(1)} %reshape.358.index, s32[16]{0:T(128)S(1)} %get-tuple-element.45.counts, bf16[1024,256]{1,0:T(8,128)(2,1)S(1)} %project.3.query, bf16[16,64,256]{2,1,0:T(8,128)(2,1)} %bitcast.5.held), custom_call_target="tpu_custom_call" | custom-call | flops 2000000000 | bytes 65536 | tf_op jit(solution)/shard_map/partial_attention/pallas_call | solution.py:181
  143.2 6.4 %collective-permute-done.8.query = bf16[1024,256]{1,0:T(8,128)(2,1)S(1)} collective-permute-done((bf16[1024,256]{1,0:T(8,128)(2,1)S(1)}, bf16[1024,256]{1,0:T(8,128)(2,1)S(1)}, u32[]{:S(2)}, u32[]{:S(2)}) %collective-permute-start.8) | collective-permute-done | bytes 524320 | tf_op jit(solution)/shard_map/ppermute | solution.py:29
  149.6 37.5 %all-gather.5.cloned.1.call-done = bf16[16384,256]{1,0:T(8,128)(2,1)} async-done(((bf16[1024,256]{1,0:T(8,128)(2,1)}), bf16[16384,256]{1,0:T(8,128)(2,1)}) %all-gather.5.cloned.1.call-update) | async-done | bytes 8388624 | tf_op jit(solution)/shard_map/all_gather | solution.py:311
  187.1 4.1 %partial_attention.9 = bf16[1088,256]{1,0:T(8,128)(2,1)S(1)} custom-call(s32[1]{0:T(128)} %bitcast.8.from_x, s32[512]{0:T(512)S(1)} %reshape.361.index, s32[64]{0:T(128)S(1)} %get-tuple-element.34.counts, bf16[1024,256]{1,0:T(8,128)(2,1)S(1)} %collective-permute-done.9.query, bf16[256,64,256]{2,1,0:T(8,128)(2,1)} %bitcast.17), custom_call_target="tpu_custom_call" | custom-call | flops 2000000000 | bytes 65536 | tf_op jit(solution)/shard_map/partial_attention/pallas_call | solution.py:181
  191.3 3.1 %collective-permute-start.13 = (bf16[1088,256]{1,0:T(8,128)(2,1)S(1)}, bf16[1088,256]{1,0:T(8,128)(2,1)S(1)}, u32[]{:S(2)}, u32[]{:S(2)}) collective-permute-start(bf16[1088,256]{1,0:T(8,128)(2,1)S(1)} %partial_attention.9), channel_id=1, source_target_pairs={{0,16},{8,24},{16,0},{24,8},{1,17},{9,25},{17,1},{25,9},{2,18},{10... | collective-permute-start | bytes 1671176 | tf_op jit(solution)/shard_map/ppermute | solution.py:29
  194.3 4.0 %partial_attention.8 = bf16[1088,256]{1,0:T(8,128)(2,1)S(1)} custom-call(s32[1]{0:T(128)} %bitcast.7.from_x, s32[512]{0:T(512)S(1)} %reshape.361.index, s32[64]{0:T(128)S(1)} %get-tuple-element.34.counts, bf16[1024,256]{1,0:T(8,128)(2,1)S(1)} %collective-permute-done.8.query, bf16[256,64,256]{2,1,0:T(8,128)(2,1)} %bitcast.18), custom_call_target="tpu_custom_call" | custom-call | flops 2000000000 | bytes 65536 | tf_op jit(solution)/shard_map/partial_attention/pallas_call | solution.py:181
  198.4 4.3 %collective-permute-start.12 = (bf16[1088,256]{1,0:T(8,128)(2,1)S(1)}, bf16[1088,256]{1,0:T(8,128)(2,1)S(1)}, u32[]{:S(2)}, u32[]{:S(2)}) collective-permute-start(bf16[1088,256]{1,0:T(8,128)(2,1)S(1)} %partial_attention.8), channel_id=1, source_target_pairs={{0,24},{8,0},{16,8},{24,16},{1,25},{9,1},{17,9},{25,17},{2,26},{10... | collective-permute-start | bytes 1671176 | tf_op jit(solution)/shard_map/ppermute | solution.py:29
  202.6 5.0 %partial_attention.7 = bf16[1088,256]{1,0:T(8,128)(2,1)} custom-call(s32[1]{0:T(128)} %bitcast.6.from_x, s32[512]{0:T(512)S(1)} %reshape.361.index, s32[64]{0:T(128)S(1)} %get-tuple-element.34.counts, bf16[1024,256]{1,0:T(8,128)(2,1)S(1)} %copy-done.1, bf16[256,64,256]{2,1,0:T(8,128)(2,1)} %bitcast.19), custom_call_target="tpu_custom_call" | custom-call | flops 2000000000 | bytes 65536 | tf_op jit(solution)/shard_map/partial_attention/pallas_call | solution.py:181
  207.6 1.9 collective-permute-start.11
  209.6 4.0 %partial_attention.6.refs_0_ = bf16[1088,256]{1,0:T(8,128)(2,1)S(1)} custom-call(s32[1]{0:T(128)} %bitcast.from_x, s32[512]{0:T(512)S(1)} %reshape.361.index, s32[64]{0:T(128)S(1)} %get-tuple-element.34.counts, bf16[1024,256]{1,0:T(8,128)(2,1)S(1)} %project.3.query, bf16[256,64,256]{2,1,0:T(8,128)(2,1)} %bitcast.20), custom_call_target="tpu_custom_call" | custom-call | flops 2000000000 | bytes 65536 | tf_op jit(solution)/shard_map/partial_attention/pallas_call | solution.py:181
  213.6 5.9 %collective-permute-done.12.refs_2_ = bf16[1088,256]{1,0:T(8,128)(2,1)S(1)} collective-permute-done((bf16[1088,256]{1,0:T(8,128)(2,1)S(1)}, bf16[1088,256]{1,0:T(8,128)(2,1)S(1)}, u32[]{:S(2)}, u32[]{:S(2)}) %collective-permute-start.12) | collective-permute-done | bytes 557088 | tf_op jit(solution)/shard_map/ppermute | solution.py:29
  219.6 4.3 %collective-permute-done.11.refs_1_ = bf16[1088,256]{1,0:T(8,128)(2,1)} collective-permute-done((bf16[1088,256]{1,0:T(8,128)(2,1)}, bf16[1088,256]{1,0:T(8,128)(2,1)}, u32[]{:S(2)}, u32[]{:S(2)}) %collective-permute-start.11) | collective-permute-done | bytes 557088 | tf_op jit(solution)/shard_map/ppermute | solution.py:29
  223.9 3.5 %combine.1 = bf16[1024,256]{1,0:T(8,128)(2,1)} custom-call(bf16[1088,256]{1,0:T(8,128)(2,1)S(1)} %partial_attention.6.refs_0_, bf16[1088,256]{1,0:T(8,128)(2,1)} %collective-permute-done.11.refs_1_, bf16[1088,256]{1,0:T(8,128)(2,1)S(1)} %collective-permute-done.12.refs_2_, bf16[1088,256]{1,0:T(8,128)(2,1)S(1)} %collective-permute-done.13.refs_3_, ...), custom_call_target="tpu_custom_call" | custom-call | tf_op jit(solution)/shard_map/combine/pallas_call | solution.py:231
  (51 shorter events, 4.6 us)
Async XLA Ops:
  6.5 72.5 %copy-start.2 = (s32[4]{0:T(128)S(1)}, s32[4]{0:T(128)}, u32[]{:S(2)}) copy-start(s32[4]{0:T(128)} %constant.120.clone) | copy-start | bytes 52
  6.5 103.7 %copy-start.4 = (s32[4]{0:T(128)S(1)}, s32[4]{0:T(128)}, u32[]{:S(2)}) copy-start(s32[4]{0:T(128)} %constant.123) | copy-start | bytes 52
  6.5 71.5 %copy-start.5 = (s32[2]{0:T(128)S(1)}, s32[2]{0:T(128)}, u32[]{:S(2)}) copy-start(s32[2]{0:T(128)} %param.11) | copy-start | bytes 28
  6.5 72.6 %copy-start.3 = (s32[16]{0:T(128)S(1)}, s32[16]{0:T(128)}, u32[]{:S(2)}) copy-start(s32[16]{0:T(128)} %param.10) | copy-start | bytes 196
  6.5 66.2 %all-gather.3.cloned.1.call-start = ((), (), s32[]{:S(2)}) async-start(), calls=%async_computation | async-start | bytes 9437184 | tf_op jit(solution)/shard_map/all_gather | solution.py:295
  7.3 179.9 %all-gather.5.cloned.1.call-start = ((), (), s32[]{:S(2)}) async-start(), calls=%async_computation.1 | async-start | bytes 8912896 | tf_op jit(solution)/shard_map/all_gather | solution.py:311
  44.1 26.9 %collective-permute-start = (bf16[4,4,64,256]{3,2,1,0:T(8,128)(2,1)S(1)}, bf16[4,4,64,256]{3,2,1,0:T(8,128)(2,1)S(1)}, u32[]{:S(2)}, u32[]{:S(2)}) collective-permute-start(bf16[4,4,64,256]{3,2,1,0:T(8,128)(2,1)S(1)} %bitcast.13), channel_id=1, source_target_pairs={{0,16},{8,24},{16,0},{24,8},{1,17},{9,25},{17,1},{25,9},{2,18},{10... | collective-permute-start | bytes 1572872 | tf_op jit(solution)/shard_map/ppermute | solution.py:29
  48.8 22.2 %collective-permute-start.1 = (bf16[4,4,64,256]{3,2,1,0:T(8,128)(2,1)S(1)}, bf16[4,4,64,256]{3,2,1,0:T(8,128)(2,1)S(1)}, u32[]{:S(2)}, u32[]{:S(2)}) collective-permute-start(bf16[4,4,64,256]{3,2,1,0:T(8,128)(2,1)S(1)} %bitcast.14), channel_id=1, source_target_pairs={{0,8},{8,16},{16,24},{24,0},{1,9},{9,17},{17,25},{25,1},{2,10},{10... | collective-permute-start | bytes 1572872 | tf_op jit(solution)/shard_map/ppermute | solution.py:29
  51.0 20.0 %collective-permute-start.2 = (bf16[4,4,64,256]{3,2,1,0:T(8,128)(2,1)S(1)}, bf16[4,4,64,256]{3,2,1,0:T(8,128)(2,1)S(1)}, u32[]{:S(2)}, u32[]{:S(2)}) collective-permute-start(bf16[4,4,64,256]{3,2,1,0:T(8,128)(2,1)S(1)} %bitcast.15), channel_id=1, source_target_pairs={{0,24},{8,0},{16,8},{24,16},{1,25},{9,1},{17,9},{25,17},{2,26},{10... | collective-permute-start | bytes 1572872 | tf_op jit(solution)/shard_map/ppermute | solution.py:29
  79.1 30.9 %collective-permute-start.6 = (s32[16]{0:T(128)S(1)}, s32[16]{0:T(128)S(1)}, u32[]{:S(2)}, u32[]{:S(2)}) collective-permute-start(s32[16]{0:T(128)S(1)} %copy-done.3), channel_id=1, source_target_pairs={{0,8},{8,16},{16,24},{24,0},{1,9},{9,17},{17,25},{25,1},{2,10},{10... | collective-permute-start | bytes 200 | tf_op jit(solution)/shard_map/ppermute | solution.py:29
  82.2 27.9 %collective-permute-start.7 = (s32[16]{0:T(128)S(1)}, s32[16]{0:T(128)S(1)}, u32[]{:S(2)}, u32[]{:S(2)}) collective-permute-start(s32[16]{0:T(128)S(1)} %copy-done.3), channel_id=1, source_target_pairs={{0,24},{8,0},{16,8},{24,16},{1,25},{9,1},{17,9},{25,17},{2,26},{10... | collective-permute-start | bytes 200 | tf_op jit(solution)/shard_map/ppermute | solution.py:29
  99.6 11.6 %collective-permute-start.3 = (bf16[4,4,64,256]{3,2,1,0:T(8,128)(2,1)S(1)}, bf16[4,4,64,256]{3,2,1,0:T(8,128)(2,1)S(1)}, u32[]{:S(2)}, u32[]{:S(2)}) collective-permute-start(bf16[4,4,64,256]{3,2,1,0:T(8,128)(2,1)S(1)} %bitcast.9), channel_id=1, source_target_pairs={{0,16},{8,24},{16,0},{24,8},{1,17},{9,25},{17,1},{25,9},{2,18},{10... | collective-permute-start | bytes 1572872 | tf_op jit(solution)/shard_map/ppermute | solution.py:29
  103.2 13.6 %collective-permute-start.4 = (bf16[4,4,64,256]{3,2,1,0:T(8,128)(2,1)S(1)}, bf16[4,4,64,256]{3,2,1,0:T(8,128)(2,1)S(1)}, u32[]{:S(2)}, u32[]{:S(2)}) collective-permute-start(bf16[4,4,64,256]{3,2,1,0:T(8,128)(2,1)S(1)} %bitcast.10), channel_id=1, source_target_pairs={{0,8},{8,16},{16,24},{24,0},{1,9},{9,17},{17,25},{25,1},{2,10},{10... | collective-permute-start | bytes 1572872 | tf_op jit(solution)/shard_map/ppermute | solution.py:29
  105.5 11.3 %collective-permute-start.5 = (bf16[4,4,64,256]{3,2,1,0:T(8,128)(2,1)S(1)}, bf16[4,4,64,256]{3,2,1,0:T(8,128)(2,1)S(1)}, u32[]{:S(2)}, u32[]{:S(2)}) collective-permute-start(bf16[4,4,64,256]{3,2,1,0:T(8,128)(2,1)S(1)} %bitcast.11), channel_id=1, source_target_pairs={{0,24},{8,0},{16,8},{24,16},{1,25},{9,1},{17,9},{25,17},{2,26},{10... | collective-permute-start | bytes 1572872 | tf_op jit(solution)/shard_map/ppermute | solution.py:29
  121.3 21.0 %collective-permute-start.10 = (bf16[1024,256]{1,0:T(8,128)(2,1)S(1)}, bf16[1024,256]{1,0:T(8,128)(2,1)S(1)}, u32[]{:S(2)}, u32[]{:S(2)}) collective-permute-start(bf16[1024,256]{1,0:T(8,128)(2,1)S(1)} %project.3.query), channel_id=1, source_target_pairs={{0,24},{8,0},{16,8},{24,16},{1,25},{9,1},{17,9},{25,17},{2,26},{10... | collective-permute-start | bytes 1572872 | tf_op jit(solution)/shard_map/ppermute | solution.py:29
  131.1 18.5 %collective-permute-start.8 = (bf16[1024,256]{1,0:T(8,128)(2,1)S(1)}, bf16[1024,256]{1,0:T(8,128)(2,1)S(1)}, u32[]{:S(2)}, u32[]{:S(2)}) collective-permute-start(bf16[1024,256]{1,0:T(8,128)(2,1)S(1)} %project.3.query), channel_id=1, source_target_pairs={{0,8},{8,16},{16,24},{24,0},{1,9},{9,17},{17,25},{25,1},{2,10},{10... | collective-permute-start | bytes 1572872 | tf_op jit(solution)/shard_map/ppermute | solution.py:29
  133.1 16.5 %collective-permute-start.9 = (bf16[1024,256]{1,0:T(8,128)(2,1)S(1)}, bf16[1024,256]{1,0:T(8,128)(2,1)S(1)}, u32[]{:S(2)}, u32[]{:S(2)}) collective-permute-start(bf16[1024,256]{1,0:T(8,128)(2,1)S(1)} %project.3.query), channel_id=1, source_target_pairs={{0,16},{8,24},{16,0},{24,8},{1,17},{9,25},{17,1},{25,9},{2,18},{10... | collective-permute-start | bytes 1572872 | tf_op jit(solution)/shard_map/ppermute | solution.py:29
  142.4 0.8 copy-start
  187.1 15.5 %copy-start.1 = (bf16[1024,256]{1,0:T(8,128)(2,1)S(1)}, bf16[1024,256]{1,0:T(8,128)(2,1)}, u32[]{:S(2)}) copy-start(bf16[1024,256]{1,0:T(8,128)(2,1)} %copy-done) | copy-start | bytes 1572868
  191.3 22.3 %collective-permute-start.13 = (bf16[1088,256]{1,0:T(8,128)(2,1)S(1)}, bf16[1088,256]{1,0:T(8,128)(2,1)S(1)}, u32[]{:S(2)}, u32[]{:S(2)}) collective-permute-start(bf16[1088,256]{1,0:T(8,128)(2,1)S(1)} %partial_attention.9), channel_id=1, source_target_pairs={{0,16},{8,24},{16,0},{24,8},{1,17},{9,25},{17,1},{25,9},{2,18},{10... | collective-permute-start | bytes 1671176 | tf_op jit(solution)/shard_map/ppermute | solution.py:29
  198.4 21.2 %collective-permute-start.12 = (bf16[1088,256]{1,0:T(8,128)(2,1)S(1)}, bf16[1088,256]{1,0:T(8,128)(2,1)S(1)}, u32[]{:S(2)}, u32[]{:S(2)}) collective-permute-start(bf16[1088,256]{1,0:T(8,128)(2,1)S(1)} %partial_attention.8), channel_id=1, source_target_pairs={{0,24},{8,0},{16,8},{24,16},{1,25},{9,1},{17,9},{25,17},{2,26},{10... | collective-permute-start | bytes 1671176 | tf_op jit(solution)/shard_map/ppermute | solution.py:29
  207.6 16.2 %collective-permute-start.11 = (bf16[1088,256]{1,0:T(8,128)(2,1)}, bf16[1088,256]{1,0:T(8,128)(2,1)}, u32[]{:S(2)}, u32[]{:S(2)}) collective-permute-start(bf16[1088,256]{1,0:T(8,128)(2,1)} %partial_attention.7), channel_id=1, source_target_pairs={{0,8},{8,16},{16,24},{24,0},{1,9},{9,17},{17,25},{25,1},{2,10},{10... | collective-permute-start | bytes 1671176 | tf_op jit(solution)/shard_map/ppermute | solution.py:29
Sparse Core Ops, SparseCore 0:
  9.5 63.1 all-gather.2
  78.1 108.9 all-gather.4

commit v7 on v5

--- a/solution.py
+++ b/solution.py
@@ -28,7 +28,7 @@
     return lax.ppermute(value, axis, [(i, (i + by) % size) for i in range(size)])
 
 
-def project_kernel(place, rows, part0, part1, part2, part3, out, buffer, weight, sems):
+def project_kernel(ring, place, rows, part0, part1, part2, part3, out, buffer, weight, sems):
     count, depth = rows.shape
 
     def copy(t):
@@ -41,7 +41,8 @@
         owner = lax.rem(place[0] + 4 - s, 4)
         for za in range(4):
             for zb in range(4):
-                weight[za * 4 + zb, owner] = part[zb, za]
+                at = lax.rem(place[1] + 4 - zb, 4) if ring else zb
+                weight[za * 4 + at, owner] = part[zb, za]
 
     def step(t, carry):
         copy(t).wait()
@@ -55,12 +56,12 @@
     lax.fori_loop(0, count // ROW_TILE, step, 0)
 
 
-def project(place, rows, parts):
+def project(ring, place, rows, parts):
     count, depth = rows.shape
     width = parts[0].shape[-1]
     vmem = pl.BlockSpec(memory_space=pltpu.VMEM)
     return pl.pallas_call(
-        project_kernel,
+        functools.partial(project_kernel, ring),
         in_specs=[pl.BlockSpec(memory_space=pltpu.SMEM), pl.BlockSpec(memory_space=pl.ANY)]
         + [vmem] * 4,
         out_specs=vmem,
@@ -296,22 +297,25 @@
     both = jnp.concatenate([kv_weight, query_weight], axis=1)
     both = lax.all_gather(both, "a", axis=0, tiled=True)
     kv_own = lax.all_gather(both[:, :width], "b", axis=0, tiled=True)
-    query_own_in, kv_own = lax.optimization_barrier((both[:, width:], kv_own))
+    query_first, kv_own = lax.optimization_barrier((both[:, width:], kv_own))
 
     def spread(own):
         own = own.reshape(4, 4, 64, width)
         return [own] + [shift(own, "x", s) for s in (1, 2, 3)]
 
     kv_parts = spread(kv_own)
-    query_own = lax.all_gather(query_own_in, "b", axis=0, tiled=True)
-    kv_parts, query_own = lax.optimization_barrier((kv_parts, query_own))
-
-    place_1 = place.reshape(1)
-    kv_rows = project(place_1, rows, kv_parts)
+    planes = 16
+    query_turns = [query_first] + [
+        lax.ppermute(query_first, ("a", "b"), [(i, (i + t) % planes) for i in range(planes)])
+        for t in (1, 2, planes - 1)
+    ]
+
+    place_2 = jnp.stack([place, lax.axis_index("b").astype(jnp.int32)])
+    kv_rows = project(False, place_2, rows, kv_parts)
     held = lax.all_gather(kv_rows, ("a", "b"), axis=0, tiled=True)
     held = held.reshape(-1, BS, 2 * HD)
-    query_own, reach, kv_rows = lax.optimization_barrier((query_own, reach, kv_rows))
-    query_rows = project(place_1, rows, spread(query_own))
+    query_turns, reach, kv_rows = lax.optimization_barrier((query_turns, reach, kv_rows))
+    query_rows = project(True, place_2, rows, spread(jnp.stack(query_turns)))
     queries = [query_rows] + [shift(query_rows, "x", s) for s in (1, 2, 3)]
 
     own_index, own_counts = own_lists(reach)

time: 236 us -> 234 us (level)
  blocking collectives: 50.7 us -> 38 us
  starting transfers between devices: 49.9 us -> 57.7 us
  waiting for transfers between devices: 79.7 us -> 82.1 us
    all_gather x1 -> x0, blocking collectives: 12.6 us -> none  [per_device(): query_own = lax.all_gather(query_own_in, 'b', axis=0, tiled=True)]
    all_gather x1, waiting for transfers between devices: 31.9 us -> 20.1 us  [per_device(): held = lax.all_gather(kv_rows, ('a', 'b'), axis=0, tiled=True)]
    ppermute x14, waiting for transfers between devices: 47.1 us -> 58.7 us  [shift(): lax.ppermute(value, axis, [(i, (i + by) % size) for i in range(size)])]
    ppermute x0 -> x3, starting transfers between devices: none -> 10.6 us  [per_device(): lax.ppermute(query_first, ('a', 'b'), [(i, (i + t) % planes) for i in ran...]
    ppermute x14, starting transfers between devices: 49.8 us -> 47.1 us  [shift(): lax.ppermute(value, axis, [(i, (i + by) % size) for i in range(size)])]
    ppermute x0 -> x3, waiting for transfers between devices: none -> 2.66 us  [per_device(): lax.ppermute(query_first, ('a', 'b'), [(i, (i + t) % planes) for i in ran...]
  transfers between devices with their start and end apart: 16 -> 19, of which waited for: 9 -> 13; matrix products, arithmetic and copies ran while one was open for 1% -> 1% of each run, Pallas kernels for 10% -> 10%
where the time goes in v7:
time: 234 us; the launch traced here: 232 us
  waiting for transfers between devices  82.1 us (35%)
  starting transfers between devices  57.7 us (25%)
  blocking collectives  38 us (16%)
  Pallas kernels  36.8 us (16%)
  between operations  13.7 us (6%)
    ppermute x14, waiting for transfers between devices, shift(): lax.ppermute(value, axis, [(i, (i + by) % size) for i in range(size)])  58.7 us
    ppermute x14, starting transfers between devices, shift(): lax.ppermute(value, axis, [(i, (i + by) % size) for i in range(size)])  47.1 us
    all_gather x1, blocking collectives, per_device(): both = lax.all_gather(both, 'a', axis=0, tiled=True)  25.2 us
    pallas_call x5, Pallas kernels, partial_attention(): pl.pallas_call(partial_kernel, in_specs=[smem] * 3 + [vmem, pl.BlockSpec(...  22.4 us
    all_gather x1, waiting for transfers between devices, per_device(): held = lax.all_gather(kv_rows, ('a', 'b'), axis=0, tiled=True)  20.1 us
    all_gather x1, blocking collectives, per_device(): kv_own = lax.all_gather(both[:, :width], 'b', axis=0, tiled=True)  12.8 us
    pallas_call x2, Pallas kernels, project(): pl.pallas_call(functools.partial(project_kernel, ring), in_specs=[pl.Bloc...  10.9 us
    ppermute x3, starting transfers between devices, per_device(): lax.ppermute(query_first, ('a', 'b'), [(i, (i + t) % planes) for i in ran...  10.6 us
  transfers between devices with their start and end apart: 19, of which 13 were waited for; matrix products, arithmetic and copies ran while one was open for 1% of the time, Pallas kernels for 10%

profile of v7, /device:TPU:1, one launch (start us, length us, event | category | flops | bytes accessed | tf_op | source)
XLA Modules:
  0.0 232.2 jit_solution(5621420088485088250)
XLA Ops:
  8.1 25.2 %all_gather.13 = bf16[256,512]{1,0:T(8,128)(2,1)S(1)} all-gather(bf16[64,512]{1,0:T(8,128)(2,1)S(1)} %pad_maximum_fusion.1), channel_id=1, replica_groups=mesh['a'=4,'b'=4,'x'=4,'y'=4,'c'=2] {'a'}, dimensions={0}, use_global_device_ids=true | all-gather | bytes 327680 | tf_op jit(solution)/shard_map/all_gather | solution.py:298
  33.4 12.8 %all_gather.14 = bf16[1024,256]{1,0:T(8,128)(2,1)S(1)} all-gather(bf16[256,256]{1,0:T(8,128)(2,1)S(1)} %get-tuple-element.43), channel_id=1, replica_groups=mesh['a'=4,'b'=4,'x'=4,'y'=4,'c'=2] {'b'}, dimensions={0}, use_global_device_ids=true | all-gather | bytes 655360 | tf_op jit(solution)/shard_map/all_gather | solution.py:299
  46.1 3.1 %collective-permute-start = (bf16[4,4,64,256]{3,2,1,0:T(8,128)(2,1)S(1)}, bf16[4,4,64,256]{3,2,1,0:T(8,128)(2,1)S(1)}, u32[]{:S(2)}, u32[]{:S(2)}) collective-permute-start(bf16[4,4,64,256]{3,2,1,0:T(8,128)(2,1)S(1)} %bitcast.13), channel_id=1, source_target_pairs={{0,8},{8,16},{16,24},{24,0},{1,9},{9,17},{17,25},{25,1},{2,10},{10... | collective-permute-start | bytes 1572872 | tf_op jit(solution)/shard_map/ppermute | solution.py:28
  49.3 4.4 %collective-permute-start.1 = (bf16[4,4,64,256]{3,2,1,0:T(8,128)(2,1)S(1)}, bf16[4,4,64,256]{3,2,1,0:T(8,128)(2,1)S(1)}, u32[]{:S(2)}, u32[]{:S(2)}) collective-permute-start(bf16[4,4,64,256]{3,2,1,0:T(8,128)(2,1)S(1)} %bitcast.14), channel_id=1, source_target_pairs={{0,16},{8,24},{16,0},{24,8},{1,17},{9,25},{17,1},{25,9},{2,18},{10... | collective-permute-start | bytes 1572872 | tf_op jit(solution)/shard_map/ppermute | solution.py:28
  53.6 3.1 %collective-permute-start.2 = (bf16[4,4,64,256]{3,2,1,0:T(8,128)(2,1)S(1)}, bf16[4,4,64,256]{3,2,1,0:T(8,128)(2,1)S(1)}, u32[]{:S(2)}, u32[]{:S(2)}) collective-permute-start(bf16[4,4,64,256]{3,2,1,0:T(8,128)(2,1)S(1)} %bitcast.15), channel_id=1, source_target_pairs={{0,24},{8,0},{16,8},{24,16},{1,25},{9,1},{17,9},{25,17},{2,26},{10... | collective-permute-start | bytes 1572872 | tf_op jit(solution)/shard_map/ppermute | solution.py:28
  57.7 11.0 %collective-permute-done.1.part2 = bf16[4,4,64,256]{3,2,1,0:T(8,128)(2,1)S(1)} collective-permute-done((bf16[4,4,64,256]{3,2,1,0:T(8,128)(2,1)S(1)}, bf16[4,4,64,256]{3,2,1,0:T(8,128)(2,1)S(1)}, u32[]{:S(2)}, u32[]{:S(2)}) %collective-permute-start.1) | collective-permute-done | bytes 524320 | tf_op jit(solution)/shard_map/ppermute | solution.py:28
  68.6 4.2 %collective-permute-done.2.part3 = bf16[4,4,64,256]{3,2,1,0:T(8,128)(2,1)S(1)} collective-permute-done((bf16[4,4,64,256]{3,2,1,0:T(8,128)(2,1)S(1)}, bf16[4,4,64,256]{3,2,1,0:T(8,128)(2,1)S(1)}, u32[]{:S(2)}, u32[]{:S(2)}) %collective-permute-start.2) | collective-permute-done | bytes 524320 | tf_op jit(solution)/shard_map/ppermute | solution.py:28
  72.8 5.8 %project.2 = bf16[1024,256]{1,0:T(8,128)(2,1)} custom-call(s32[2]{0:T(128)S(1)} %pad_add_fusion.1.place, bf16[1024,4096]{1,0:T(8,128)(2,1)} %all-gather.3.cloned.1.call-done.rows, bf16[4,4,64,256]{3,2,1,0:T(8,128)(2,1)S(1)} %bitcast.16, bf16[4,4,64,256]{3,2,1,0:T(8,128)(2,1)S(1)} %collective-permute-done.part1, ...), custom_call_target="tpu_custom_call" | custom-call | flops 2147483648 | bytes 11010048 | tf_op jit(solution)/shard_map/project/pallas_call | solution.py:63
  78.7 3.1 %collective-permute-start.3 = (bf16[256,256]{1,0:T(8,128)(2,1)S(1)}, bf16[256,256]{1,0:T(8,128)(2,1)S(1)}, u32[]{:S(2)}, u32[]{:S(2)}) collective-permute-start(bf16[256,256]{1,0:T(8,128)(2,1)S(1)} %get-tuple-element.24), channel_id=1, source_target_pairs={{0,32},{32,64},{64,96},{96,128},{128,160},{160,192},{192,224},{224... | collective-permute-start | bytes 393224 | tf_op jit(solution)/shard_map/ppermute | solution.py:309
  81.7 4.2 %collective-permute-start.4 = (bf16[256,256]{1,0:T(8,128)(2,1)S(1)}, bf16[256,256]{1,0:T(8,128)(2,1)S(1)}, u32[]{:S(2)}, u32[]{:S(2)}) collective-permute-start(bf16[256,256]{1,0:T(8,128)(2,1)S(1)} %get-tuple-element.24), channel_id=1, source_target_pairs={{0,64},{32,96},{64,128},{96,160},{128,192},{160,224},{192,256},{22... | collective-permute-start | bytes 393224 | tf_op jit(solution)/shard_map/ppermute | solution.py:309
  85.9 3.3 %collective-permute-start.5 = (bf16[256,256]{1,0:T(8,128)(2,1)S(1)}, bf16[256,256]{1,0:T(8,128)(2,1)S(1)}, u32[]{:S(2)}, u32[]{:S(2)}) collective-permute-start(bf16[256,256]{1,0:T(8,128)(2,1)S(1)} %get-tuple-element.24), channel_id=1, source_target_pairs={{0,480},{32,0},{64,32},{96,64},{128,96},{160,128},{192,160},{224,1... | collective-permute-start | bytes 393224 | tf_op jit(solution)/shard_map/ppermute | solution.py:309
  93.0 4.2 %collective-permute-start.9 = (s32[16]{0:T(128)S(1)}, s32[16]{0:T(128)S(1)}, u32[]{:S(2)}, u32[]{:S(2)}) collective-permute-start(s32[16]{0:T(128)S(1)} %copy-done.3), channel_id=1, source_target_pairs={{0,8},{8,16},{16,24},{24,0},{1,9},{9,17},{17,25},{25,1},{2,10},{10... | collective-permute-start | bytes 200 | tf_op jit(solution)/shard_map/ppermute | solution.py:28
  99.5 3.0 %collective-permute-start.6 = (bf16[4,4,64,256]{3,2,1,0:T(8,128)(2,1)S(1)}, bf16[4,4,64,256]{3,2,1,0:T(8,128)(2,1)S(1)}, u32[]{:S(2)}, u32[]{:S(2)}) collective-permute-start(bf16[4,4,64,256]{3,2,1,0:T(8,128)(2,1)S(1)} %pad_maximum_fusion.part0), channel_id=1, source_target_pairs={{0,8},{8,16},{16,24},{24,0},{1,9},{9,17},{17,25},{25,1},{2,10},{10... | collective-permute-start | bytes 1572872 | tf_op jit(solution)/shard_map/ppermute | solution.py:28
  102.5 3.0 %collective-permute-start.7 = (bf16[4,4,64,256]{3,2,1,0:T(8,128)(2,1)S(1)}, bf16[4,4,64,256]{3,2,1,0:T(8,128)(2,1)S(1)}, u32[]{:S(2)}, u32[]{:S(2)}) collective-permute-start(bf16[4,4,64,256]{3,2,1,0:T(8,128)(2,1)S(1)} %pad_maximum_fusion.part0), channel_id=1, source_target_pairs={{0,16},{8,24},{16,0},{24,8},{1,17},{9,25},{17,1},{25,9},{2,18},{10... | collective-permute-start | bytes 1572872 | tf_op jit(solution)/shard_map/ppermute | solution.py:28
  105.5 3.3 %collective-permute-start.8 = (bf16[4,4,64,256]{3,2,1,0:T(8,128)(2,1)S(1)}, bf16[4,4,64,256]{3,2,1,0:T(8,128)(2,1)S(1)}, u32[]{:S(2)}, u32[]{:S(2)}) collective-permute-start(bf16[4,4,64,256]{3,2,1,0:T(8,128)(2,1)S(1)} %pad_maximum_fusion.part0), channel_id=1, source_target_pairs={{0,24},{8,0},{16,8},{24,16},{1,25},{9,1},{17,9},{25,17},{2,26},{10... | collective-permute-start | bytes 1572872 | tf_op jit(solution)/shard_map/ppermute | solution.py:28
  112.2 9.7 %collective-permute-done.7.part2 = bf16[4,4,64,256]{3,2,1,0:T(8,128)(2,1)S(1)} collective-permute-done((bf16[4,4,64,256]{3,2,1,0:T(8,128)(2,1)S(1)}, bf16[4,4,64,256]{3,2,1,0:T(8,128)(2,1)S(1)}, u32[]{:S(2)}, u32[]{:S(2)}) %collective-permute-start.7) | collective-permute-done | bytes 524320 | tf_op jit(solution)/shard_map/ppermute | solution.py:28
  121.8 6.2 %collective-permute-done.8.part3 = bf16[4,4,64,256]{3,2,1,0:T(8,128)(2,1)S(1)} collective-permute-done((bf16[4,4,64,256]{3,2,1,0:T(8,128)(2,1)S(1)}, bf16[4,4,64,256]{3,2,1,0:T(8,128)(2,1)S(1)}, u32[]{:S(2)}, u32[]{:S(2)}) %collective-permute-start.8) | collective-permute-done | bytes 524320 | tf_op jit(solution)/shard_map/ppermute | solution.py:28
  128.0 5.1 %project.3.query = bf16[1024,256]{1,0:T(8,128)(2,1)S(1)} custom-call(s32[2]{0:T(128)S(1)} %pad_add_fusion.1.place, bf16[1024,4096]{1,0:T(8,128)(2,1)} %all-gather.3.cloned.1.call-done.rows, bf16[4,4,64,256]{3,2,1,0:T(8,128)(2,1)S(1)} %pad_maximum_fusion.part0, bf16[4,4,64,256]{3,2,1,0:T(8,128)(2,1)S(1)} %collective-permute-done.6.part1, ...), custom_call_target="tpu_custom_call" | custom-call | flops 2147483648 | bytes 11010048 | tf_op jit(solution)/shard_map/project/pallas_call | solution.py:63
  133.1 4.0 %collective-permute-start.11 = (bf16[1024,256]{1,0:T(8,128)(2,1)S(1)}, bf16[1024,256]{1,0:T(8,128)(2,1)S(1)}, u32[]{:S(2)}, u32[]{:S(2)}) collective-permute-start(bf16[1024,256]{1,0:T(8,128)(2,1)S(1)} %project.3.query), channel_id=1, source_target_pairs={{0,8},{8,16},{16,24},{24,0},{1,9},{9,17},{17,25},{25,1},{2,10},{10... | collective-permute-start | bytes 1572872 | tf_op jit(solution)/shard_map/ppermute | solution.py:28
  137.0 4.6 %collective-permute-start.12 = (bf16[1024,256]{1,0:T(8,128)(2,1)S(1)}, bf16[1024,256]{1,0:T(8,128)(2,1)S(1)}, u32[]{:S(2)}, u32[]{:S(2)}) collective-permute-start(bf16[1024,256]{1,0:T(8,128)(2,1)S(1)} %project.3.query), channel_id=1, source_target_pairs={{0,16},{8,24},{16,0},{24,8},{1,17},{9,25},{17,1},{25,9},{2,18},{10... | collective-permute-start | bytes 1572872 | tf_op jit(solution)/shard_map/ppermute | solution.py:28
  144.0 5.5 %partial_attention.5.refs_4_ = bf16[1088,256]{1,0:T(8,128)(2,1)S(1)} custom-call(s32[1]{0:T(128)} %constant.108.clone.1.from_x, s32[128]{0:T(128)S(1)} %reshape.360.index, s32[16]{0:T(128)S(1)} %get-tuple-element.41.counts, bf16[1024,256]{1,0:T(8,128)(2,1)S(1)} %project.3.query, bf16[16,64,256]{2,1,0:T(8,128)(2,1)} %bitcast.9.held), custom_call_target="tpu_custom_call" | custom-call | flops 2000000000 | bytes 65536 | tf_op jit(solution)/shard_map/partial_attention/pallas_call | solution.py:181
  149.5 11.7 %collective-permute-done.12.query = bf16[1024,256]{1,0:T(8,128)(2,1)S(1)} collective-permute-done((bf16[1024,256]{1,0:T(8,128)(2,1)S(1)}, bf16[1024,256]{1,0:T(8,128)(2,1)S(1)}, u32[]{:S(2)}, u32[]{:S(2)}) %collective-permute-start.12) | collective-permute-done | bytes 524320 | tf_op jit(solution)/shard_map/ppermute | solution.py:28
  164.5 20.1 %all-gather.5.cloned.1.call-done = bf16[16384,256]{1,0:T(8,128)(2,1)} async-done(((bf16[1024,256]{1,0:T(8,128)(2,1)}), bf16[16384,256]{1,0:T(8,128)(2,1)}) %all-gather.5.cloned.1.call-update) | async-done | bytes 8388624 | tf_op jit(solution)/shard_map/all_gather | solution.py:315
  184.6 4.0 %partial_attention.9 = bf16[1088,256]{1,0:T(8,128)(2,1)S(1)} custom-call(s32[1]{0:T(128)} %bitcast.12.from_x, s32[512]{0:T(512)S(1)} %reshape.362.index, s32[64]{0:T(128)S(1)} %get-tuple-element.30.counts, bf16[1024,256]{1,0:T(8,128)(2,1)S(1)} %collective-permute-done.12.query, bf16[256,64,256]{2,1,0:T(8,128)(2,1)} %bitcast.17), custom_call_target="tpu_custom_call" | custom-call | flops 2000000000 | bytes 65536 | tf_op jit(solution)/shard_map/partial_attention/pallas_call | solution.py:181
  188.6 5.1 %collective-permute-start.16 = (bf16[1088,256]{1,0:T(8,128)(2,1)S(1)}, bf16[1088,256]{1,0:T(8,128)(2,1)S(1)}, u32[]{:S(2)}, u32[]{:S(2)}) collective-permute-start(bf16[1088,256]{1,0:T(8,128)(2,1)S(1)} %partial_attention.9), channel_id=1, source_target_pairs={{0,16},{8,24},{16,0},{24,8},{1,17},{9,25},{17,1},{25,9},{2,18},{10... | collective-permute-start | bytes 1671176 | tf_op jit(solution)/shard_map/ppermute | solution.py:28
  193.7 4.0 %partial_attention.8 = bf16[1088,256]{1,0:T(8,128)(2,1)S(1)} custom-call(s32[1]{0:T(128)} %bitcast.11.from_x, s32[512]{0:T(512)S(1)} %reshape.362.index, s32[64]{0:T(128)S(1)} %get-tuple-element.30.counts, bf16[1024,256]{1,0:T(8,128)(2,1)S(1)} %collective-permute-done.11.query, bf16[256,64,256]{2,1,0:T(8,128)(2,1)} %bitcast.18), custom_call_target="tpu_custom_call" | custom-call | flops 2000000000 | bytes 65536 | tf_op jit(solution)/shard_map/partial_attention/pallas_call | solution.py:181
  197.7 3.1 %collective-permute-start.15 = (bf16[1088,256]{1,0:T(8,128)(2,1)S(1)}, bf16[1088,256]{1,0:T(8,128)(2,1)S(1)}, u32[]{:S(2)}, u32[]{:S(2)}) collective-permute-start(bf16[1088,256]{1,0:T(8,128)(2,1)S(1)} %partial_attention.8), channel_id=1, source_target_pairs={{0,24},{8,0},{16,8},{24,16},{1,25},{9,1},{17,9},{25,17},{2,26},{10... | collective-permute-start | bytes 1671176 | tf_op jit(solution)/shard_map/ppermute | solution.py:28
  200.7 4.9 %partial_attention.7 = bf16[1088,256]{1,0:T(8,128)(2,1)} custom-call(s32[1]{0:T(128)} %bitcast.10.from_x, s32[512]{0:T(512)S(1)} %reshape.362.index, s32[64]{0:T(128)S(1)} %get-tuple-element.30.counts, bf16[1024,256]{1,0:T(8,128)(2,1)S(1)} %copy-done.1, bf16[256,64,256]{2,1,0:T(8,128)(2,1)} %bitcast.19), custom_call_target="tpu_custom_call" | custom-call | flops 2000000000 | bytes 65536 | tf_op jit(solution)/shard_map/partial_attention/pallas_call | solution.py:181
  207.8 4.0 %partial_attention.6.refs_0_ = bf16[1088,256]{1,0:T(8,128)(2,1)S(1)} custom-call(s32[1]{0:T(128)} %bitcast.from_x, s32[512]{0:T(512)S(1)} %reshape.362.index, s32[64]{0:T(128)S(1)} %get-tuple-element.30.counts, bf16[1024,256]{1,0:T(8,128)(2,1)S(1)} %project.3.query, bf16[256,64,256]{2,1,0:T(8,128)(2,1)} %bitcast.20), custom_call_target="tpu_custom_call" | custom-call | flops 2000000000 | bytes 65536 | tf_op jit(solution)/shard_map/partial_attention/pallas_call | solution.py:181
  211.9 6.1 %collective-permute-done.15.refs_2_ = bf16[1088,256]{1,0:T(8,128)(2,1)S(1)} collective-permute-done((bf16[1088,256]{1,0:T(8,128)(2,1)S(1)}, bf16[1088,256]{1,0:T(8,128)(2,1)S(1)}, u32[]{:S(2)}, u32[]{:S(2)}) %collective-permute-start.15) | collective-permute-done | bytes 557088 | tf_op jit(solution)/shard_map/ppermute | solution.py:28
  218.0 3.9 %collective-permute-done.14.refs_1_ = bf16[1088,256]{1,0:T(8,128)(2,1)} collective-permute-done((bf16[1088,256]{1,0:T(8,128)(2,1)}, bf16[1088,256]{1,0:T(8,128)(2,1)}, u32[]{:S(2)}, u32[]{:S(2)}) %collective-permute-start.14) | collective-permute-done | bytes 557088 | tf_op jit(solution)/shard_map/ppermute | solution.py:28
  221.9 3.5 %combine.1 = bf16[1024,256]{1,0:T(8,128)(2,1)} custom-call(bf16[1088,256]{1,0:T(8,128)(2,1)S(1)} %partial_attention.6.refs_0_, bf16[1088,256]{1,0:T(8,128)(2,1)} %collective-permute-done.14.refs_1_, bf16[1088,256]{1,0:T(8,128)(2,1)S(1)} %collective-permute-done.15.refs_2_, bf16[1088,256]{1,0:T(8,128)(2,1)S(1)} %collective-permute-done.16.refs_3_, ...), custom_call_target="tpu_custom_call" | custom-call | tf_op jit(solution)/shard_map/combine/pallas_call | solution.py:231
  (59 shorter events, 19.6 us)
Async XLA Ops:
  6.5 82.8 %copy-start.2 = (s32[4]{0:T(128)S(1)}, s32[4]{0:T(128)}, u32[]{:S(2)}) copy-start(s32[4]{0:T(128)} %constant.120.clone) | copy-start | bytes 52
  6.5 102.9 %copy-start.4 = (s32[4]{0:T(128)S(1)}, s32[4]{0:T(128)}, u32[]{:S(2)}) copy-start(s32[4]{0:T(128)} %constant.123) | copy-start | bytes 52
  6.5 82.8 %copy-start.5 = (s32[2]{0:T(128)S(1)}, s32[2]{0:T(128)}, u32[]{:S(2)}) copy-start(s32[2]{0:T(128)} %param.11) | copy-start | bytes 28
  6.5 86.4 %copy-start.3 = (s32[16]{0:T(128)S(1)}, s32[16]{0:T(128)}, u32[]{:S(2)}) copy-start(s32[16]{0:T(128)} %param.10) | copy-start | bytes 196
  6.5 66.3 %all-gather.3.cloned.1.call-start = ((), (), s32[]{:S(2)}) async-start(), calls=%async_computation | async-start | bytes 9437184 | tf_op jit(solution)/shard_map/all_gather | solution.py:295
  7.3 177.3 %all-gather.5.cloned.1.call-start = ((), (), s32[]{:S(2)}) async-start(), calls=%async_computation.1 | async-start | bytes 8912896 | tf_op jit(solution)/shard_map/all_gather | solution.py:315
  46.1 11.5 %collective-permute-start = (bf16[4,4,64,256]{3,2,1,0:T(8,128)(2,1)S(1)}, bf16[4,4,64,256]{3,2,1,0:T(8,128)(2,1)S(1)}, u32[]{:S(2)}, u32[]{:S(2)}) collective-permute-start(bf16[4,4,64,256]{3,2,1,0:T(8,128)(2,1)S(1)} %bitcast.13), channel_id=1, source_target_pairs={{0,8},{8,16},{16,24},{24,0},{1,9},{9,17},{17,25},{25,1},{2,10},{10... | collective-permute-start | bytes 1572872 | tf_op jit(solution)/shard_map/ppermute | solution.py:28
  49.3 19.4 %collective-permute-start.1 = (bf16[4,4,64,256]{3,2,1,0:T(8,128)(2,1)S(1)}, bf16[4,4,64,256]{3,2,1,0:T(8,128)(2,1)S(1)}, u32[]{:S(2)}, u32[]{:S(2)}) collective-permute-start(bf16[4,4,64,256]{3,2,1,0:T(8,128)(2,1)S(1)} %bitcast.14), channel_id=1, source_target_pairs={{0,16},{8,24},{16,0},{24,8},{1,17},{9,25},{17,1},{25,9},{2,18},{10... | collective-permute-start | bytes 1572872 | tf_op jit(solution)/shard_map/ppermute | solution.py:28
  53.6 19.2 %collective-permute-start.2 = (bf16[4,4,64,256]{3,2,1,0:T(8,128)(2,1)S(1)}, bf16[4,4,64,256]{3,2,1,0:T(8,128)(2,1)S(1)}, u32[]{:S(2)}, u32[]{:S(2)}) collective-permute-start(bf16[4,4,64,256]{3,2,1,0:T(8,128)(2,1)S(1)} %bitcast.15), channel_id=1, source_target_pairs={{0,24},{8,0},{16,8},{24,16},{1,25},{9,1},{17,9},{25,17},{2,26},{10... | collective-permute-start | bytes 1572872 | tf_op jit(solution)/shard_map/ppermute | solution.py:28
  78.7 11.6 %collective-permute-start.3 = (bf16[256,256]{1,0:T(8,128)(2,1)S(1)}, bf16[256,256]{1,0:T(8,128)(2,1)S(1)}, u32[]{:S(2)}, u32[]{:S(2)}) collective-permute-start(bf16[256,256]{1,0:T(8,128)(2,1)S(1)} %get-tuple-element.24), channel_id=1, source_target_pairs={{0,32},{32,64},{64,96},{96,128},{128,160},{160,192},{192,224},{224... | collective-permute-start | bytes 393224 | tf_op jit(solution)/shard_map/ppermute | solution.py:309
  81.7 9.6 %collective-permute-start.4 = (bf16[256,256]{1,0:T(8,128)(2,1)S(1)}, bf16[256,256]{1,0:T(8,128)(2,1)S(1)}, u32[]{:S(2)}, u32[]{:S(2)}) collective-permute-start(bf16[256,256]{1,0:T(8,128)(2,1)S(1)} %get-tuple-element.24), channel_id=1, source_target_pairs={{0,64},{32,96},{64,128},{96,160},{128,192},{160,224},{192,256},{22... | collective-permute-start | bytes 393224 | tf_op jit(solution)/shard_map/ppermute | solution.py:309
  85.9 7.0 %collective-permute-start.5 = (bf16[256,256]{1,0:T(8,128)(2,1)S(1)}, bf16[256,256]{1,0:T(8,128)(2,1)S(1)}, u32[]{:S(2)}, u32[]{:S(2)}) collective-permute-start(bf16[256,256]{1,0:T(8,128)(2,1)S(1)} %get-tuple-element.24), channel_id=1, source_target_pairs={{0,480},{32,0},{64,32},{96,64},{128,96},{160,128},{192,160},{224,1... | collective-permute-start | bytes 393224 | tf_op jit(solution)/shard_map/ppermute | solution.py:309
  93.0 16.2 %collective-permute-start.9 = (s32[16]{0:T(128)S(1)}, s32[16]{0:T(128)S(1)}, u32[]{:S(2)}, u32[]{:S(2)}) collective-permute-start(s32[16]{0:T(128)S(1)} %copy-done.3), channel_id=1, source_target_pairs={{0,8},{8,16},{16,24},{24,0},{1,9},{9,17},{17,25},{25,1},{2,10},{10... | collective-permute-start | bytes 200 | tf_op jit(solution)/shard_map/ppermute | solution.py:28
  97.1 12.2 %collective-permute-start.10 = (s32[16]{0:T(128)S(1)}, s32[16]{0:T(128)S(1)}, u32[]{:S(2)}, u32[]{:S(2)}) collective-permute-start(s32[16]{0:T(128)S(1)} %copy-done.3), channel_id=1, source_target_pairs={{0,24},{8,0},{16,8},{24,16},{1,25},{9,1},{17,9},{25,17},{2,26},{10... | collective-permute-start | bytes 200 | tf_op jit(solution)/shard_map/ppermute | solution.py:28
  99.5 12.6 %collective-permute-start.6 = (bf16[4,4,64,256]{3,2,1,0:T(8,128)(2,1)S(1)}, bf16[4,4,64,256]{3,2,1,0:T(8,128)(2,1)S(1)}, u32[]{:S(2)}, u32[]{:S(2)}) collective-permute-start(bf16[4,4,64,256]{3,2,1,0:T(8,128)(2,1)S(1)} %pad_maximum_fusion.part0), channel_id=1, source_target_pairs={{0,8},{8,16},{16,24},{24,0},{1,9},{9,17},{17,25},{25,1},{2,10},{10... | collective-permute-start | bytes 1572872 | tf_op jit(solution)/shard_map/ppermute | solution.py:28
  102.5 19.3 %collective-permute-start.7 = (bf16[4,4,64,256]{3,2,1,0:T(8,128)(2,1)S(1)}, bf16[4,4,64,256]{3,2,1,0:T(8,128)(2,1)S(1)}, u32[]{:S(2)}, u32[]{:S(2)}) collective-permute-start(bf16[4,4,64,256]{3,2,1,0:T(8,128)(2,1)S(1)} %pad_maximum_fusion.part0), channel_id=1, source_target_pairs={{0,16},{8,24},{16,0},{24,8},{1,17},{9,25},{17,1},{25,9},{2,18},{10... | collective-permute-start | bytes 1572872 | tf_op jit(solution)/shard_map/ppermute | solution.py:28
  105.5 22.5 %collective-permute-start.8 = (bf16[4,4,64,256]{3,2,1,0:T(8,128)(2,1)S(1)}, bf16[4,4,64,256]{3,2,1,0:T(8,128)(2,1)S(1)}, u32[]{:S(2)}, u32[]{:S(2)}) collective-permute-start(bf16[4,4,64,256]{3,2,1,0:T(8,128)(2,1)S(1)} %pad_maximum_fusion.part0), channel_id=1, source_target_pairs={{0,24},{8,0},{16,8},{24,16},{1,25},{9,1},{17,9},{25,17},{2,26},{10... | collective-permute-start | bytes 1572872 | tf_op jit(solution)/shard_map/ppermute | solution.py:28
  133.1 16.4 %collective-permute-start.11 = (bf16[1024,256]{1,0:T(8,128)(2,1)S(1)}, bf16[1024,256]{1,0:T(8,128)(2,1)S(1)}, u32[]{:S(2)}, u32[]{:S(2)}) collective-permute-start(bf16[1024,256]{1,0:T(8,128)(2,1)S(1)} %project.3.query), channel_id=1, source_target_pairs={{0,8},{8,16},{16,24},{24,0},{1,9},{9,17},{17,25},{25,1},{2,10},{10... | collective-permute-start | bytes 1572872 | tf_op jit(solution)/shard_map/ppermute | solution.py:28
  137.0 24.2 %collective-permute-start.12 = (bf16[1024,256]{1,0:T(8,128)(2,1)S(1)}, bf16[1024,256]{1,0:T(8,128)(2,1)S(1)}, u32[]{:S(2)}, u32[]{:S(2)}) collective-permute-start(bf16[1024,256]{1,0:T(8,128)(2,1)S(1)} %project.3.query), channel_id=1, source_target_pairs={{0,16},{8,24},{16,0},{24,8},{1,17},{9,25},{17,1},{25,9},{2,18},{10... | collective-permute-start | bytes 1572872 | tf_op jit(solution)/shard_map/ppermute | solution.py:28
  141.6 22.0 %collective-permute-start.13 = (bf16[1024,256]{1,0:T(8,128)(2,1)S(1)}, bf16[1024,256]{1,0:T(8,128)(2,1)S(1)}, u32[]{:S(2)}, u32[]{:S(2)}) collective-permute-start(bf16[1024,256]{1,0:T(8,128)(2,1)S(1)} %project.3.query), channel_id=1, source_target_pairs={{0,24},{8,0},{16,8},{24,16},{1,25},{9,1},{17,9},{25,17},{2,26},{10... | collective-permute-start | bytes 1572872 | tf_op jit(solution)/shard_map/ppermute | solution.py:28
  163.6 0.8 copy-start
  184.5 16.2 %copy-start.1 = (bf16[1024,256]{1,0:T(8,128)(2,1)S(1)}, bf16[1024,256]{1,0:T(8,128)(2,1)}, u32[]{:S(2)}) copy-start(bf16[1024,256]{1,0:T(8,128)(2,1)} %copy-done) | copy-start | bytes 1572868
  188.6 23.3 %collective-permute-start.16 = (bf16[1088,256]{1,0:T(8,128)(2,1)S(1)}, bf16[1088,256]{1,0:T(8,128)(2,1)S(1)}, u32[]{:S(2)}, u32[]{:S(2)}) collective-permute-start(bf16[1088,256]{1,0:T(8,128)(2,1)S(1)} %partial_attention.9), channel_id=1, source_target_pairs={{0,16},{8,24},{16,0},{24,8},{1,17},{9,25},{17,1},{25,9},{2,18},{10... | collective-permute-start | bytes 1671176 | tf_op jit(solution)/shard_map/ppermute | solution.py:28
  197.7 20.3 %collective-permute-start.15 = (bf16[1088,256]{1,0:T(8,128)(2,1)S(1)}, bf16[1088,256]{1,0:T(8,128)(2,1)S(1)}, u32[]{:S(2)}, u32[]{:S(2)}) collective-permute-start(bf16[1088,256]{1,0:T(8,128)(2,1)S(1)} %partial_attention.8), channel_id=1, source_target_pairs={{0,24},{8,0},{16,8},{24,16},{1,25},{9,1},{17,9},{25,17},{2,26},{10... | collective-permute-start | bytes 1671176 | tf_op jit(solution)/shard_map/ppermute | solution.py:28
  205.6 16.3 %collective-permute-start.14 = (bf16[1088,256]{1,0:T(8,128)(2,1)}, bf16[1088,256]{1,0:T(8,128)(2,1)}, u32[]{:S(2)}, u32[]{:S(2)}) collective-permute-start(bf16[1088,256]{1,0:T(8,128)(2,1)} %partial_attention.7), channel_id=1, source_target_pairs={{0,8},{8,16},{16,24},{24,0},{1,9},{9,17},{17,25},{25,1},{2,10},{10... | collective-permute-start | bytes 1671176 | tf_op jit(solution)/shard_map/ppermute | solution.py:28
Sparse Core Ops, SparseCore 0:
  9.5 63.1 all-gather.2
  78.8 105.7 all-gather.4

commit v8 on v5

--- a/solution.py
+++ b/solution.py
@@ -78,6 +78,16 @@
         ),
         name="project",
     )(place, rows, *parts)
+
+
+def terms_of(level):
+    level = jnp.where(lax.broadcasted_iota(jnp.int32, level.shape, 1) < RUN_BLOCKS, level, 0.0)
+    high = level.astype(BF16).astype(F32)
+    middle = (level - high).astype(BF16).astype(F32)
+    low = level - high - middle
+    return (
+        high + pltpu.roll(middle, RUN_BLOCKS, 1) + pltpu.roll(low, 2 * RUN_BLOCKS, 1)
+    ).astype(BF16)
 
 
 def partial_kernel(from_x, index, counts, query, held, out, slabs, tops_at, sums_at, sems):
@@ -161,14 +171,7 @@
     tops_at[...] = jnp.zeros_like(tops_at)
     sums_at[...] = jnp.ones_like(sums_at)
     lax.fori_loop(0, RUN_BLOCKS // UNROLL, group, 0)
-    spot = lax.broadcasted_iota(jnp.int32, (2 * BS, HD), 1)
-    level = jnp.where(spot < RUN_BLOCKS, tops_at[...] + jnp.log2(sums_at[...]), 0.0)
-    high = level.astype(BF16).astype(F32)
-    middle = (level - high).astype(BF16).astype(F32)
-    low = level - high - middle
-    packed = (
-        high + pltpu.roll(middle, RUN_BLOCKS, 1) + pltpu.roll(low, 2 * RUN_BLOCKS, 1)
-    ).astype(BF16)
+    packed = terms_of(tops_at[...] + jnp.log2(sums_at[...]))
     out[pl.ds(RUN_BLOCKS * BS, PAD), 0:HD] = packed[:BS]
     out[pl.ds(RUN_BLOCKS * BS, PAD), HD : 2 * HD] = packed[BS:]
 
@@ -196,7 +199,7 @@
     )(from_x, index, counts, query, held)
 
 
-def combine_kernel(*refs):
+def combine_kernel(keep, *refs):
     parts, out = refs[:-1], refs[-1]
     rows = pl.ds(RUN_BLOCKS * BS, PAD)
     scales = []
@@ -212,7 +215,10 @@
             )
         top = functools.reduce(jnp.maximum, levels)
         shares = [jnp.exp2(level - top) for level in levels]
-        norm = 1.0 / functools.reduce(jnp.add, shares)
+        total = functools.reduce(jnp.add, shares)
+        norm = 1.0 / total
+        if keep:
+            out[rows, lanes] = terms_of(top + jnp.log2(total))
         scales.append([share * norm for share in shares])
     for j in range(RUN_BLOCKS):
         block = slice(j * BS, (j + 1) * BS)
@@ -225,13 +231,13 @@
             out[block, lanes] = functools.reduce(jnp.add, terms).astype(BF16)
 
 
-def combine(parts):
+def combine(parts, keep=False):
     vmem = pl.BlockSpec(memory_space=pltpu.VMEM)
     return pl.pallas_call(
-        combine_kernel,
+        functools.partial(combine_kernel, keep),
         in_specs=[vmem] * len(parts),
         out_specs=vmem,
-        out_shape=jax.ShapeDtypeStruct((RUN_BLOCKS * BS, 2 * HD), BF16),
+        out_shape=jax.ShapeDtypeStruct((RUN_BLOCKS * BS + keep * PAD, 2 * HD), BF16),
         compiler_params=pltpu.CompilerParams(vmem_limit_bytes=16 << 20),
         name="combine",
     )(*parts)
@@ -331,7 +337,8 @@
         from_x = ((turn + 4 - s) % 4).reshape(1)
         part = partial_attention(from_x, index, counts, queries[s], held)
         parts[s] = part if s == 0 else shift(part, "x", 4 - s)
-    return combine([parts[0], parts[3], parts[1], parts[2], windows])
+    most = combine([parts[0], parts[1], parts[2], windows], keep=True)
+    return combine([most, parts[3]])
 
 
 def solution(mesh):

time: 236 us -> 232 us (0.983)
  waiting for transfers between devices: 79.7 us -> 76.2 us
    ppermute x14, waiting for transfers between devices: 47.1 us -> 43.6 us  [shift(): lax.ppermute(value, axis, [(i, (i + by) % size) for i in range(size)])]
    pallas_call x1 -> x2, Pallas kernels: 3.45 us -> 5.18 us  [combine(): pl.pallas_call(functools.partial(combine_kernel, keep), in_specs=[vmem] *...]
  transfers between devices with their start and end apart: 16 -> 16, of which waited for: 9 -> 9; matrix products, arithmetic and copies ran while one was open for 1% -> 1% of each run, Pallas kernels for 10% -> 11%
where the time goes in v8:
time: 232 us; the launch traced here: 230 us
  waiting for transfers between devices  76.2 us (33%)
  blocking collectives  50.7 us (22%)
  starting transfers between devices  49.9 us (22%)
  Pallas kernels  36.5 us (16%)
  between operations  13.7 us (6%)
    ppermute x14, starting transfers between devices, shift(): lax.ppermute(value, axis, [(i, (i + by) % size) for i in range(size)])  49.8 us
    ppermute x14, waiting for transfers between devices, shift(): lax.ppermute(value, axis, [(i, (i + by) % size) for i in range(size)])  43.6 us
    all_gather x1, waiting for transfers between devices, per_device(): held = lax.all_gather(kv_rows, ('a', 'b'), axis=0, tiled=True)  31.9 us
    all_gather x1, blocking collectives, per_device(): both = lax.all_gather(both, 'a', axis=0, tiled=True)  25.2 us
    pallas_call x5, Pallas kernels, partial_attention(): pl.pallas_call(partial_kernel, in_specs=[smem] * 3 + [vmem, pl.BlockSpec(...  21.5 us
    all_gather x1, blocking collectives, per_device(): kv_own = lax.all_gather(both[:, :width], 'b', axis=0, tiled=True)  12.8 us
    all_gather x1, blocking collectives, per_device(): query_own = lax.all_gather(query_own_in, 'b', axis=0, tiled=True)  12.6 us
    pallas_call x2, Pallas kernels, project(): pl.pallas_call(project_kernel, in_specs=[pl.BlockSpec(memory_space=pltpu....  9.76 us
  transfers between devices with their start and end apart: 16, of which 9 were waited for; matrix products, arithmetic and copies ran while one was open for 1% of the time, Pallas kernels for 11%

profile of v8, /device:TPU:1, one launch (start us, length us, event | category | flops | bytes accessed | tf_op | source)
XLA Modules:
  0.0 229.8 jit_solution(2644205955856127410)
XLA Ops:
  8.1 25.2 %all_gather.16 = bf16[256,512]{1,0:T(8,128)(2,1)S(1)} all-gather(bf16[64,512]{1,0:T(8,128)(2,1)S(1)} %pad_maximum_fusion), channel_id=1, replica_groups=mesh['a'=4,'b'=4,'x'=4,'y'=4,'c'=2] {'a'}, dimensions={0}, use_global_device_ids=true | all-gather | bytes 327680 | tf_op jit(solution)/shard_map/all_gather | solution.py:303
  33.4 12.8 %all_gather.17 = bf16[1024,256]{1,0:T(8,128)(2,1)S(1)} all-gather(bf16[256,256]{1,0:T(8,128)(2,1)S(1)} %get-tuple-element.47), channel_id=1, replica_groups=mesh['a'=4,'b'=4,'x'=4,'y'=4,'c'=2] {'b'}, dimensions={0}, use_global_device_ids=true | all-gather | bytes 655360 | tf_op jit(solution)/shard_map/all_gather | solution.py:304
  46.1 3.1 %collective-permute-start = (bf16[4,4,64,256]{3,2,1,0:T(8,128)(2,1)S(1)}, bf16[4,4,64,256]{3,2,1,0:T(8,128)(2,1)S(1)}, u32[]{:S(2)}, u32[]{:S(2)}) collective-permute-start(bf16[4,4,64,256]{3,2,1,0:T(8,128)(2,1)S(1)} %bitcast.13), channel_id=1, source_target_pairs={{0,8},{8,16},{16,24},{24,0},{1,9},{9,17},{17,25},{25,1},{2,10},{10... | collective-permute-start | bytes 1572872 | tf_op jit(solution)/shard_map/ppermute | solution.py:28
  49.3 4.4 %collective-permute-start.1 = (bf16[4,4,64,256]{3,2,1,0:T(8,128)(2,1)S(1)}, bf16[4,4,64,256]{3,2,1,0:T(8,128)(2,1)S(1)}, u32[]{:S(2)}, u32[]{:S(2)}) collective-permute-start(bf16[4,4,64,256]{3,2,1,0:T(8,128)(2,1)S(1)} %bitcast.14), channel_id=1, source_target_pairs={{0,16},{8,24},{16,0},{24,8},{1,17},{9,25},{17,1},{25,9},{2,18},{10... | collective-permute-start | bytes 1572872 | tf_op jit(solution)/shard_map/ppermute | solution.py:28
  53.6 3.1 %collective-permute-start.2 = (bf16[4,4,64,256]{3,2,1,0:T(8,128)(2,1)S(1)}, bf16[4,4,64,256]{3,2,1,0:T(8,128)(2,1)S(1)}, u32[]{:S(2)}, u32[]{:S(2)}) collective-permute-start(bf16[4,4,64,256]{3,2,1,0:T(8,128)(2,1)S(1)} %bitcast.15), channel_id=1, source_target_pairs={{0,24},{8,0},{16,8},{24,16},{1,25},{9,1},{17,9},{25,17},{2,26},{10... | collective-permute-start | bytes 1572872 | tf_op jit(solution)/shard_map/ppermute | solution.py:28
  56.7 12.6 %all_gather.18 = bf16[1024,256]{1,0:T(8,128)(2,1)S(1)} all-gather(bf16[256,256]{1,0:T(8,128)(2,1)S(1)} %get-tuple-element.24), channel_id=1, replica_groups=mesh['a'=4,'b'=4,'x'=4,'y'=4,'c'=2] {'b'}, dimensions={0}, use_global_device_ids=true | all-gather | bytes 655360 | tf_op jit(solution)/shard_map/all_gather | solution.py:312
  69.3 3.5 %collective-permute-done.2.part3 = bf16[4,4,64,256]{3,2,1,0:T(8,128)(2,1)S(1)} collective-permute-done((bf16[4,4,64,256]{3,2,1,0:T(8,128)(2,1)S(1)}, bf16[4,4,64,256]{3,2,1,0:T(8,128)(2,1)S(1)}, u32[]{:S(2)}, u32[]{:S(2)}) %collective-permute-start.2) | collective-permute-done | bytes 524320 | tf_op jit(solution)/shard_map/ppermute | solution.py:28
  72.8 5.3 %project.2 = bf16[1024,256]{1,0:T(8,128)(2,1)} custom-call(s32[1]{0:T(128)} %bitcast.1.place, bf16[1024,4096]{1,0:T(8,128)(2,1)} %all-gather.3.cloned.1.call-done.rows, bf16[4,4,64,256]{3,2,1,0:T(8,128)(2,1)S(1)} %bitcast.16, bf16[4,4,64,256]{3,2,1,0:T(8,128)(2,1)S(1)} %collective-permute-done.part1, ...), custom_call_target="tpu_custom_call" | custom-call | flops 2147483648 | bytes 11010048 | tf_op jit(solution)/shard_map/project/pallas_call | solution.py:62
  79.2 6.3 %collective-permute-start.6 = (s32[16]{0:T(128)S(1)}, s32[16]{0:T(128)S(1)}, u32[]{:S(2)}, u32[]{:S(2)}) collective-permute-start(s32[16]{0:T(128)S(1)} %copy-done.1), channel_id=1, source_target_pairs={{0,8},{8,16},{16,24},{24,0},{1,9},{9,17},{17,25},{25,1},{2,10},{10... | collective-permute-start | bytes 200 | tf_op jit(solution)/shard_map/ppermute | solution.py:28
  87.5 3.4 %collective-permute-start.3 = (bf16[4,4,64,256]{3,2,1,0:T(8,128)(2,1)S(1)}, bf16[4,4,64,256]{3,2,1,0:T(8,128)(2,1)S(1)}, u32[]{:S(2)}, u32[]{:S(2)}) collective-permute-start(bf16[4,4,64,256]{3,2,1,0:T(8,128)(2,1)S(1)} %bitcast.9), channel_id=1, source_target_pairs={{0,8},{8,16},{16,24},{24,0},{1,9},{9,17},{17,25},{25,1},{2,10},{10... | collective-permute-start | bytes 1572872 | tf_op jit(solution)/shard_map/ppermute | solution.py:28
  90.8 2.3 collective-permute-start.4
  93.1 4.0 %collective-permute-start.5 = (bf16[4,4,64,256]{3,2,1,0:T(8,128)(2,1)S(1)}, bf16[4,4,64,256]{3,2,1,0:T(8,128)(2,1)S(1)}, u32[]{:S(2)}, u32[]{:S(2)}) collective-permute-start(bf16[4,4,64,256]{3,2,1,0:T(8,128)(2,1)S(1)} %bitcast.11), channel_id=1, source_target_pairs={{0,24},{8,0},{16,8},{24,16},{1,25},{9,1},{17,9},{25,17},{2,26},{10... | collective-permute-start | bytes 1572872 | tf_op jit(solution)/shard_map/ppermute | solution.py:28
  97.7 2.2 collective-permute-done.3.part1
  99.9 10.6 %collective-permute-done.4.part2 = bf16[4,4,64,256]{3,2,1,0:T(8,128)(2,1)S(1)} collective-permute-done((bf16[4,4,64,256]{3,2,1,0:T(8,128)(2,1)S(1)}, bf16[4,4,64,256]{3,2,1,0:T(8,128)(2,1)S(1)}, u32[]{:S(2)}, u32[]{:S(2)}) %collective-permute-start.4) | collective-permute-done | bytes 524320 | tf_op jit(solution)/shard_map/ppermute | solution.py:28
  110.5 6.1 %collective-permute-done.5.part3 = bf16[4,4,64,256]{3,2,1,0:T(8,128)(2,1)S(1)} collective-permute-done((bf16[4,4,64,256]{3,2,1,0:T(8,128)(2,1)S(1)}, bf16[4,4,64,256]{3,2,1,0:T(8,128)(2,1)S(1)}, u32[]{:S(2)}, u32[]{:S(2)}) %collective-permute-start.5) | collective-permute-done | bytes 524320 | tf_op jit(solution)/shard_map/ppermute | solution.py:28
  116.7 4.5 %project.3.query = bf16[1024,256]{1,0:T(8,128)(2,1)S(1)} custom-call(s32[1]{0:T(128)} %bitcast.1.place, bf16[1024,4096]{1,0:T(8,128)(2,1)} %all-gather.3.cloned.1.call-done.rows, bf16[4,4,64,256]{3,2,1,0:T(8,128)(2,1)S(1)} %bitcast.12, bf16[4,4,64,256]{3,2,1,0:T(8,128)(2,1)S(1)} %collective-permute-done.3.part1, ...), custom_call_target="tpu_custom_call" | custom-call | flops 2147483648 | bytes 11010048 | tf_op jit(solution)/shard_map/project/pallas_call | solution.py:62
  121.1 5.4 %collective-permute-start.10 = (bf16[1024,256]{1,0:T(8,128)(2,1)S(1)}, bf16[1024,256]{1,0:T(8,128)(2,1)S(1)}, u32[]{:S(2)}, u32[]{:S(2)}) collective-permute-start(bf16[1024,256]{1,0:T(8,128)(2,1)S(1)} %project.3.query), channel_id=1, source_target_pairs={{0,24},{8,0},{16,8},{24,16},{1,25},{9,1},{17,9},{25,17},{2,26},{10... | collective-permute-start | bytes 1572872 | tf_op jit(solution)/shard_map/ppermute | solution.py:28
  128.5 3.1 %collective-permute-start.9 = (bf16[1024,256]{1,0:T(8,128)(2,1)S(1)}, bf16[1024,256]{1,0:T(8,128)(2,1)S(1)}, u32[]{:S(2)}, u32[]{:S(2)}) collective-permute-start(bf16[1024,256]{1,0:T(8,128)(2,1)S(1)} %project.3.query), channel_id=1, source_target_pairs={{0,16},{8,24},{16,0},{24,8},{1,17},{9,25},{17,1},{25,9},{2,18},{10... | collective-permute-start | bytes 1572872 | tf_op jit(solution)/shard_map/ppermute | solution.py:28
  132.0 5.6 %partial_attention.5.refs_3_ = bf16[1088,256]{1,0:T(8,128)(2,1)S(1)} custom-call(s32[1]{0:T(128)} %constant.107.clone.1.from_x, s32[128]{0:T(128)S(1)} %reshape.358.index, s32[16]{0:T(128)S(1)} %get-tuple-element.45.counts, bf16[1024,256]{1,0:T(8,128)(2,1)S(1)} %project.3.query, bf16[16,64,256]{2,1,0:T(8,128)(2,1)} %bitcast.5.held), custom_call_target="tpu_custom_call" | custom-call | flops 2000000000 | bytes 65536 | tf_op jit(solution)/shard_map/partial_attention/pallas_call | solution.py:183
  137.6 5.7 %collective-permute-done.8.query = bf16[1024,256]{1,0:T(8,128)(2,1)S(1)} collective-permute-done((bf16[1024,256]{1,0:T(8,128)(2,1)S(1)}, bf16[1024,256]{1,0:T(8,128)(2,1)S(1)}, u32[]{:S(2)}, u32[]{:S(2)}) %collective-permute-start.8) | collective-permute-done | bytes 524320 | tf_op jit(solution)/shard_map/ppermute | solution.py:28
  143.3 8.8 %collective-permute-done.9.query = bf16[1024,256]{1,0:T(8,128)(2,1)S(1)} collective-permute-done((bf16[1024,256]{1,0:T(8,128)(2,1)S(1)}, bf16[1024,256]{1,0:T(8,128)(2,1)S(1)}, u32[]{:S(2)}, u32[]{:S(2)}) %collective-permute-start.9) | collective-permute-done | bytes 524320 | tf_op jit(solution)/shard_map/ppermute | solution.py:28
  152.1 31.9 %all-gather.5.cloned.1.call-done = bf16[16384,256]{1,0:T(8,128)(2,1)} async-done(((bf16[1024,256]{1,0:T(8,128)(2,1)}), bf16[16384,256]{1,0:T(8,128)(2,1)}) %all-gather.5.cloned.1.call-update) | async-done | bytes 8388624 | tf_op jit(solution)/shard_map/all_gather | solution.py:317
  184.0 4.0 %partial_attention.8 = bf16[1088,256]{1,0:T(8,128)(2,1)S(1)} custom-call(s32[1]{0:T(128)} %bitcast.7.from_x, s32[512]{0:T(512)S(1)} %reshape.361.index, s32[64]{0:T(128)S(1)} %get-tuple-element.34.counts, bf16[1024,256]{1,0:T(8,128)(2,1)S(1)} %collective-permute-done.9.query, bf16[256,64,256]{2,1,0:T(8,128)(2,1)} %bitcast.17), custom_call_target="tpu_custom_call" | custom-call | flops 2000000000 | bytes 65536 | tf_op jit(solution)/shard_map/partial_attention/pallas_call | solution.py:183
  188.0 5.4 %collective-permute-start.12 = (bf16[1088,256]{1,0:T(8,128)(2,1)S(1)}, bf16[1088,256]{1,0:T(8,128)(2,1)}, u32[]{:S(2)}, u32[]{:S(2)}) collective-permute-start(bf16[1088,256]{1,0:T(8,128)(2,1)S(1)} %partial_attention.8), channel_id=1, source_target_pairs={{0,16},{8,24},{16,0},{24,8},{1,17},{9,25},{17,1},{25,9},{2,18},{10... | collective-permute-start | bytes 1671176 | tf_op jit(solution)/shard_map/ppermute | solution.py:28
  193.4 4.0 %partial_attention.7 = bf16[1088,256]{1,0:T(8,128)(2,1)S(1)} custom-call(s32[1]{0:T(128)} %bitcast.6.from_x, s32[512]{0:T(512)S(1)} %reshape.361.index, s32[64]{0:T(128)S(1)} %get-tuple-element.34.counts, bf16[1024,256]{1,0:T(8,128)(2,1)S(1)} %collective-permute-done.8.query, bf16[256,64,256]{2,1,0:T(8,128)(2,1)} %bitcast.18), custom_call_target="tpu_custom_call" | custom-call | flops 2000000000 | bytes 65536 | tf_op jit(solution)/shard_map/partial_attention/pallas_call | solution.py:183
  197.4 2.8 %collective-permute-start.11 = (bf16[1088,256]{1,0:T(8,128)(2,1)S(1)}, bf16[1088,256]{1,0:T(8,128)(2,1)}, u32[]{:S(2)}, u32[]{:S(2)}) collective-permute-start(bf16[1088,256]{1,0:T(8,128)(2,1)S(1)} %partial_attention.7), channel_id=1, source_target_pairs={{0,24},{8,0},{16,8},{24,16},{1,25},{9,1},{17,9},{25,17},{2,26},{10... | collective-permute-start | bytes 1671176 | tf_op jit(solution)/shard_map/ppermute | solution.py:28
  200.3 4.0 %partial_attention.9 = bf16[1088,256]{1,0:T(8,128)(2,1)S(1)} custom-call(s32[1]{0:T(128)} %bitcast.8.from_x, s32[512]{0:T(512)S(1)} %reshape.361.index, s32[64]{0:T(128)S(1)} %get-tuple-element.34.counts, bf16[1024,256]{1,0:T(8,128)(2,1)S(1)} %collective-permute-done.10.query, bf16[256,64,256]{2,1,0:T(8,128)(2,1)} %bitcast.19), custom_call_target="tpu_custom_call" | custom-call | flops 2000000000 | bytes 65536 | tf_op jit(solution)/shard_map/partial_attention/pallas_call | solution.py:183
  204.3 2.8 %collective-permute-start.13 = (bf16[1088,256]{1,0:T(8,128)(2,1)S(1)}, bf16[1088,256]{1,0:T(8,128)(2,1)}, u32[]{:S(2)}, u32[]{:S(2)}) collective-permute-start(bf16[1088,256]{1,0:T(8,128)(2,1)S(1)} %partial_attention.9), channel_id=1, source_target_pairs={{0,8},{8,16},{16,24},{24,0},{1,9},{9,17},{17,25},{25,1},{2,10},{10... | collective-permute-start | bytes 1671176 | tf_op jit(solution)/shard_map/ppermute | solution.py:28
  207.1 4.0 %partial_attention.6.refs_0_ = bf16[1088,256]{1,0:T(8,128)(2,1)S(1)} custom-call(s32[1]{0:T(128)} %bitcast.from_x, s32[512]{0:T(512)S(1)} %reshape.361.index, s32[64]{0:T(128)S(1)} %get-tuple-element.34.counts, bf16[1024,256]{1,0:T(8,128)(2,1)S(1)} %project.3.query, bf16[256,64,256]{2,1,0:T(8,128)(2,1)} %bitcast.20), custom_call_target="tpu_custom_call" | custom-call | flops 2000000000 | bytes 65536 | tf_op jit(solution)/shard_map/partial_attention/pallas_call | solution.py:183
  211.1 6.4 %collective-permute-done.11.refs_1_ = bf16[1088,256]{1,0:T(8,128)(2,1)} collective-permute-done((bf16[1088,256]{1,0:T(8,128)(2,1)S(1)}, bf16[1088,256]{1,0:T(8,128)(2,1)}, u32[]{:S(2)}, u32[]{:S(2)}) %collective-permute-start.11) | collective-permute-done | bytes 557088 | tf_op jit(solution)/shard_map/ppermute | solution.py:28
  217.5 2.6 %combine.2.refs_0_ = bf16[1088,256]{1,0:T(8,128)(2,1)S(1)} custom-call(bf16[1088,256]{1,0:T(8,128)(2,1)S(1)} %partial_attention.6.refs_0_, bf16[1088,256]{1,0:T(8,128)(2,1)} %collective-permute-done.11.refs_1_, bf16[1088,256]{1,0:T(8,128)(2,1)} %collective-permute-done.12.refs_2_, bf16[1088,256]{1,0:T(8,128)(2,1)S(1)} %partial_attention.5.refs_3_), custom_call_target="tpu_custom_call" | custom-call | tf_op jit(solution)/shard_map/combine/pallas_call | solution.py:236
  220.4 2.6 %combine.3 = bf16[1024,256]{1,0:T(8,128)(2,1)} custom-call(bf16[1088,256]{1,0:T(8,128)(2,1)S(1)} %combine.2.refs_0_, bf16[1088,256]{1,0:T(8,128)(2,1)} %collective-permute-done.13.refs_1_), custom_call_target="tpu_custom_call" | custom-call | tf_op jit(solution)/shard_map/combine/pallas_call | solution.py:236
  (49 shorter events, 7.8 us)
Async XLA Ops:
  6.5 72.6 %copy-start = (s32[4]{0:T(128)S(1)}, s32[4]{0:T(128)}, u32[]{:S(2)}) copy-start(s32[4]{0:T(128)} %constant.120.clone) | copy-start | bytes 52
  6.5 91.1 %copy-start.2 = (s32[4]{0:T(128)S(1)}, s32[4]{0:T(128)}, u32[]{:S(2)}) copy-start(s32[4]{0:T(128)} %constant.123) | copy-start | bytes 52
  6.5 71.6 %copy-start.3 = (s32[2]{0:T(128)S(1)}, s32[2]{0:T(128)}, u32[]{:S(2)}) copy-start(s32[2]{0:T(128)} %param.11) | copy-start | bytes 28
  6.5 72.7 %copy-start.1 = (s32[16]{0:T(128)S(1)}, s32[16]{0:T(128)}, u32[]{:S(2)}) copy-start(s32[16]{0:T(128)} %param.10) | copy-start | bytes 196
  6.5 66.3 %all-gather.3.cloned.1.call-start = ((), (), s32[]{:S(2)}) async-start(), calls=%async_computation | async-start | bytes 9437184 | tf_op jit(solution)/shard_map/all_gather | solution.py:300
  7.3 176.7 %all-gather.5.cloned.1.call-start = ((), (), s32[]{:S(2)}) async-start(), calls=%async_computation.1 | async-start | bytes 8912896 | tf_op jit(solution)/shard_map/all_gather | solution.py:317
  46.1 23.2 %collective-permute-start = (bf16[4,4,64,256]{3,2,1,0:T(8,128)(2,1)S(1)}, bf16[4,4,64,256]{3,2,1,0:T(8,128)(2,1)S(1)}, u32[]{:S(2)}, u32[]{:S(2)}) collective-permute-start(bf16[4,4,64,256]{3,2,1,0:T(8,128)(2,1)S(1)} %bitcast.13), channel_id=1, source_target_pairs={{0,8},{8,16},{16,24},{24,0},{1,9},{9,17},{17,25},{25,1},{2,10},{10... | collective-permute-start | bytes 1572872 | tf_op jit(solution)/shard_map/ppermute | solution.py:28
  49.3 20.1 %collective-permute-start.1 = (bf16[4,4,64,256]{3,2,1,0:T(8,128)(2,1)S(1)}, bf16[4,4,64,256]{3,2,1,0:T(8,128)(2,1)S(1)}, u32[]{:S(2)}, u32[]{:S(2)}) collective-permute-start(bf16[4,4,64,256]{3,2,1,0:T(8,128)(2,1)S(1)} %bitcast.14), channel_id=1, source_target_pairs={{0,16},{8,24},{16,0},{24,8},{1,17},{9,25},{17,1},{25,9},{2,18},{10... | collective-permute-start | bytes 1572872 | tf_op jit(solution)/shard_map/ppermute | solution.py:28
  53.6 19.2 %collective-permute-start.2 = (bf16[4,4,64,256]{3,2,1,0:T(8,128)(2,1)S(1)}, bf16[4,4,64,256]{3,2,1,0:T(8,128)(2,1)S(1)}, u32[]{:S(2)}, u32[]{:S(2)}) collective-permute-start(bf16[4,4,64,256]{3,2,1,0:T(8,128)(2,1)S(1)} %bitcast.15), channel_id=1, source_target_pairs={{0,24},{8,0},{16,8},{24,16},{1,25},{9,1},{17,9},{25,17},{2,26},{10... | collective-permute-start | bytes 1572872 | tf_op jit(solution)/shard_map/ppermute | solution.py:28
  79.2 18.2 %collective-permute-start.6 = (s32[16]{0:T(128)S(1)}, s32[16]{0:T(128)S(1)}, u32[]{:S(2)}, u32[]{:S(2)}) collective-permute-start(s32[16]{0:T(128)S(1)} %copy-done.1), channel_id=1, source_target_pairs={{0,8},{8,16},{16,24},{24,0},{1,9},{9,17},{17,25},{25,1},{2,10},{10... | collective-permute-start | bytes 200 | tf_op jit(solution)/shard_map/ppermute | solution.py:28
  85.5 12.0 %collective-permute-start.7 = (s32[16]{0:T(128)S(1)}, s32[16]{0:T(128)S(1)}, u32[]{:S(2)}, u32[]{:S(2)}) collective-permute-start(s32[16]{0:T(128)S(1)} %copy-done.1), channel_id=1, source_target_pairs={{0,24},{8,0},{16,8},{24,16},{1,25},{9,1},{17,9},{25,17},{2,26},{10... | collective-permute-start | bytes 200 | tf_op jit(solution)/shard_map/ppermute | solution.py:28
  87.5 12.4 %collective-permute-start.3 = (bf16[4,4,64,256]{3,2,1,0:T(8,128)(2,1)S(1)}, bf16[4,4,64,256]{3,2,1,0:T(8,128)(2,1)S(1)}, u32[]{:S(2)}, u32[]{:S(2)}) collective-permute-start(bf16[4,4,64,256]{3,2,1,0:T(8,128)(2,1)S(1)} %bitcast.9), channel_id=1, source_target_pairs={{0,8},{8,16},{16,24},{24,0},{1,9},{9,17},{17,25},{25,1},{2,10},{10... | collective-permute-start | bytes 1572872 | tf_op jit(solution)/shard_map/ppermute | solution.py:28
  90.8 19.7 %collective-permute-start.4 = (bf16[4,4,64,256]{3,2,1,0:T(8,128)(2,1)S(1)}, bf16[4,4,64,256]{3,2,1,0:T(8,128)(2,1)S(1)}, u32[]{:S(2)}, u32[]{:S(2)}) collective-permute-start(bf16[4,4,64,256]{3,2,1,0:T(8,128)(2,1)S(1)} %bitcast.10), channel_id=1, source_target_pairs={{0,16},{8,24},{16,0},{24,8},{1,17},{9,25},{17,1},{25,9},{2,18},{10... | collective-permute-start | bytes 1572872 | tf_op jit(solution)/shard_map/ppermute | solution.py:28
  93.1 23.6 %collective-permute-start.5 = (bf16[4,4,64,256]{3,2,1,0:T(8,128)(2,1)S(1)}, bf16[4,4,64,256]{3,2,1,0:T(8,128)(2,1)S(1)}, u32[]{:S(2)}, u32[]{:S(2)}) collective-permute-start(bf16[4,4,64,256]{3,2,1,0:T(8,128)(2,1)S(1)} %bitcast.11), channel_id=1, source_target_pairs={{0,24},{8,0},{16,8},{24,16},{1,25},{9,1},{17,9},{25,17},{2,26},{10... | collective-permute-start | bytes 1572872 | tf_op jit(solution)/shard_map/ppermute | solution.py:28
  121.1 16.4 %collective-permute-start.10 = (bf16[1024,256]{1,0:T(8,128)(2,1)S(1)}, bf16[1024,256]{1,0:T(8,128)(2,1)S(1)}, u32[]{:S(2)}, u32[]{:S(2)}) collective-permute-start(bf16[1024,256]{1,0:T(8,128)(2,1)S(1)} %project.3.query), channel_id=1, source_target_pairs={{0,24},{8,0},{16,8},{24,16},{1,25},{9,1},{17,9},{25,17},{2,26},{10... | collective-permute-start | bytes 1572872 | tf_op jit(solution)/shard_map/ppermute | solution.py:28
  126.6 16.7 %collective-permute-start.8 = (bf16[1024,256]{1,0:T(8,128)(2,1)S(1)}, bf16[1024,256]{1,0:T(8,128)(2,1)S(1)}, u32[]{:S(2)}, u32[]{:S(2)}) collective-permute-start(bf16[1024,256]{1,0:T(8,128)(2,1)S(1)} %project.3.query), channel_id=1, source_target_pairs={{0,8},{8,16},{16,24},{24,0},{1,9},{9,17},{17,25},{25,1},{2,10},{10... | collective-permute-start | bytes 1572872 | tf_op jit(solution)/shard_map/ppermute | solution.py:28
  128.5 23.6 %collective-permute-start.9 = (bf16[1024,256]{1,0:T(8,128)(2,1)S(1)}, bf16[1024,256]{1,0:T(8,128)(2,1)S(1)}, u32[]{:S(2)}, u32[]{:S(2)}) collective-permute-start(bf16[1024,256]{1,0:T(8,128)(2,1)S(1)} %project.3.query), channel_id=1, source_target_pairs={{0,16},{8,24},{16,0},{24,8},{1,17},{9,25},{17,1},{25,9},{2,18},{10... | collective-permute-start | bytes 1572872 | tf_op jit(solution)/shard_map/ppermute | solution.py:28
  188.0 23.1 %collective-permute-start.12 = (bf16[1088,256]{1,0:T(8,128)(2,1)S(1)}, bf16[1088,256]{1,0:T(8,128)(2,1)}, u32[]{:S(2)}, u32[]{:S(2)}) collective-permute-start(bf16[1088,256]{1,0:T(8,128)(2,1)S(1)} %partial_attention.8), channel_id=1, source_target_pairs={{0,16},{8,24},{16,0},{24,8},{1,17},{9,25},{17,1},{25,9},{2,18},{10... | collective-permute-start | bytes 1671176 | tf_op jit(solution)/shard_map/ppermute | solution.py:28
  197.4 20.0 %collective-permute-start.11 = (bf16[1088,256]{1,0:T(8,128)(2,1)S(1)}, bf16[1088,256]{1,0:T(8,128)(2,1)}, u32[]{:S(2)}, u32[]{:S(2)}) collective-permute-start(bf16[1088,256]{1,0:T(8,128)(2,1)S(1)} %partial_attention.7), channel_id=1, source_target_pairs={{0,24},{8,0},{16,8},{24,16},{1,25},{9,1},{17,9},{25,17},{2,26},{10... | collective-permute-start | bytes 1671176 | tf_op jit(solution)/shard_map/ppermute | solution.py:28
  204.3 16.1 %collective-permute-start.13 = (bf16[1088,256]{1,0:T(8,128)(2,1)S(1)}, bf16[1088,256]{1,0:T(8,128)(2,1)}, u32[]{:S(2)}, u32[]{:S(2)}) collective-permute-start(bf16[1088,256]{1,0:T(8,128)(2,1)S(1)} %partial_attention.9), channel_id=1, source_target_pairs={{0,8},{8,16},{16,24},{24,0},{1,9},{9,17},{17,25},{25,1},{2,10},{10... | collective-permute-start | bytes 1671176 | tf_op jit(solution)/shard_map/ppermute | solution.py:28
Sparse Core Ops, SparseCore 0:
  9.5 63.1 all-gather.2
  78.2 105.7 all-gather.4
